TPU v7x, 32 devices: a whole 2x2x4 slice. The times are simulated.
32 devices in a mesh: runs: 2 (over y), mode: 8 (over z, x), mer: 2 (over core).
Axes of the slice: x: 2, y: 2, z: 4, core: 2. Of those that a mesh axis runs over, the one named last changes fastest.
Arguments:
- velocity: float32 [6, 2, 16, 4096], P('runs', None, 'mode', 'mer'), parts along dimension 0, may hold values from -6 to 6
- vorticity: float32 [6, 2, 16, 4096], P('runs', None, 'mode', 'mer'), parts along dimension 0, may hold values from -6 to 6
- magnetic: float32 [6, 2, 16, 4096], P('runs', None, 'mode', 'mer'), parts along dimension 0, may hold values from -6 to 6
- current: float32 [6, 2, 16, 4096], P('runs', None, 'mode', 'mer'), parts along dimension 0, may hold values from -6 to 6
- elem_nodes: int32 [6, 2048], P(None, 'mer'), may hold values from 0 to 2047, as said below
- mass_coef: float32 [2048], P('mer'), may hold values from 0.5 to 2
- stiff_coef: float32 [2048], P('mer'), may hold values from 0.05 to 0.5
- radial_coef: float32 [2048], P('mer'), may hold values from 0.5 to 4
- iface: int32 [2, 128], P('mer'), may hold values from 0 to 2047, as said below
Outputs:
- velocity_new: float32 [6, 2, 16, 4096], P('runs', None, 'mode', 'mer'), parts along dimension 0
- magnetic_new: float32 [6, 2, 16, 4096], P('runs', None, 'mode', 'mer'), parts along dimension 0
There are 2 independent parts, one for each index of `runs`. A program takes and returns all parts, laid end to end along the dimension named above; an argument that names none is the same for every part. Nothing has to cross between parts.
Inputs may be any that keep to these rules, and one draw needn't show every extreme that they name: `elem_nodes`: every node of a partition is named by some triangle of that partition. `iface`: entries of one row are distinct.
All inputs are finite; a program needn't handle non-finite values.
Results may differ from a plain program's by a relative error of at most 0.0003.
Values sent between devices are 32-bit elements; how exact they have to be, the bound alone decides.
No kernel may reach another device: no remote copies, remote signals or barrier semaphores. Data moves between devices by JAX's collectives and lax.ppermute only.
A program may use at most 64 MiB of HBM per device.

v0:
```python
import functools
import math

import jax
import jax.numpy as jnp
import numpy as np
from jax import lax
from jax.experimental import pallas as pl
from jax.experimental.pallas import tpu as pltpu
from jax.sharding import PartitionSpec as P

step_size = 0.05
diffusion_ratio = 2.0
f32 = jnp.float32
bf16 = jnp.bfloat16
vmem_limit = 16 * 2**20


def params():
    return pltpu.CompilerParams(vmem_limit_bytes=vmem_limit)


def halves(table):
    high = table.astype(np.float32).astype(jnp.bfloat16)
    low = (table - high.astype(np.float64)).astype(np.float32).astype(jnp.bfloat16)
    return high, low


def trig_tables(modes, per_dev):
    angles = 2 * modes
    order = np.arange(modes)
    points = np.arange(angles)
    phase = (points[:, None] * order[None, :] % angles) * (2.0 * math.pi / angles)
    both = np.stack([np.cos(phase), np.sin(phase)])
    both = both.reshape(2, angles, modes // per_dev, per_dev)
    factor = np.where(order == 0, 1.0, 2.0).reshape(modes // per_dev, per_dev) / angles
    same = np.eye(2)
    synthesis = np.einsum("pq,sajk->pajqsk", same, both).reshape(2 * angles, -1)
    analysis = np.einsum("pq,sajk,jk->jqskpa", same, both, factor * step_size).reshape(-1, 2 * angles)
    out = []
    for table in (synthesis, analysis):
        high, low = halves(table)
        out.append(jnp.asarray(np.concatenate([high, high, low], axis=1)))
    return out


def pieces(array, count):
    parts = []
    rest = array
    for i in range(count):
        part = rest.astype(bf16).astype(f32)
        parts.append(part)
        rest = rest - part
    return jnp.concatenate(parts, axis=0).astype(bf16)


def product(array, exact, contract, count=2):
    rows = array.shape[0]
    out = lax.dot_general(
        pieces(array, count), exact, (((1,), (contract,)), ((), ())), preferred_element_type=f32
    )
    total = out[:rows]
    for i in range(1, count):
        total = total + out[i * rows : (i + 1) * rows]
    return total


def table_product(table, values):
    high = values.astype(bf16)
    low = (values - high.astype(f32)).astype(bf16)
    return jnp.dot(table, jnp.concatenate([high, low, high], axis=0), preferred_element_type=f32)


def pack_kernel(vel, mag, vort, cur, out):
    blocks, _, block = out.shape
    row = 0
    for field in (vel, mag, vort, cur):
        comps, _, per_dev, _ = field.shape
        for c in range(comps):
            for s in range(2):
                piece = field[c, s]
                for b in range(blocks):
                    out[b, row : row + per_dev, :] = piece[:, b * block : (b + 1) * block]
                row += per_dev


def nonlinear_kernel(fields, synthesis, analysis, out):
    owners, rows, block = fields.shape
    pair = rows // 6
    angles = synthesis.shape[0] // 2
    phys = []
    for t in range(6):
        coef = jnp.concatenate([fields[j, t * pair : (t + 1) * pair, :] for j in range(owners)], axis=0)
        values = table_product(synthesis[...], coef)
        phys += [values[:angles], values[angles:]]
    vel, mag, vort, cur = phys[0:3], phys[3:6], phys[6:9], phys[9:12]

    def cross(a, b, i):
        j, k = (i + 1) % 3, (i + 2) % 3
        return a[j] * b[k] - a[k] * b[j]

    terms = [cross(vel, vort, i) + cross(cur, mag, i) for i in range(3)]
    terms += [cross(vel, mag, i) for i in range(3)]
    for t in range(3):
        coef = table_product(analysis[...], jnp.concatenate([terms[2 * t], terms[2 * t + 1]], axis=0))
        for j in range(owners):
            span = slice(t * pair, (t + 1) * pair)
            out[j, span, :] = fields[j, span, :] + coef[j * pair : (j + 1) * pair]


def mesh_kernel(elem_nodes, mass, radial, stiff, iface, touch, at_iface, diag):
    nodes, elems = touch.shape
    shared = iface.shape[1]
    fields = 8
    words = nodes // fields
    width = math.gcd(elems, 256)

    def chunk(c, carry):
        span = pl.ds(pl.multiple_of(c * width, width), width)
        word = lax.broadcasted_iota(jnp.int32, (words, width), 0)
        total = jnp.zeros((words, width), jnp.int32)
        for i in range(elem_nodes.shape[0]):
            ids = elem_nodes[i : i + 1, span]
            field = ids // words
            value = jnp.left_shift(1, field * 4)
            total = total + jnp.where(ids - field * words == word, value, 0)
        for q in range(fields):
            count = jnp.right_shift(total, 4 * q) & 15
            touch[q * words : (q + 1) * words, span] = count.astype(f32).astype(bf16)
        return carry

    lax.fori_loop(0, elems // width, chunk, 0)
    node = lax.broadcasted_iota(jnp.int32, (nodes, shared), 0)
    at_iface[...] = jnp.where(iface[...] == node, 1.0, 0.0).astype(bf16)
    zero = jnp.zeros((5, elems), f32)
    coefs = jnp.concatenate([mass[...] / 12.0, radial[...] / 12.0, 6.0 * stiff[...], zero], axis=0)
    sums = product(coefs, touch[...], 1, 3)
    ones = jnp.ones((16, shared), bf16)
    hits = lax.dot_general(ones, at_iface[...], (((1,), (1,)), ((), ())), preferred_element_type=f32)
    row = lax.broadcasted_iota(jnp.int32, (8, nodes), 0)
    diag[...] = jnp.where(row == 3, 1.0 - 0.5 * hits[:8], sums)


def row_factors(place, rows, per_dev, modes):
    row = lax.broadcasted_iota(jnp.int32, (rows, 1), 0)
    order = (place * per_dev + row % per_dev).astype(f32)
    shift = (order / modes) ** 2
    scale = jnp.where(row < rows // 2, 1.0, diffusion_ratio).astype(f32)
    return shift, scale


def operator_parts(place, rows, per_dev, modes, mass, radial, stiff, diag):
    shift, scale = row_factors(place[0], rows, per_dev, modes)
    per_elem = (mass[...] + shift * radial[...]) / 12.0 - scale * stiff[...]
    per_node = diag[0:1, :] + shift * diag[1:2, :] + scale * diag[2:3, :]
    return per_elem, per_node


def row_sum(array):
    return jnp.sum(array, axis=1, keepdims=True)


def rhs_kernel(forcing, touch, at_iface, diag, mass, local, edge):
    blocks = forcing.shape[0]
    given = jnp.concatenate([forcing[b] for b in range(blocks)], axis=1)
    sums = product(given, touch[...], 0)
    image = diag[0:1, :] * given + product(sums * (mass[...] / 12.0), touch[...], 1)
    local[...] = image
    edge[...] = product(image, at_iface[...], 0, 3)


def first_kernel(per_dev, modes, place, local, edge, touch, at_iface, diag, mass, radial, stiff, rhs_out, image_out, sums_out, edge_out):
    rows, shared = edge.shape
    per_elem, per_node = operator_parts(place, rows, per_dev, modes, mass, radial, stiff, diag)
    rhs = local[...] + product(edge[...], at_iface[...], 1, 3)
    rhs_out[...] = rhs
    sums = product(rhs, touch[...], 0)
    sums_out[...] = sums
    spread = per_elem * sums
    image = per_node * rhs + product(spread, touch[...], 1)
    image_out[...] = image
    norm = row_sum(diag[3:4, :] * rhs * rhs)
    curvature = row_sum(per_node * rhs * rhs) + row_sum(spread * sums)
    edge_out[:, :shared] = product(image, at_iface[...], 0, 3)
    lane = lax.broadcasted_iota(jnp.int32, (rows, 128), 1)
    edge_out[:, shared:] = jnp.where(lane == 0, norm, curvature)


def second_kernel(per_dev, modes, place, image, edge, own, touch, at_iface, diag, mass, radial, stiff, rhs, sums, resid_out, norms_out):
    rows = image.shape[0]
    shared = edge.shape[1] - 128
    per_elem, per_node = operator_parts(place, rows, per_dev, modes, mass, radial, stiff, diag)
    norm = own[:, shared : shared + 1] + edge[:, shared : shared + 1]
    curvature = own[:, shared + 1 : shared + 2] + edge[:, shared + 1 : shared + 2]
    alpha = norm / curvature
    full = image[...] + product(edge[:, :shared], at_iface[...], 1, 3)
    resid = rhs[...] - alpha * full
    resid_out[...] = resid
    new = product(resid, touch[...], 0)
    after = row_sum(diag[3:4, :] * resid * resid)
    square = row_sum(per_node * resid * resid) + row_sum(per_elem * new * new)
    mixed = row_sum(per_node * resid * rhs[...]) + row_sum(per_elem * new * sums[...])
    lane = lax.broadcasted_iota(jnp.int32, (rows, 128), 1)
    norms_out[...] = jnp.where(lane == 0, after, jnp.where(lane == 1, square, mixed))


def last_kernel(edge, own, norms_own, norms, resid, rhs, vel_out, mag_out):
    shared = edge.shape[1] - 128
    norm = own[:, shared : shared + 1] + edge[:, shared : shared + 1]
    curvature = own[:, shared + 1 : shared + 2] + edge[:, shared + 1 : shared + 2]
    alpha = norm / curvature
    after = norms_own[:, 0:1] + norms[:, 0:1]
    square = norms_own[:, 1:2] + norms[:, 1:2]
    mixed = norms_own[:, 2:3] + norms[:, 2:3]
    beta = after / norm
    alpha_next = after / (square + 2.0 * beta * mixed + beta * beta * curvature)
    answer = (alpha + alpha_next * beta) * rhs[...] + alpha_next * resid[...]
    row = 0
    for out in (vel_out, mag_out):
        comps, _, per_dev, _ = out.shape
        for c in range(comps):
            for s in range(2):
                out[c, s] = answer[row : row + per_dev]
                row += per_dev


def per_device(velocity, vorticity, magnetic, current, elem_nodes, mass_coef, stiff_coef, radial_coef, iface):
    comps, _, per_dev, nodes = velocity.shape
    owners = lax.axis_size("mode")
    modes = per_dev * owners
    block = nodes // owners
    rows = 4 * comps * per_dev
    elems = elem_nodes.shape[1]
    shared = iface.shape[1]
    mass, radial, stiff = (a.reshape(1, elems) for a in (mass_coef, radial_coef, stiff_coef))
    synthesis, analysis = trig_tables(modes, per_dev)
    place = lax.axis_index("mode").astype(jnp.int32).reshape(1)

    def shape(*dims, kind=f32):
        return jax.ShapeDtypeStruct(dims, kind)

    if block % 128 == 0:
        packed = pl.pallas_call(
            pack_kernel, out_shape=shape(owners, 2 * rows, block), compiler_params=params(), name="pack"
        )(velocity, magnetic, vorticity, current)
    else:
        packed = jnp.concatenate(
            [a.reshape(rows // 2, owners, block) for a in (velocity, magnetic, vorticity, current)], axis=0
        ).transpose(1, 0, 2)
    columns = lax.all_to_all(packed, "mode", 0, 0, tiled=True)
    touch, at_iface, diag = pl.pallas_call(
        mesh_kernel,
        out_shape=(shape(nodes, elems, kind=bf16), shape(nodes, shared, kind=bf16), shape(8, nodes)),
        compiler_params=params(),
        name="incidence",
        cost_estimate=pl.CostEstimate(flops=2**31, bytes_accessed=2**23, transcendentals=0),
    )(elem_nodes, mass, radial, stiff, iface)
    terms = pl.pallas_call(
        nonlinear_kernel, out_shape=shape(owners, rows, block), compiler_params=params(), name="nonlinear"
    )(columns, synthesis, analysis)
    forcing = lax.all_to_all(terms, "mode", 0, 0, tiled=True)
    if block % 128:
        forcing = forcing.transpose(1, 0, 2).reshape(1, rows, nodes)

    def swap(array):
        return lax.ppermute(array, "mer", [(0, 1), (1, 0)])

    in_smem = pl.BlockSpec(memory_space=pltpu.SMEM)
    in_vmem = pl.BlockSpec(memory_space=pltpu.VMEM)
    local, edge = pl.pallas_call(
        rhs_kernel, out_shape=(shape(rows, nodes), shape(rows, shared)), compiler_params=params(), name="rhs"
    )(forcing, touch, at_iface, diag, mass)
    rhs, image, sums, edge_own = pl.pallas_call(
        functools.partial(first_kernel, per_dev, modes),
        in_specs=[in_smem] + [in_vmem] * 8,
        out_shape=(shape(rows, nodes), shape(rows, nodes), shape(rows, elems), shape(rows, shared + 128)),
        compiler_params=params(),
        name="first",
    )(place, local, swap(edge), touch, at_iface, diag, mass, radial, stiff)
    edge_other = swap(edge_own)
    resid, norms_own = pl.pallas_call(
        functools.partial(second_kernel, per_dev, modes),
        in_specs=[in_smem] + [in_vmem] * 11,
        out_shape=(shape(rows, nodes), shape(rows, 128)),
        compiler_params=params(),
        name="second",
    )(place, image, edge_other, edge_own, touch, at_iface, diag, mass, radial, stiff, rhs, sums)
    out = shape(*velocity.shape)
    return pl.pallas_call(
        last_kernel, out_shape=(out, out), compiler_params=params(), name="last"
    )(edge_other, edge_own, norms_own, swap(norms_own), resid, rhs)


def solution(mesh):
    field = P("runs", None, "mode", "mer")
    placed = (field, field, field, field, P(None, "mer"), P("mer"), P("mer"), P("mer"), P("mer", None))
    return jax.shard_map(
        per_device, mesh=mesh, in_specs=placed, out_specs=(field, field), check_vma=False
    )
```

profile of v0, /device:TPU:0, one launch (start us, length us, event | category | flops | bytes accessed | tf_op | source)
XLA Modules:
  0.0 53.2 jit_solution(934657860223646740)
XLA Ops:
  0.6 0.0 copy-start.3
  0.6 0.9 %copy-done.3 = f32[3,2,2,2048]{3,2,1,0:T(2,128)S(1)} copy-done((f32[3,2,2,2048]{3,2,1,0:T(2,128)S(1)}, f32[3,2,2,2048]{3,2,1,0:T(2,128)}, u32[]{:S(2)}) %copy-start.3) | copy-done | bytes 98328
  1.5 0.0 copy-start.4
  1.5 0.9 %copy-done.4 = f32[3,2,2,2048]{3,2,1,0:T(2,128)S(1)} copy-done((f32[3,2,2,2048]{3,2,1,0:T(2,128)S(1)}, f32[3,2,2,2048]{3,2,1,0:T(2,128)}, u32[]{:S(2)}) %copy-start.4) | copy-done | bytes 98328
  2.4 0.0 copy-start.5
  2.4 0.9 %copy-done.5 = f32[3,2,2,2048]{3,2,1,0:T(2,128)S(1)} copy-done((f32[3,2,2,2048]{3,2,1,0:T(2,128)S(1)}, f32[3,2,2,2048]{3,2,1,0:T(2,128)}, u32[]{:S(2)}) %copy-start.5) | copy-done | bytes 98328
  3.3 0.9 %copy-done.6 = f32[3,2,2,2048]{3,2,1,0:T(2,128)S(1)} copy-done((f32[3,2,2,2048]{3,2,1,0:T(2,128)S(1)}, f32[3,2,2,2048]{3,2,1,0:T(2,128)}, u32[]{:S(2)}) %copy-start.6) | copy-done | bytes 98328
  4.2 0.1 pack.1
  4.3 19.1 %all_to_all.10.fields = f32[8,48,256]{2,1,0:T(8,128)S(1)} all-to-all(f32[8,48,256]{2,1,0:T(8,128)S(1)} %pack.1), channel_id=1, replica_groups=mesh['runs'=2,'mode'=8,'mer'=2] {'mode'}, dimensions={0} | all-to-all | bytes 786432 | tf_op jit(solution)/shard_map/all_to_all | solution.py:250
  23.5 0.0 copy-start.9
  23.5 0.8 %copy-done.9 = bf16[64,192]{1,0:T(8,128)(2,1)S(1)} copy-done((bf16[64,192]{1,0:T(8,128)(2,1)S(1)}, bf16[64,192]{1,0:T(8,128)(2,1)}, u32[]{:S(2)}) %copy-start.9) | copy-done | bytes 24600
  24.2 0.0 copy-start.10
  24.2 0.8 %copy-done.10 = bf16[64,192]{1,0:T(8,128)(2,1)S(1)} copy-done((bf16[64,192]{1,0:T(8,128)(2,1)S(1)}, bf16[64,192]{1,0:T(8,128)(2,1)}, u32[]{:S(2)}) %copy-start.10) | copy-done | bytes 24600
  25.0 1.1 %nonlinear.1 = f32[8,24,256]{2,1,0:T(8,128)} custom-call(f32[8,48,256]{2,1,0:T(8,128)S(1)} %all_to_all.10.fields, bf16[64,192]{1,0:T(8,128)(2,1)S(1)} %copy-done.10, bf16[64,192]{1,0:T(8,128)(2,1)S(1)} %copy-done.9), custom_call_target="tpu_custom_call" | custom-call | tf_op jit(solution)/shard_map/nonlinear/pallas_call | solution.py:258
  26.1 0.0 copy-start.8
  26.1 3.5 %all-to-all-start.1 = ((f32[8,24,256]{2,1,0:T(8,128)}), f32[8,24,256]{2,1,0:T(8,128)S(1)}, u32[]{:S(2)}, u32[]{:S(2)}) async-start(f32[8,24,256]{2,1,0:T(8,128)} %nonlinear.1), calls=%async_computation.1 | async-start | bytes 393216 | tf_op jit(solution)/shard_map/all_to_all | solution.py:261
  29.6 0.0 copy-start.7
  29.6 0.7 %copy-done.7 = f32[1024]{0:T(1024)S(1)} copy-done((f32[1024]{0:T(1024)S(1)}, f32[1024]{0:T(1024)}, u32[]{:S(2)}) %copy-start.7) | copy-done | bytes 4120
  30.3 0.0 copy-start.11
  30.3 0.7 %copy-done.11 = f32[1024]{0:T(1024)S(1)} copy-done((f32[1024]{0:T(1024)S(1)}, f32[1024]{0:T(1024)}, u32[]{:S(2)}) %copy-start.11) | copy-done | bytes 4120
  31.0 0.0 copy-start.13
  31.0 0.7 %copy-done.13 = f32[1024]{0:T(1024)S(1)} copy-done((f32[1024]{0:T(1024)S(1)}, f32[1024]{0:T(1024)}, u32[]{:S(2)}) %copy-start.13) | copy-done | bytes 4120
  31.7 0.0 copy-start.15
  31.7 0.8 %copy-done.15 = s32[6,1024]{1,0:T(8,128)S(1)} copy-done((s32[6,1024]{1,0:T(8,128)S(1)}, s32[6,1024]{1,0:T(8,128)}, u32[]{:S(2)}) %copy-start.15) | copy-done | bytes 24600
  32.5 0.0 copy-start.16
  32.5 0.7 %copy-done.16 = s32[1,128]{1,0:T(1,128)S(1)} copy-done((s32[1,128]{1,0:T(1,128)S(1)}, s32[1,128]{1,0:T(1,128)}, u32[]{:S(2)}) %copy-start.16) | copy-done | bytes 536
  33.1 0.0 copy-start.14
  33.1 3.1 %incidence.1 = (bf16[2048,1024]{1,0:T(8,128)(2,1)S(1)}, bf16[2048,128]{1,0:T(8,128)(2,1)S(1)}, f32[8,2048]{1,0:T(8,128)S(1)}) custom-call(s32[6,1024]{1,0:T(8,128)S(1)} %copy-done.15, f32[1,1024]{1,0:T(1,128)S(1)} %bitcast.4, f32[1,1024]{1,0:T(1,128)S(1)} %bitcast.8, f32[1,1024]{1,0:T(1,128)S(1)} %bitcast.11, s32[1,128]{1,0:T(1,128)S(1)} %copy-done.16), custom_call_target="tpu_custom_call" | custom-call | flops 2147483648 | bytes 8388608 | tf_op jit(solution)/shard_map/incidence/pallas_call | solution.py:251
  36.3 0.0 copy-start
  36.3 2.0 %copy-done = bf16[2048,1024]{1,0:T(8,128)(2,1)} copy-done((bf16[2048,1024]{1,0:T(8,128)(2,1)}, bf16[2048,1024]{1,0:T(8,128)(2,1)S(1)}, u32[]{:S(2)}) %copy-start) | copy-done | bytes 4194328
  38.2 0.0 all-to-all-done.1.forcing
  38.2 0.0 copy-done.8
  38.2 0.0 copy-start.1
  38.2 2.2 %copy-done.1 = bf16[2048,1024]{1,0:T(8,128)(2,1)S(1)} copy-done((bf16[2048,1024]{1,0:T(8,128)(2,1)S(1)}, bf16[2048,1024]{1,0:T(8,128)(2,1)}, u32[]{:S(2)}) %copy-start.1) | copy-done | bytes 4194328
  40.4 2.2 %rhs.1 = (f32[24,2048]{1,0:T(8,128)S(1)}, f32[24,128]{1,0:T(8,128)S(1)}) custom-call(f32[8,24,256]{2,1,0:T(8,128)S(1)} %all-to-all-done.1.forcing, bf16[2048,1024]{1,0:T(8,128)(2,1)S(1)} %copy-done.1, bf16[2048,128]{1,0:T(8,128)(2,1)S(1)} %get-tuple-element.14.at_iface, f32[8,2048]{1,0:T(8,128)S(1)} %get-tuple-element.15.diag, f32[1,1024]{1,0:T(1,128)S(1)} %bitcast.5), custom_call_target="tpu_custom_call" | custom-call | tf_op jit(solution)/shard_map/rhs/pallas_call | solution.py:270
  42.6 0.1 collective-permute-start
  42.7 1.2 %collective-permute-done.edge = f32[24,128]{1,0:T(8,128)S(1)} collective-permute-done((f32[24,128]{1,0:T(8,128)S(1)}, f32[24,128]{1,0:T(8,128)S(1)}, u32[]{:S(2)}, u32[]{:S(2)}) %collective-permute-start) | collective-permute-done | bytes 12320 | tf_op jit(solution)/shard_map/ppermute | solution.py:266
  43.9 0.0 copy-done.14
  43.9 0.0 copy-done.12
  43.9 0.0 copy-start.2
  43.9 2.2 %copy-done.2 = bf16[2048,1024]{1,0:T(8,128)(2,1)S(1)} copy-done((bf16[2048,1024]{1,0:T(8,128)(2,1)S(1)}, bf16[2048,1024]{1,0:T(8,128)(2,1)}, u32[]{:S(2)}) %copy-start.2) | copy-done | bytes 4194328
  46.1 2.5 %first.1 = (f32[24,2048]{1,0:T(8,128)S(1)}, f32[24,2048]{1,0:T(8,128)S(1)}, f32[24,1024]{1,0:T(8,128)S(1)}, f32[24,256]{1,0:T(8,128)S(1)}) custom-call(s32[1]{0:T(128)} %bitcast.place, f32[24,2048]{1,0:T(8,128)S(1)} %get-tuple-element.16.local, f32[24,128]{1,0:T(8,128)S(1)} %collective-permute-done.edge, bf16[2048,1024]{1,0:T(8,128)(2,1)S(1)} %copy-done.2, ...), custom_call_target="tpu_custom_call" | custom-call | tf_op jit(solution)/shard_map/first/pallas_call | solution.py:273
  48.6 0.2 collective-permute-start.1
  48.8 1.0 %collective-permute-done.1.edge = f32[24,256]{1,0:T(8,128)S(1)} collective-permute-done((f32[24,256]{1,0:T(8,128)S(1)}, f32[24,256]{1,0:T(8,128)S(1)}, u32[]{:S(2)}, u32[]{:S(2)}) %collective-permute-start.1) | collective-permute-done | bytes 24608 | tf_op jit(solution)/shard_map/ppermute | solution.py:266
  49.8 1.2 %second.1 = (f32[24,2048]{1,0:T(8,128)S(1)}, f32[24,128]{1,0:T(8,128)S(1)}) custom-call(s32[1]{0:T(128)} %bitcast.place, f32[24,2048]{1,0:T(8,128)S(1)} %get-tuple-element.19.image, f32[24,256]{1,0:T(8,128)S(1)} %collective-permute-done.1.edge, f32[24,256]{1,0:T(8,128)S(1)} %get-tuple-element.18.own, bf16[2048,1024]{1,0:T(8,128)(2,1)S(1)} %copy-done.2, ...), custom_call_target="tpu_custom_call" | custom-call | tf_op jit(solution)/shard_map/second/pallas_call | solution.py:281
  51.0 0.2 collective-permute-start.2
  51.2 1.0 %collective-permute-done.2.norms = f32[24,128]{1,0:T(8,128)S(1)} collective-permute-done((f32[24,128]{1,0:T(8,128)S(1)}, f32[24,128]{1,0:T(8,128)S(1)}, u32[]{:S(2)}, u32[]{:S(2)}) %collective-permute-start.2) | collective-permute-done | bytes 12320 | tf_op jit(solution)/shard_map/ppermute | solution.py:266
  52.2 1.0 %last.1 = (f32[3,2,2,2048]{3,2,1,0:T(2,128)}, f32[3,2,2,2048]{3,2,1,0:T(2,128)}) custom-call(f32[24,256]{1,0:T(8,128)S(1)} %collective-permute-done.1.edge, f32[24,256]{1,0:T(8,128)S(1)} %get-tuple-element.18.own, f32[24,128]{1,0:T(8,128)S(1)} %get-tuple-element.22.norms_own, f32[24,128]{1,0:T(8,128)S(1)} %collective-permute-done.2.norms, ...), custom_call_target="tpu_custom_call" | custom-call | tf_op jit(solution)/shard_map/last/pallas_call | solution.py:289
  (2 shorter events, 0.0 us)
Async XLA Ops:
  0.6 0.9 %copy-start.3 = (f32[3,2,2,2048]{3,2,1,0:T(2,128)S(1)}, f32[3,2,2,2048]{3,2,1,0:T(2,128)}, u32[]{:S(2)}) copy-start(f32[3,2,2,2048]{3,2,1,0:T(2,128)} %vel.1) | copy-start | bytes 294916
  1.5 0.9 %copy-start.4 = (f32[3,2,2,2048]{3,2,1,0:T(2,128)S(1)}, f32[3,2,2,2048]{3,2,1,0:T(2,128)}, u32[]{:S(2)}) copy-start(f32[3,2,2,2048]{3,2,1,0:T(2,128)} %mag.1) | copy-start | bytes 294916
  2.4 0.9 %copy-start.5 = (f32[3,2,2,2048]{3,2,1,0:T(2,128)S(1)}, f32[3,2,2,2048]{3,2,1,0:T(2,128)}, u32[]{:S(2)}) copy-start(f32[3,2,2,2048]{3,2,1,0:T(2,128)} %vort.1) | copy-start | bytes 294916
  3.3 0.9 %copy-start.6 = (f32[3,2,2,2048]{3,2,1,0:T(2,128)S(1)}, f32[3,2,2,2048]{3,2,1,0:T(2,128)}, u32[]{:S(2)}) copy-start(f32[3,2,2,2048]{3,2,1,0:T(2,128)} %cur.1) | copy-start | bytes 294916
  23.5 0.8 %copy-start.9 = (bf16[64,192]{1,0:T(8,128)(2,1)S(1)}, bf16[64,192]{1,0:T(8,128)(2,1)}, u32[]{:S(2)}) copy-start(bf16[64,192]{1,0:T(8,128)(2,1)} %constant.11.clone.analysis) | copy-start | bytes 73732
  24.2 0.8 %copy-start.10 = (bf16[64,192]{1,0:T(8,128)(2,1)S(1)}, bf16[64,192]{1,0:T(8,128)(2,1)}, u32[]{:S(2)}) copy-start(bf16[64,192]{1,0:T(8,128)(2,1)} %constant.10.clone.synthesis) | copy-start | bytes 73732
  26.1 12.1 %copy-start.8 = (f32[1024]{0:T(1024)S(1)}, f32[1024]{0:T(1024)}, u32[]{:S(2)}) copy-start(f32[1024]{0:T(1024)} %param.16) | copy-start | bytes 12292
  26.1 12.1 %all-to-all-start.1 = ((f32[8,24,256]{2,1,0:T(8,128)}), f32[8,24,256]{2,1,0:T(8,128)S(1)}, u32[]{:S(2)}, u32[]{:S(2)}) async-start(f32[8,24,256]{2,1,0:T(8,128)} %nonlinear.1), calls=%async_computation.1 | async-start | bytes 393216 | tf_op jit(solution)/shard_map/all_to_all | solution.py:261
  29.6 0.7 %copy-start.7 = (f32[1024]{0:T(1024)S(1)}, f32[1024]{0:T(1024)}, u32[]{:S(2)}) copy-start(f32[1024]{0:T(1024)} %param.16) | copy-start | bytes 12292
  30.3 0.7 %copy-start.11 = (f32[1024]{0:T(1024)S(1)}, f32[1024]{0:T(1024)}, u32[]{:S(2)}) copy-start(f32[1024]{0:T(1024)} %param.18) | copy-start | bytes 12292
  31.0 0.7 %copy-start.13 = (f32[1024]{0:T(1024)S(1)}, f32[1024]{0:T(1024)}, u32[]{:S(2)}) copy-start(f32[1024]{0:T(1024)} %param.17) | copy-start | bytes 12292
  31.7 0.8 %copy-start.15 = (s32[6,1024]{1,0:T(8,128)S(1)}, s32[6,1024]{1,0:T(8,128)}, u32[]{:S(2)}) copy-start(s32[6,1024]{1,0:T(8,128)} %elem_nodes.1) | copy-start | bytes 73732
  32.5 0.7 %copy-start.16 = (s32[1,128]{1,0:T(1,128)S(1)}, s32[1,128]{1,0:T(1,128)}, u32[]{:S(2)}) copy-start(s32[1,128]{1,0:T(1,128)} %iface.1) | copy-start | bytes 1540
  33.1 10.8 %copy-start.14 = (f32[1024]{0:T(1024)S(1)}, f32[1024]{0:T(1024)}, u32[]{:S(2)}) copy-start(f32[1024]{0:T(1024)} %param.17) | copy-start | bytes 12292
  36.3 2.0 %copy-start = (bf16[2048,1024]{1,0:T(8,128)(2,1)}, bf16[2048,1024]{1,0:T(8,128)(2,1)S(1)}, u32[]{:S(2)}) copy-start(bf16[2048,1024]{1,0:T(8,128)(2,1)S(1)} %get-tuple-element.13.touch) | copy-start | bytes 12582916
  38.2 5.7 %copy-start.12 = (f32[1024]{0:T(1024)S(1)}, f32[1024]{0:T(1024)}, u32[]{:S(2)}) copy-start(f32[1024]{0:T(1024)} %param.18) | copy-start | bytes 12292
  38.2 2.2 %copy-start.1 = (bf16[2048,1024]{1,0:T(8,128)(2,1)S(1)}, bf16[2048,1024]{1,0:T(8,128)(2,1)}, u32[]{:S(2)}) copy-start(bf16[2048,1024]{1,0:T(8,128)(2,1)} %copy-done) | copy-start | bytes 12582916
  42.6 1.2 %collective-permute-start = (f32[24,128]{1,0:T(8,128)S(1)}, f32[24,128]{1,0:T(8,128)S(1)}, u32[]{:S(2)}, u32[]{:S(2)}) collective-permute-start(f32[24,128]{1,0:T(8,128)S(1)} %get-tuple-element.17), channel_id=1, source_target_pairs={{0,1},{1,0},{2,3},{3,2},{4,5},{5,4},{6,7},{7,6},{8,9},{9,8},{10,11... | collective-permute-start | bytes 36872 | tf_op jit(solution)/shard_map/ppermute | solution.py:266
  43.9 2.2 %copy-start.2 = (bf16[2048,1024]{1,0:T(8,128)(2,1)S(1)}, bf16[2048,1024]{1,0:T(8,128)(2,1)}, u32[]{:S(2)}) copy-start(bf16[2048,1024]{1,0:T(8,128)(2,1)} %copy-done) | copy-start | bytes 12582916
  48.6 1.3 %collective-permute-start.1 = (f32[24,256]{1,0:T(8,128)S(1)}, f32[24,256]{1,0:T(8,128)S(1)}, u32[]{:S(2)}, u32[]{:S(2)}) collective-permute-start(f32[24,256]{1,0:T(8,128)S(1)} %get-tuple-element.18.own), channel_id=1, source_target_pairs={{0,1},{1,0},{2,3},{3,2},{4,5},{5,4},{6,7},{7,6},{8,9},{9,8},{10,11... | collective-permute-start | bytes 73736 | tf_op jit(solution)/shard_map/ppermute | solution.py:266
  51.0 1.2 %collective-permute-start.2 = (f32[24,128]{1,0:T(8,128)S(1)}, f32[24,128]{1,0:T(8,128)S(1)}, u32[]{:S(2)}, u32[]{:S(2)}) collective-permute-start(f32[24,128]{1,0:T(8,128)S(1)} %get-tuple-element.22.norms_own), channel_id=1, source_target_pairs={{0,1},{1,0},{2,3},{3,2},{4,5},{5,4},{6,7},{7,6},{8,9},{9,8},{10,11... | collective-permute-start | bytes 36872 | tf_op jit(solution)/shard_map/ppermute | solution.py:266
where the time goes:
time: 54 us; the launch traced here: 53.2 us
  blocking collectives  19.1 us (35%)
  local copies, waits for them, and re-layouts  14.9 us (28%)
  Pallas kernels  11.2 us (21%)
  starting transfers between devices  4.02 us (7%)
  waiting for transfers between devices  3.21 us (6%)
  between operations  0.71 us (1%)
    all_to_all x1, blocking collectives, per_device(): columns = lax.all_to_all(packed, 'mode', 0, 0, tiled=True)  19.1 us
    unnamed x34, local copies, waits for them, and re-layouts  14.9 us
    all_to_all x1, starting transfers between devices, per_device(): forcing = lax.all_to_all(terms, 'mode', 0, 0, tiled=True)  3.52 us
    ppermute x3, waiting for transfers between devices, swap(): return lax.ppermute(array, 'mer', [(0, 1), (1, 0)])  3.2 us
    pallas_call x1, Pallas kernels, per_device(): pl.pallas_call(mesh_kernel, out_shape=(shape(nodes, elems, kind=bf16), sh...  3.14 us
    pallas_call x1, Pallas kernels, per_device(): pl.pallas_call(functools.partial(first_kernel, per_dev, modes), in_specs=...  2.47 us
    pallas_call x1, Pallas kernels, per_device(): pl.pallas_call(rhs_kernel, out_shape=(shape(rows, nodes), shape(rows, sha...  2.21 us
    pallas_call x1, Pallas kernels, per_device(): pl.pallas_call(functools.partial(second_kernel, per_dev, modes), in_specs...  1.17 us
  transfers between devices with their start and end apart: 4, of which 3 were waited for; matrix products, arithmetic and copies ran while one was open for 0% of the time, Pallas kernels for 6%

commit v1 on v0

--- a/solution.py
+++ b/solution.py
@@ -13,11 +13,11 @@
 diffusion_ratio = 2.0
 f32 = jnp.float32
 bf16 = jnp.bfloat16
-vmem_limit = 16 * 2**20
-
-
-def params():
-    return pltpu.CompilerParams(vmem_limit_bytes=vmem_limit)
+small, medium, large = 16 * 2**20, 54 * 2**20, 60 * 2**20
+
+
+def params(limit=small):
+    return pltpu.CompilerParams(vmem_limit_bytes=limit)
 
 
 def halves(table):
@@ -71,21 +71,48 @@
     return jnp.dot(table, jnp.concatenate([high, low, high], axis=0), preferred_element_type=f32)
 
 
-def pack_kernel(vel, mag, vort, cur, out):
-    blocks, _, block = out.shape
+def start_all(sources, targets, sems):
+    copies = [
+        pltpu.make_async_copy(source, target, sems.at[i])
+        for i, (source, target) in enumerate(zip(sources, targets))
+    ]
+    for copy in copies:
+        copy.start()
+    return copies
+
+
+def pack_kernel(vel, mag, vort, cur, out, held, ready, in_sems, out_sems):
+    blocks, rows, block = out.shape
+    copies = start_all((vel, mag, vort, cur), [held.at[i] for i in range(4)], in_sems)
+    sent = []
     row = 0
-    for field in (vel, mag, vort, cur):
+    for i in range(4):
+        copies[i].wait()
+        field = held.at[i]
         comps, _, per_dev, _ = field.shape
         for c in range(comps):
             for s in range(2):
                 piece = field[c, s]
                 for b in range(blocks):
-                    out[b, row : row + per_dev, :] = piece[:, b * block : (b + 1) * block]
+                    ready[b, row : row + per_dev, :] = piece[:, b * block : (b + 1) * block]
                 row += per_dev
-
-
-def nonlinear_kernel(fields, synthesis, analysis, out):
+        if i % 2:
+            half = pl.ds(i // 2 * (rows // 2), rows // 2)
+            sent.append(pltpu.make_async_copy(ready.at[:, half, :], out.at[:, half, :], out_sems.at[i // 2]))
+            sent[-1].start()
+    for copy in sent:
+        copy.wait()
+
+
+def nonlinear_kernel(fields, synthesis, analysis, touch_hbm, iface_hbm, diag_hbm, coefs_hbm, out, touch, at_iface, diag, coefs, sems):
     owners, rows, block = fields.shape
+    part = touch.shape[0] // 4
+    spans = [pl.ds(i * part, part) for i in range(4)]
+    loads = start_all(
+        [touch_hbm.at[span, :] for span in spans] + [iface_hbm, diag_hbm, coefs_hbm],
+        [touch.at[span, :] for span in spans] + [at_iface, diag, coefs],
+        sems,
+    )
     pair = rows // 6
     angles = synthesis.shape[0] // 2
     phys = []
@@ -106,17 +133,24 @@
         for j in range(owners):
             span = slice(t * pair, (t + 1) * pair)
             out[j, span, :] = fields[j, span, :] + coef[j * pair : (j + 1) * pair]
-
-
-def mesh_kernel(elem_nodes, mass, radial, stiff, iface, touch, at_iface, diag):
+    for load in loads:
+        load.wait()
+
+
+def mesh_kernel(nodes_hbm, mass_hbm, radial_hbm, stiff_hbm, iface_hbm, touch_out, at_iface, diag, coefs, touch, elem_nodes, mass, radial, stiff, iface, in_sems, out_sems):
+    loads = start_all(
+        (nodes_hbm, mass_hbm, radial_hbm, stiff_hbm, iface_hbm), (elem_nodes, mass, radial, stiff, iface), in_sems
+    )
+    for load in loads:
+        load.wait()
     nodes, elems = touch.shape
     shared = iface.shape[1]
     fields = 8
     words = nodes // fields
     width = math.gcd(elems, 256)
-
-    def chunk(c, carry):
-        span = pl.ds(pl.multiple_of(c * width, width), width)
+    sent = []
+    for c in range(elems // width):
+        span = slice(c * width, (c + 1) * width)
         word = lax.broadcasted_iota(jnp.int32, (words, width), 0)
         total = jnp.zeros((words, width), jnp.int32)
         for i in range(elem_nodes.shape[0]):
@@ -127,31 +161,34 @@
         for q in range(fields):
             count = jnp.right_shift(total, 4 * q) & 15
             touch[q * words : (q + 1) * words, span] = count.astype(f32).astype(bf16)
-        return carry
-
-    lax.fori_loop(0, elems // width, chunk, 0)
+        column = pl.ds(c * width, width)
+        sent.append(pltpu.make_async_copy(touch.at[:, column], touch_out.at[:, column], out_sems.at[c]))
+        sent[-1].start()
     node = lax.broadcasted_iota(jnp.int32, (nodes, shared), 0)
     at_iface[...] = jnp.where(iface[...] == node, 1.0, 0.0).astype(bf16)
     zero = jnp.zeros((5, elems), f32)
-    coefs = jnp.concatenate([mass[...] / 12.0, radial[...] / 12.0, 6.0 * stiff[...], zero], axis=0)
-    sums = product(coefs, touch[...], 1, 3)
+    coefs[...] = jnp.concatenate([mass[...] / 12.0, radial[...] / 12.0, stiff[...], zero], axis=0)
+    scaled = jnp.concatenate([mass[...] / 12.0, radial[...] / 12.0, 6.0 * stiff[...], zero], axis=0)
+    sums = product(scaled, touch[...], 1, 3)
     ones = jnp.ones((16, shared), bf16)
     hits = lax.dot_general(ones, at_iface[...], (((1,), (1,)), ((), ())), preferred_element_type=f32)
     row = lax.broadcasted_iota(jnp.int32, (8, nodes), 0)
     diag[...] = jnp.where(row == 3, 1.0 - 0.5 * hits[:8], sums)
-
-
-def row_factors(place, rows, per_dev, modes):
+    for copy in sent:
+        copy.wait()
+
+
+def row_factors(rows, per_dev, modes):
     row = lax.broadcasted_iota(jnp.int32, (rows, 1), 0)
-    order = (place * per_dev + row % per_dev).astype(f32)
+    order = (lax.axis_index("mode") * per_dev + row % per_dev).astype(f32)
     shift = (order / modes) ** 2
     scale = jnp.where(row < rows // 2, 1.0, diffusion_ratio).astype(f32)
     return shift, scale
 
 
-def operator_parts(place, rows, per_dev, modes, mass, radial, stiff, diag):
-    shift, scale = row_factors(place[0], rows, per_dev, modes)
-    per_elem = (mass[...] + shift * radial[...]) / 12.0 - scale * stiff[...]
+def operator_parts(rows, per_dev, modes, coefs, diag):
+    shift, scale = row_factors(rows, per_dev, modes)
+    per_elem = coefs[0:1, :] + shift * coefs[1:2, :] - scale * coefs[2:3, :]
     per_node = diag[0:1, :] + shift * diag[1:2, :] + scale * diag[2:3, :]
     return per_elem, per_node
 
@@ -160,18 +197,18 @@
     return jnp.sum(array, axis=1, keepdims=True)
 
 
-def rhs_kernel(forcing, touch, at_iface, diag, mass, local, edge):
+def rhs_kernel(forcing, touch, at_iface, diag, coefs, local, edge):
     blocks = forcing.shape[0]
     given = jnp.concatenate([forcing[b] for b in range(blocks)], axis=1)
     sums = product(given, touch[...], 0)
-    image = diag[0:1, :] * given + product(sums * (mass[...] / 12.0), touch[...], 1)
+    image = diag[0:1, :] * given + product(sums * coefs[0:1, :], touch[...], 1)
     local[...] = image
     edge[...] = product(image, at_iface[...], 0, 3)
 
 
-def first_kernel(per_dev, modes, place, local, edge, touch, at_iface, diag, mass, radial, stiff, rhs_out, image_out, sums_out, edge_out):
+def first_kernel(per_dev, modes, local, edge, touch, at_iface, diag, coefs, rhs_out, image_out, sums_out, edge_out):
     rows, shared = edge.shape
-    per_elem, per_node = operator_parts(place, rows, per_dev, modes, mass, radial, stiff, diag)
+    per_elem, per_node = operator_parts(rows, per_dev, modes, coefs, diag)
     rhs = local[...] + product(edge[...], at_iface[...], 1, 3)
     rhs_out[...] = rhs
     sums = product(rhs, touch[...], 0)
@@ -186,10 +223,10 @@
     edge_out[:, shared:] = jnp.where(lane == 0, norm, curvature)
 
 
-def second_kernel(per_dev, modes, place, image, edge, own, touch, at_iface, diag, mass, radial, stiff, rhs, sums, resid_out, norms_out):
+def second_kernel(per_dev, modes, image, edge, own, touch, at_iface, diag, coefs, rhs, sums, resid_out, norms_out):
     rows = image.shape[0]
     shared = edge.shape[1] - 128
-    per_elem, per_node = operator_parts(place, rows, per_dev, modes, mass, radial, stiff, diag)
+    per_elem, per_node = operator_parts(rows, per_dev, modes, coefs, diag)
     norm = own[:, shared : shared + 1] + edge[:, shared : shared + 1]
     curvature = own[:, shared + 1 : shared + 2] + edge[:, shared + 1 : shared + 2]
     alpha = norm / curvature
@@ -234,30 +271,66 @@
     shared = iface.shape[1]
     mass, radial, stiff = (a.reshape(1, elems) for a in (mass_coef, radial_coef, stiff_coef))
     synthesis, analysis = trig_tables(modes, per_dev)
-    place = lax.axis_index("mode").astype(jnp.int32).reshape(1)
 
     def shape(*dims, kind=f32):
         return jax.ShapeDtypeStruct(dims, kind)
 
+    in_hbm = pl.BlockSpec(memory_space=pltpu.HBM)
     if block % 128 == 0:
         packed = pl.pallas_call(
-            pack_kernel, out_shape=shape(owners, 2 * rows, block), compiler_params=params(), name="pack"
+            pack_kernel,
+            in_specs=[in_hbm] * 4,
+            out_shape=shape(owners, 2 * rows, block),
+            out_specs=in_hbm,
+            scratch_shapes=[
+                pltpu.VMEM((4, *velocity.shape), f32),
+                pltpu.VMEM((owners, 2 * rows, block), f32),
+                pltpu.SemaphoreType.DMA((4,)),
+                pltpu.SemaphoreType.DMA((2,)),
+            ],
+            compiler_params=params(large),
+            name="pack",
         )(velocity, magnetic, vorticity, current)
     else:
         packed = jnp.concatenate(
             [a.reshape(rows // 2, owners, block) for a in (velocity, magnetic, vorticity, current)], axis=0
         ).transpose(1, 0, 2)
     columns = lax.all_to_all(packed, "mode", 0, 0, tiled=True)
-    touch, at_iface, diag = pl.pallas_call(
+    tables = (
+        shape(nodes, elems, kind=bf16),
+        shape(nodes, shared, kind=bf16),
+        shape(8, nodes),
+        shape(8, elems),
+    )
+    in_vmem = pl.BlockSpec(memory_space=pltpu.VMEM)
+    built = pl.pallas_call(
         mesh_kernel,
-        out_shape=(shape(nodes, elems, kind=bf16), shape(nodes, shared, kind=bf16), shape(8, nodes)),
-        compiler_params=params(),
+        in_specs=[in_hbm] * 5,
+        out_specs=(in_hbm, in_vmem, in_vmem, in_vmem),
+        out_shape=tables,
+        scratch_shapes=[
+            pltpu.VMEM((nodes, elems), bf16),
+            pltpu.VMEM(elem_nodes.shape, jnp.int32),
+            pltpu.VMEM((1, elems), f32),
+            pltpu.VMEM((1, elems), f32),
+            pltpu.VMEM((1, elems), f32),
+            pltpu.VMEM(iface.shape, jnp.int32),
+            pltpu.SemaphoreType.DMA((5,)),
+            pltpu.SemaphoreType.DMA((elems // math.gcd(elems, 256),)),
+        ],
+        compiler_params=params(large),
         name="incidence",
         cost_estimate=pl.CostEstimate(flops=2**31, bytes_accessed=2**23, transcendentals=0),
     )(elem_nodes, mass, radial, stiff, iface)
-    terms = pl.pallas_call(
-        nonlinear_kernel, out_shape=shape(owners, rows, block), compiler_params=params(), name="nonlinear"
-    )(columns, synthesis, analysis)
+    columns, *built = lax.optimization_barrier((columns, *built))
+    terms, touch, at_iface, diag, coefs = pl.pallas_call(
+        nonlinear_kernel,
+        in_specs=[in_vmem] * 3 + [in_hbm] * 4,
+        out_shape=(pltpu.VMEM((owners, rows, block), f32), *(pltpu.VMEM(t.shape, t.dtype) for t in tables)),
+        scratch_shapes=[pltpu.SemaphoreType.DMA((7,))],
+        compiler_params=params(medium),
+        name="nonlinear",
+    )(pltpu.with_memory_space_constraint(columns, pltpu.VMEM), synthesis, analysis, *built)
     forcing = lax.all_to_all(terms, "mode", 0, 0, tiled=True)
     if block % 128:
         forcing = forcing.transpose(1, 0, 2).reshape(1, rows, nodes)
@@ -265,26 +338,22 @@
     def swap(array):
         return lax.ppermute(array, "mer", [(0, 1), (1, 0)])
 
-    in_smem = pl.BlockSpec(memory_space=pltpu.SMEM)
-    in_vmem = pl.BlockSpec(memory_space=pltpu.VMEM)
     local, edge = pl.pallas_call(
         rhs_kernel, out_shape=(shape(rows, nodes), shape(rows, shared)), compiler_params=params(), name="rhs"
-    )(forcing, touch, at_iface, diag, mass)
+    )(forcing, touch, at_iface, diag, coefs)
     rhs, image, sums, edge_own = pl.pallas_call(
         functools.partial(first_kernel, per_dev, modes),
-        in_specs=[in_smem] + [in_vmem] * 8,
         out_shape=(shape(rows, nodes), shape(rows, nodes), shape(rows, elems), shape(rows, shared + 128)),
         compiler_params=params(),
         name="first",
-    )(place, local, swap(edge), touch, at_iface, diag, mass, radial, stiff)
+    )(local, swap(edge), touch, at_iface, diag, coefs)
     edge_other = swap(edge_own)
     resid, norms_own = pl.pallas_call(
         functools.partial(second_kernel, per_dev, modes),
-        in_specs=[in_smem] + [in_vmem] * 11,
         out_shape=(shape(rows, nodes), shape(rows, 128)),
         compiler_params=params(),
         name="second",
-    )(place, image, edge_other, edge_own, touch, at_iface, diag, mass, radial, stiff, rhs, sums)
+    )(image, edge_other, edge_own, touch, at_iface, diag, coefs, rhs, sums)
     out = shape(*velocity.shape)
     return pl.pallas_call(
         last_kernel, out_shape=(out, out), compiler_params=params(), name="last"

time: 54 us -> 46.7 us (0.86)
  local copies, waits for them, and re-layouts: 14.9 us -> 0 us
  blocking collectives: 19.1 us -> 11.2 us
  waiting for transfers between devices: 3.21 us -> 9.74 us
  Pallas kernels: 11.2 us -> 16.9 us
  starting transfers between devices: 4.02 us -> 7.77 us
    unnamed x34 -> x0, local copies, waits for them, and re-layouts: 14.9 us -> none
    all_to_all x1, blocking collectives: 19.1 us -> 11.2 us  [per_device(): forcing = lax.all_to_all(terms, 'mode', 0, 0, tiled=True)]
    all_to_all x1, waiting for transfers between devices: 0.01 us -> 6.53 us  [per_device(): columns = lax.all_to_all(packed, 'mode', 0, 0, tiled=True)]
    pallas_call x5, Pallas kernels: 8.02 us -> 13.7 us  [the longest x1 5.15 us: per_device(): pl.pallas_call(mesh_kernel, in_specs=[in_hbm] * 5, out_specs=(in_hbm, in_...]
    all_to_all x1, starting transfers between devices: 3.52 us -> 7.26 us  [per_device(): columns = lax.all_to_all(packed, 'mode', 0, 0, tiled=True)]
  transfers between devices with their start and end apart: 4 -> 4, of which waited for: 3 -> 4; matrix products, arithmetic and copies ran while one was open for 0% -> 0% of each run, Pallas kernels for 6% -> 11%
where the time goes in v1:
time: 46.7 us; the launch traced here: 46.3 us
  Pallas kernels  16.9 us (36%)
  blocking collectives  11.2 us (24%)
  waiting for transfers between devices  9.74 us (21%)
  starting transfers between devices  7.77 us (17%)
  between operations  0.68 us (1%)
    all_to_all x1, blocking collectives, per_device(): forcing = lax.all_to_all(terms, 'mode', 0, 0, tiled=True)  11.2 us
    all_to_all x1, starting transfers between devices, per_device(): columns = lax.all_to_all(packed, 'mode', 0, 0, tiled=True)  7.26 us
    all_to_all x1, waiting for transfers between devices, per_device(): columns = lax.all_to_all(packed, 'mode', 0, 0, tiled=True)  6.53 us
    pallas_call x1, Pallas kernels, per_device(): pl.pallas_call(mesh_kernel, in_specs=[in_hbm] * 5, out_specs=(in_hbm, in_...  5.15 us
    ppermute x3, waiting for transfers between devices, swap(): return lax.ppermute(array, 'mer', [(0, 1), (1, 0)])  3.21 us
    pallas_call x1, Pallas kernels, per_device(): pl.pallas_call(nonlinear_kernel, in_specs=[in_vmem] * 3 + [in_hbm] * 4, o...  3.14 us
    pallas_call x1, Pallas kernels, per_device(): pl.pallas_call(functools.partial(first_kernel, per_dev, modes), out_shape...  2.45 us
    pallas_call x1, Pallas kernels, per_device(): pl.pallas_call(rhs_kernel, out_shape=(shape(rows, nodes), shape(rows, sha...  2.21 us
  transfers between devices with their start and end apart: 4, of which 4 were waited for; matrix products, arithmetic and copies ran while one was open for 0% of the time, Pallas kernels for 11%

profile of v1, /device:TPU:0, one launch (start us, length us, event | category | flops | bytes accessed | tf_op | source)
XLA Modules:
  0.0 46.3 jit_solution(14115835168791375915)
XLA Ops:
  0.6 1.8 %pack.1 = f32[8,48,256]{2,1,0:T(8,128)} custom-call(f32[3,2,2,2048]{3,2,1,0:T(2,128)} %vel.1, f32[3,2,2,2048]{3,2,1,0:T(2,128)} %mag.1, f32[3,2,2,2048]{3,2,1,0:T(2,128)} %vort.1, f32[3,2,2,2048]{3,2,1,0:T(2,128)} %cur.1), custom_call_target="tpu_custom_call" | custom-call | tf_op jit(solution)/shard_map/pack/pallas_call | solution.py:280
  2.4 7.3 %all-to-all-start = ((f32[8,48,256]{2,1,0:T(8,128)}), f32[8,48,256]{2,1,0:T(8,128)S(1)}, u32[]{:S(2)}, u32[]{:S(2)}) async-start(f32[8,48,256]{2,1,0:T(8,128)} %pack.1), calls=%async_computation | async-start | bytes 786432 | tf_op jit(solution)/shard_map/all_to_all | solution.py:298
  9.7 5.2 %incidence.1 = (bf16[2048,1024]{1,0:T(8,128)(2,1)}, bf16[2048,128]{1,0:T(8,128)(2,1)}, f32[8,2048]{1,0:T(8,128)}, f32[8,1024]{1,0:T(8,128)}) custom-call(s32[6,1024]{1,0:T(8,128)} %nodes_hbm.1, f32[1,1024]{1,0:T(1,128)} %bitcast.3, f32[1,1024]{1,0:T(1,128)} %bitcast.4, f32[1,1024]{1,0:T(1,128)} %bitcast.5, s32[1,128]{1,0:T(1,128)} %iface_hbm.1), custom_call_target="tpu_custom_call" | custom-call | flops 2147483648 | bytes 8388608 | tf_op jit(solution)/shard_map/incidence/pallas_call | solution.py:306
  14.9 6.5 %all-to-all-done.fields = f32[8,48,256]{2,1,0:T(8,128)S(1)} async-done(((f32[8,48,256]{2,1,0:T(8,128)}), f32[8,48,256]{2,1,0:T(8,128)S(1)}, u32[]{:S(2)}, u32[]{:S(2)}) %all-to-all-start) | async-done | bytes 393248 | tf_op jit(solution)/shard_map/all_to_all | solution.py:298
  21.4 3.1 %nonlinear.1 = (f32[8,24,256]{2,1,0:T(8,128)S(1)}, bf16[2048,1024]{1,0:T(8,128)(2,1)S(1)}, bf16[2048,128]{1,0:T(8,128)(2,1)S(1)}, f32[8,2048]{1,0:T(8,128)S(1)}, f32[8,1024]{1,0:T(8,128)S(1)}) custom-call(f32[8,48,256]{2,1,0:T(8,128)S(1)} %all-to-all-done.fields, bf16[64,192]{1,0:T(8,128)(2,1)} %constant.4.clone.synthesis, ...), custom_call_target="tpu_custom_call" | custom-call | tf_op jit(solution)/shard_map/nonlinear/pallas_call | solution.py:326
  24.5 11.2 %all_to_all.10.forcing = f32[8,24,256]{2,1,0:T(8,128)S(1)} all-to-all(f32[8,24,256]{2,1,0:T(8,128)S(1)} %get-tuple-element.33), channel_id=1, replica_groups=mesh['runs'=2,'mode'=8,'mer'=2] {'mode'}, dimensions={0} | all-to-all | bytes 393216 | tf_op jit(solution)/shard_map/all_to_all | solution.py:334
  35.8 2.2 %rhs.1 = (f32[24,2048]{1,0:T(8,128)S(1)}, f32[24,128]{1,0:T(8,128)S(1)}) custom-call(f32[8,24,256]{2,1,0:T(8,128)S(1)} %all_to_all.10.forcing, bf16[2048,1024]{1,0:T(8,128)(2,1)S(1)} %get-tuple-element.34.touch, bf16[2048,128]{1,0:T(8,128)(2,1)S(1)} %get-tuple-element.35.at_iface, f32[8,2048]{1,0:T(8,128)S(1)} %get-tuple-element.36.diag, ...), custom_call_target="tpu_custom_call" | custom-call | tf_op jit(solution)/shard_map/rhs/pallas_call | solution.py:341
  38.0 0.1 collective-permute-start
  38.1 1.2 %collective-permute-done.edge = f32[24,128]{1,0:T(8,128)S(1)} collective-permute-done((f32[24,128]{1,0:T(8,128)S(1)}, f32[24,128]{1,0:T(8,128)S(1)}, u32[]{:S(2)}, u32[]{:S(2)}) %collective-permute-start) | collective-permute-done | bytes 12320 | tf_op jit(solution)/shard_map/ppermute | solution.py:339
  39.2 2.5 %first.1 = (f32[24,2048]{1,0:T(8,128)S(1)}, f32[24,2048]{1,0:T(8,128)S(1)}, f32[24,1024]{1,0:T(8,128)S(1)}, f32[24,256]{1,0:T(8,128)S(1)}) custom-call(f32[24,2048]{1,0:T(8,128)S(1)} %get-tuple-element.38.local, f32[24,128]{1,0:T(8,128)S(1)} %collective-permute-done.edge, bf16[2048,1024]{1,0:T(8,128)(2,1)S(1)} %get-tuple-element.34.touch, ...), custom_call_target="tpu_custom_call" | custom-call | tf_op jit(solution)/shard_map/first/pallas_call | solution.py:344
  41.7 0.2 collective-permute-start.1
  41.9 1.0 %collective-permute-done.1.edge = f32[24,256]{1,0:T(8,128)S(1)} collective-permute-done((f32[24,256]{1,0:T(8,128)S(1)}, f32[24,256]{1,0:T(8,128)S(1)}, u32[]{:S(2)}, u32[]{:S(2)}) %collective-permute-start.1) | collective-permute-done | bytes 24608 | tf_op jit(solution)/shard_map/ppermute | solution.py:339
  43.0 1.1 %second.1 = (f32[24,2048]{1,0:T(8,128)S(1)}, f32[24,128]{1,0:T(8,128)S(1)}) custom-call(f32[24,2048]{1,0:T(8,128)S(1)} %get-tuple-element.41.image, f32[24,256]{1,0:T(8,128)S(1)} %collective-permute-done.1.edge, f32[24,256]{1,0:T(8,128)S(1)} %get-tuple-element.40.own, bf16[2048,1024]{1,0:T(8,128)(2,1)S(1)} %get-tuple-element.34.touch, ...), custom_call_target="tpu_custom_call" | custom-call | tf_op jit(solution)/shard_map/second/pallas_call | solution.py:351
  44.1 0.2 collective-permute-start.2
  44.3 1.0 %collective-permute-done.2.norms = f32[24,128]{1,0:T(8,128)S(1)} collective-permute-done((f32[24,128]{1,0:T(8,128)S(1)}, f32[24,128]{1,0:T(8,128)S(1)}, u32[]{:S(2)}, u32[]{:S(2)}) %collective-permute-start.2) | collective-permute-done | bytes 12320 | tf_op jit(solution)/shard_map/ppermute | solution.py:339
  45.3 1.0 %last.1 = (f32[3,2,2,2048]{3,2,1,0:T(2,128)}, f32[3,2,2,2048]{3,2,1,0:T(2,128)}) custom-call(f32[24,256]{1,0:T(8,128)S(1)} %collective-permute-done.1.edge, f32[24,256]{1,0:T(8,128)S(1)} %get-tuple-element.40.own, f32[24,128]{1,0:T(8,128)S(1)} %get-tuple-element.44.norms_own, f32[24,128]{1,0:T(8,128)S(1)} %collective-permute-done.2.norms, ...), custom_call_target="tpu_custom_call" | custom-call | tf_op jit(solution)/shard_map/last/pallas_call | solution.py:358
Async XLA Ops:
  2.4 19.0 %all-to-all-start = ((f32[8,48,256]{2,1,0:T(8,128)}), f32[8,48,256]{2,1,0:T(8,128)S(1)}, u32[]{:S(2)}, u32[]{:S(2)}) async-start(f32[8,48,256]{2,1,0:T(8,128)} %pack.1), calls=%async_computation | async-start | bytes 786432 | tf_op jit(solution)/shard_map/all_to_all | solution.py:298
  38.0 1.2 %collective-permute-start = (f32[24,128]{1,0:T(8,128)S(1)}, f32[24,128]{1,0:T(8,128)S(1)}, u32[]{:S(2)}, u32[]{:S(2)}) collective-permute-start(f32[24,128]{1,0:T(8,128)S(1)} %get-tuple-element.39), channel_id=1, source_target_pairs={{0,1},{1,0},{2,3},{3,2},{4,5},{5,4},{6,7},{7,6},{8,9},{9,8},{10,11... | collective-permute-start | bytes 36872 | tf_op jit(solution)/shard_map/ppermute | solution.py:339
  41.7 1.3 %collective-permute-start.1 = (f32[24,256]{1,0:T(8,128)S(1)}, f32[24,256]{1,0:T(8,128)S(1)}, u32[]{:S(2)}, u32[]{:S(2)}) collective-permute-start(f32[24,256]{1,0:T(8,128)S(1)} %get-tuple-element.40.own), channel_id=1, source_target_pairs={{0,1},{1,0},{2,3},{3,2},{4,5},{5,4},{6,7},{7,6},{8,9},{9,8},{10,11... | collective-permute-start | bytes 73736 | tf_op jit(solution)/shard_map/ppermute | solution.py:339
  44.1 1.2 %collective-permute-start.2 = (f32[24,128]{1,0:T(8,128)S(1)}, f32[24,128]{1,0:T(8,128)S(1)}, u32[]{:S(2)}, u32[]{:S(2)}) collective-permute-start(f32[24,128]{1,0:T(8,128)S(1)} %get-tuple-element.44.norms_own), channel_id=1, source_target_pairs={{0,1},{1,0},{2,3},{3,2},{4,5},{5,4},{6,7},{7,6},{8,9},{9,8},{10,11... | collective-permute-start | bytes 36872 | tf_op jit(solution)/shard_map/ppermute | solution.py:339

commit v2 on v1

--- a/solution.py
+++ b/solution.py
@@ -104,15 +104,8 @@
         copy.wait()
 
 
-def nonlinear_kernel(fields, synthesis, analysis, touch_hbm, iface_hbm, diag_hbm, coefs_hbm, out, touch, at_iface, diag, coefs, sems):
+def nonlinear_kernel(fields, synthesis, analysis, out):
     owners, rows, block = fields.shape
-    part = touch.shape[0] // 4
-    spans = [pl.ds(i * part, part) for i in range(4)]
-    loads = start_all(
-        [touch_hbm.at[span, :] for span in spans] + [iface_hbm, diag_hbm, coefs_hbm],
-        [touch.at[span, :] for span in spans] + [at_iface, diag, coefs],
-        sems,
-    )
     pair = rows // 6
     angles = synthesis.shape[0] // 2
     phys = []
@@ -133,8 +126,6 @@
         for j in range(owners):
             span = slice(t * pair, (t + 1) * pair)
             out[j, span, :] = fields[j, span, :] + coef[j * pair : (j + 1) * pair]
-    for load in loads:
-        load.wait()
 
 
 def mesh_kernel(nodes_hbm, mass_hbm, radial_hbm, stiff_hbm, iface_hbm, touch_out, at_iface, diag, coefs, touch, elem_nodes, mass, radial, stiff, iface, in_sems, out_sems):
@@ -323,14 +314,14 @@
         cost_estimate=pl.CostEstimate(flops=2**31, bytes_accessed=2**23, transcendentals=0),
     )(elem_nodes, mass, radial, stiff, iface)
     columns, *built = lax.optimization_barrier((columns, *built))
-    terms, touch, at_iface, diag, coefs = pl.pallas_call(
+    touch, at_iface, diag, coefs = built
+    terms = pl.pallas_call(
         nonlinear_kernel,
-        in_specs=[in_vmem] * 3 + [in_hbm] * 4,
-        out_shape=(pltpu.VMEM((owners, rows, block), f32), *(pltpu.VMEM(t.shape, t.dtype) for t in tables)),
-        scratch_shapes=[pltpu.SemaphoreType.DMA((7,))],
-        compiler_params=params(medium),
+        out_shape=pltpu.VMEM((owners, rows, block), f32),
+        compiler_params=params(),
         name="nonlinear",
-    )(pltpu.with_memory_space_constraint(columns, pltpu.VMEM), synthesis, analysis, *built)
+        cost_estimate=pl.CostEstimate(flops=2**33, bytes_accessed=2**24, transcendentals=0),
+    )(pltpu.with_memory_space_constraint(columns, pltpu.VMEM), synthesis, analysis)
     forcing = lax.all_to_all(terms, "mode", 0, 0, tiled=True)
     if block % 128:
         forcing = forcing.transpose(1, 0, 2).reshape(1, rows, nodes)

time: 46.7 us -> 44.3 us (0.949)
  Pallas kernels: 16.9 us -> 14.1 us
    pallas_call x1, Pallas kernels: 3.14 us -> 0.41 us  [per_device(): pl.pallas_call(nonlinear_kernel, out_shape=pltpu.VMEM((owners, rows, bloc...]
  transfers between devices with their start and end apart: 4 -> 4, of which waited for: 4 -> 4; matrix products, arithmetic and copies ran while one was open for 0% -> 0% of each run, Pallas kernels for 11% -> 12%
where the time goes in v2:
time: 44.3 us; the launch traced here: 43.9 us
  Pallas kernels  14.1 us (32%)
  blocking collectives  11.5 us (26%)
  waiting for transfers between devices  9.75 us (22%)
  starting transfers between devices  7.77 us (18%)
  between operations  0.72 us (2%)
    all_to_all x1, blocking collectives, per_device(): forcing = lax.all_to_all(terms, 'mode', 0, 0, tiled=True)  11.5 us
    all_to_all x1, starting transfers between devices, per_device(): columns = lax.all_to_all(packed, 'mode', 0, 0, tiled=True)  7.26 us
    all_to_all x1, waiting for transfers between devices, per_device(): columns = lax.all_to_all(packed, 'mode', 0, 0, tiled=True)  6.54 us
    pallas_call x1, Pallas kernels, per_device(): pl.pallas_call(mesh_kernel, in_specs=[in_hbm] * 5, out_specs=(in_hbm, in_...  5.14 us
    ppermute x3, waiting for transfers between devices, swap(): return lax.ppermute(array, 'mer', [(0, 1), (1, 0)])  3.21 us
    pallas_call x1, Pallas kernels, per_device(): pl.pallas_call(functools.partial(first_kernel, per_dev, modes), out_shape...  2.45 us
    pallas_call x1, Pallas kernels, per_device(): pl.pallas_call(rhs_kernel, out_shape=(shape(rows, nodes), shape(rows, sha...  2.22 us
    pallas_call x1, Pallas kernels, per_device(): pl.pallas_call(pack_kernel, in_specs=[in_hbm] * 4, out_shape=shape(owners...  1.79 us
  transfers between devices with their start and end apart: 4, of which 4 were waited for; matrix products, arithmetic and copies ran while one was open for 0% of the time, Pallas kernels for 12%

profile of v2, /device:TPU:0, one launch (start us, length us, event | category | flops | bytes accessed | tf_op | source)
XLA Modules:
  0.0 43.9 jit_solution(15149355343904140805)
XLA Ops:
  0.6 1.8 %pack.1 = f32[8,48,256]{2,1,0:T(8,128)} custom-call(f32[3,2,2,2048]{3,2,1,0:T(2,128)} %vel.1, f32[3,2,2,2048]{3,2,1,0:T(2,128)} %mag.1, f32[3,2,2,2048]{3,2,1,0:T(2,128)} %vort.1, f32[3,2,2,2048]{3,2,1,0:T(2,128)} %cur.1), custom_call_target="tpu_custom_call" | custom-call | tf_op jit(solution)/shard_map/pack/pallas_call | solution.py:271
  2.4 0.0 copy-start.4
  2.4 0.0 copy-start.5
  2.5 7.3 %all-to-all-start = ((f32[8,48,256]{2,1,0:T(8,128)}), f32[8,48,256]{2,1,0:T(8,128)S(1)}, u32[]{:S(2)}, u32[]{:S(2)}) async-start(f32[8,48,256]{2,1,0:T(8,128)} %pack.1), calls=%async_computation | async-start | bytes 786432 | tf_op jit(solution)/shard_map/all_to_all | solution.py:289
  9.7 5.1 %incidence.1 = (bf16[2048,1024]{1,0:T(8,128)(2,1)}, bf16[2048,128]{1,0:T(8,128)(2,1)}, f32[8,2048]{1,0:T(8,128)}, f32[8,1024]{1,0:T(8,128)}) custom-call(s32[6,1024]{1,0:T(8,128)} %nodes_hbm.1, f32[1,1024]{1,0:T(1,128)} %bitcast.3, f32[1,1024]{1,0:T(1,128)} %bitcast.4, f32[1,1024]{1,0:T(1,128)} %bitcast.5, s32[1,128]{1,0:T(1,128)} %iface_hbm.1), custom_call_target="tpu_custom_call" | custom-call | flops 2147483648 | bytes 8388608 | tf_op jit(solution)/shard_map/incidence/pallas_call | solution.py:297
  14.9 6.5 %all-to-all-done.fields = f32[8,48,256]{2,1,0:T(8,128)S(1)} async-done(((f32[8,48,256]{2,1,0:T(8,128)}), f32[8,48,256]{2,1,0:T(8,128)S(1)}, u32[]{:S(2)}, u32[]{:S(2)}) %all-to-all-start) | async-done | bytes 393248 | tf_op jit(solution)/shard_map/all_to_all | solution.py:289
  21.4 0.0 copy-done.4
  21.4 0.0 copy-done.5
  21.4 0.0 copy-start
  21.4 0.0 copy-start.1
  21.4 0.0 copy-start.2
  21.4 0.0 copy-start.3
  21.4 0.4 nonlinear.1
  21.9 11.5 %all_to_all.10.forcing = f32[8,24,256]{2,1,0:T(8,128)S(1)} all-to-all(f32[8,24,256]{2,1,0:T(8,128)S(1)} %nonlinear.1), channel_id=1, replica_groups=mesh['runs'=2,'mode'=8,'mer'=2] {'mode'}, dimensions={0} | all-to-all | bytes 393216 | tf_op jit(solution)/shard_map/all_to_all | solution.py:325
  33.4 0.0 copy-done
  33.4 0.0 copy-done.1
  33.4 0.0 copy-done.2
  33.4 0.0 copy-done.3
  33.4 2.2 %rhs.1 = (f32[24,2048]{1,0:T(8,128)S(1)}, f32[24,128]{1,0:T(8,128)S(1)}) custom-call(f32[8,24,256]{2,1,0:T(8,128)S(1)} %all_to_all.10.forcing, bf16[2048,1024]{1,0:T(8,128)(2,1)S(1)} %copy-done, bf16[2048,128]{1,0:T(8,128)(2,1)S(1)} %copy-done.1, f32[8,2048]{1,0:T(8,128)S(1)} %copy-done.2, f32[8,1024]{1,0:T(8,128)S(1)} %copy-done.3), custom_call_target="tpu_custom_call" | custom-call | tf_op jit(solution)/shard_map/rhs/pallas_call | solution.py:332
  35.6 0.1 collective-permute-start
  35.7 1.2 %collective-permute-done.edge = f32[24,128]{1,0:T(8,128)S(1)} collective-permute-done((f32[24,128]{1,0:T(8,128)S(1)}, f32[24,128]{1,0:T(8,128)S(1)}, u32[]{:S(2)}, u32[]{:S(2)}) %collective-permute-start) | collective-permute-done | bytes 12320 | tf_op jit(solution)/shard_map/ppermute | solution.py:330
  36.8 2.5 %first.1 = (f32[24,2048]{1,0:T(8,128)S(1)}, f32[24,2048]{1,0:T(8,128)S(1)}, f32[24,1024]{1,0:T(8,128)S(1)}, f32[24,256]{1,0:T(8,128)S(1)}) custom-call(f32[24,2048]{1,0:T(8,128)S(1)} %get-tuple-element.28.local, f32[24,128]{1,0:T(8,128)S(1)} %collective-permute-done.edge, bf16[2048,1024]{1,0:T(8,128)(2,1)S(1)} %copy-done, bf16[2048,128]{1,0:T(8,128)(2,1)S(1)} %copy-done.1, ...), custom_call_target="tpu_custom_call" | custom-call | tf_op jit(solution)/shard_map/first/pallas_call | solution.py:335
  39.3 0.2 collective-permute-start.1
  39.5 1.0 %collective-permute-done.1.edge = f32[24,256]{1,0:T(8,128)S(1)} collective-permute-done((f32[24,256]{1,0:T(8,128)S(1)}, f32[24,256]{1,0:T(8,128)S(1)}, u32[]{:S(2)}, u32[]{:S(2)}) %collective-permute-start.1) | collective-permute-done | bytes 24608 | tf_op jit(solution)/shard_map/ppermute | solution.py:330
  40.6 1.1 %second.1 = (f32[24,2048]{1,0:T(8,128)S(1)}, f32[24,128]{1,0:T(8,128)S(1)}) custom-call(f32[24,2048]{1,0:T(8,128)S(1)} %get-tuple-element.31.image, f32[24,256]{1,0:T(8,128)S(1)} %collective-permute-done.1.edge, f32[24,256]{1,0:T(8,128)S(1)} %get-tuple-element.30.own, bf16[2048,1024]{1,0:T(8,128)(2,1)S(1)} %copy-done, bf16[2048,128]{1,0:T(8,128)(2,1)S(1)} %copy-done.1, ...), custom_call_target="tpu_custom_call" | custom-call | tf_op jit(solution)/shard_map/second/pallas_call | solution.py:342
  41.7 0.2 collective-permute-start.2
  41.9 1.0 %collective-permute-done.2.norms = f32[24,128]{1,0:T(8,128)S(1)} collective-permute-done((f32[24,128]{1,0:T(8,128)S(1)}, f32[24,128]{1,0:T(8,128)S(1)}, u32[]{:S(2)}, u32[]{:S(2)}) %collective-permute-start.2) | collective-permute-done | bytes 12320 | tf_op jit(solution)/shard_map/ppermute | solution.py:330
  42.9 1.0 %last.1 = (f32[3,2,2,2048]{3,2,1,0:T(2,128)}, f32[3,2,2,2048]{3,2,1,0:T(2,128)}) custom-call(f32[24,256]{1,0:T(8,128)S(1)} %collective-permute-done.1.edge, f32[24,256]{1,0:T(8,128)S(1)} %get-tuple-element.30.own, f32[24,128]{1,0:T(8,128)S(1)} %get-tuple-element.34.norms_own, f32[24,128]{1,0:T(8,128)S(1)} %collective-permute-done.2.norms, ...), custom_call_target="tpu_custom_call" | custom-call | tf_op jit(solution)/shard_map/last/pallas_call | solution.py:349
Async XLA Ops:
  2.4 19.0 %copy-start.4 = (bf16[64,192]{1,0:T(8,128)(2,1)S(1)}, bf16[64,192]{1,0:T(8,128)(2,1)}, u32[]{:S(2)}) copy-start(bf16[64,192]{1,0:T(8,128)(2,1)} %constant.5.clone.analysis) | copy-start | bytes 73732
  2.4 19.0 %copy-start.5 = (bf16[64,192]{1,0:T(8,128)(2,1)S(1)}, bf16[64,192]{1,0:T(8,128)(2,1)}, u32[]{:S(2)}) copy-start(bf16[64,192]{1,0:T(8,128)(2,1)} %constant.4.clone.synthesis) | copy-start | bytes 73732
  2.5 19.0 %all-to-all-start = ((f32[8,48,256]{2,1,0:T(8,128)}), f32[8,48,256]{2,1,0:T(8,128)S(1)}, u32[]{:S(2)}, u32[]{:S(2)}) async-start(f32[8,48,256]{2,1,0:T(8,128)} %pack.1), calls=%async_computation | async-start | bytes 786432 | tf_op jit(solution)/shard_map/all_to_all | solution.py:289
  21.4 11.9 %copy-start = (bf16[2048,1024]{1,0:T(8,128)(2,1)S(1)}, bf16[2048,1024]{1,0:T(8,128)(2,1)}, u32[]{:S(2)}) copy-start(bf16[2048,1024]{1,0:T(8,128)(2,1)} %get-tuple-element.24.touch) | copy-start | bytes 12582916
  21.4 11.9 %copy-start.1 = (bf16[2048,128]{1,0:T(8,128)(2,1)S(1)}, bf16[2048,128]{1,0:T(8,128)(2,1)}, u32[]{:S(2)}) copy-start(bf16[2048,128]{1,0:T(8,128)(2,1)} %get-tuple-element.25.at_iface) | copy-start | bytes 1572868
  21.4 11.9 %copy-start.2 = (f32[8,2048]{1,0:T(8,128)S(1)}, f32[8,2048]{1,0:T(8,128)}, u32[]{:S(2)}) copy-start(f32[8,2048]{1,0:T(8,128)} %get-tuple-element.26.diag) | copy-start | bytes 196612
  21.4 11.9 %copy-start.3 = (f32[8,1024]{1,0:T(8,128)S(1)}, f32[8,1024]{1,0:T(8,128)}, u32[]{:S(2)}) copy-start(f32[8,1024]{1,0:T(8,128)} %get-tuple-element.27.coefs) | copy-start | bytes 98308
  35.6 1.2 %collective-permute-start = (f32[24,128]{1,0:T(8,128)S(1)}, f32[24,128]{1,0:T(8,128)S(1)}, u32[]{:S(2)}, u32[]{:S(2)}) collective-permute-start(f32[24,128]{1,0:T(8,128)S(1)} %get-tuple-element.29), channel_id=1, source_target_pairs={{0,1},{1,0},{2,3},{3,2},{4,5},{5,4},{6,7},{7,6},{8,9},{9,8},{10,11... | collective-permute-start | bytes 36872 | tf_op jit(solution)/shard_map/ppermute | solution.py:330
  39.3 1.3 %collective-permute-start.1 = (f32[24,256]{1,0:T(8,128)S(1)}, f32[24,256]{1,0:T(8,128)S(1)}, u32[]{:S(2)}, u32[]{:S(2)}) collective-permute-start(f32[24,256]{1,0:T(8,128)S(1)} %get-tuple-element.30.own), channel_id=1, source_target_pairs={{0,1},{1,0},{2,3},{3,2},{4,5},{5,4},{6,7},{7,6},{8,9},{9,8},{10,11... | collective-permute-start | bytes 73736 | tf_op jit(solution)/shard_map/ppermute | solution.py:330
  41.7 1.2 %collective-permute-start.2 = (f32[24,128]{1,0:T(8,128)S(1)}, f32[24,128]{1,0:T(8,128)S(1)}, u32[]{:S(2)}, u32[]{:S(2)}) collective-permute-start(f32[24,128]{1,0:T(8,128)S(1)} %get-tuple-element.34.norms_own), channel_id=1, source_target_pairs={{0,1},{1,0},{2,3},{3,2},{4,5},{5,4},{6,7},{7,6},{8,9},{9,8},{10,11... | collective-permute-start | bytes 36872 | tf_op jit(solution)/shard_map/ppermute | solution.py:330

commit v3 on v2

--- a/solution.py
+++ b/solution.py
@@ -128,7 +128,7 @@
             out[j, span, :] = fields[j, span, :] + coef[j * pair : (j + 1) * pair]
 
 
-def mesh_kernel(nodes_hbm, mass_hbm, radial_hbm, stiff_hbm, iface_hbm, touch_out, at_iface, diag, coefs, touch, elem_nodes, mass, radial, stiff, iface, in_sems, out_sems):
+def mesh_kernel(nodes_hbm, mass_hbm, radial_hbm, stiff_hbm, iface_hbm, touch_out, at_iface, diag, coefs, edge_touch, edge_diag, touch, elem_nodes, mass, radial, stiff, iface, in_sems, out_sems):
     loads = start_all(
         (nodes_hbm, mass_hbm, radial_hbm, stiff_hbm, iface_hbm), (elem_nodes, mass, radial, stiff, iface), in_sems
     )
@@ -165,6 +165,9 @@
     hits = lax.dot_general(ones, at_iface[...], (((1,), (1,)), ((), ())), preferred_element_type=f32)
     row = lax.broadcasted_iota(jnp.int32, (8, nodes), 0)
     diag[...] = jnp.where(row == 3, 1.0 - 0.5 * hits[:8], sums)
+    edge_diag[...] = product(sums, at_iface[...], 0, 3)
+    counts = lax.dot_general(at_iface[...], touch[...], (((0,), (0,)), ((), ())), preferred_element_type=f32)
+    edge_touch[...] = counts.astype(bf16)
     for copy in sent:
         copy.wait()
 
@@ -177,59 +180,88 @@
     return shift, scale
 
 
-def operator_parts(rows, per_dev, modes, coefs, diag):
-    shift, scale = row_factors(rows, per_dev, modes)
-    per_elem = coefs[0:1, :] + shift * coefs[1:2, :] - scale * coefs[2:3, :]
-    per_node = diag[0:1, :] + shift * diag[1:2, :] + scale * diag[2:3, :]
-    return per_elem, per_node
+def at_elems(factors, coefs):
+    shift, scale = factors
+    return coefs[0:1, :] + shift * coefs[1:2, :] - scale * coefs[2:3, :]
+
+
+def at_nodes(factors, diag):
+    shift, scale = factors
+    return diag[0:1, :] + shift * diag[1:2, :] + scale * diag[2:3, :]
 
 
 def row_sum(array):
     return jnp.sum(array, axis=1, keepdims=True)
 
 
-def rhs_kernel(forcing, touch, at_iface, diag, coefs, local, edge):
-    blocks = forcing.shape[0]
-    given = jnp.concatenate([forcing[b] for b in range(blocks)], axis=1)
-    sums = product(given, touch[...], 0)
-    image = diag[0:1, :] * given + product(sums * coefs[0:1, :], touch[...], 1)
+def lanes(*columns):
+    rows = columns[0].shape[0]
+    lane = lax.broadcasted_iota(jnp.int32, (rows, 128), 1)
+    out = jnp.broadcast_to(columns[-1], (rows, 128))
+    for i in reversed(range(len(columns) - 1)):
+        out = jnp.where(lane == i, columns[i], out)
+    return out
+
+
+def together(forcing):
+    return jnp.concatenate([forcing[b] for b in range(forcing.shape[0])], axis=1)
+
+
+def rhs_edge_kernel(forcing, touch, at_iface, edge_touch, edge_diag, coefs, spread_out, edge):
+    given = together(forcing)
+    spread = product(given, touch[...], 0) * coefs[0:1, :]
+    spread_out[...] = spread
+    edge[...] = edge_diag[0:1, :] * product(given, at_iface[...], 0, 3) + product(spread, edge_touch[...], 1, 3)
+
+
+def rhs_kernel(per_dev, modes, forcing, spread, touch, diag, local, sums, inner):
+    rows = spread.shape[0]
+    image = diag[0:1, :] * together(forcing) + product(spread[...], touch[...], 1)
     local[...] = image
-    edge[...] = product(image, at_iface[...], 0, 3)
-
-
-def first_kernel(per_dev, modes, local, edge, touch, at_iface, diag, coefs, rhs_out, image_out, sums_out, edge_out):
+    sums[...] = product(image, touch[...], 0)
+    square = (2.0 * diag[3:4, :] - 1.0) * image * image
+    inner[...] = lanes(row_sum(square), row_sum(at_nodes(row_factors(rows, per_dev, modes), diag) * square))
+
+
+def image_edge_kernel(per_dev, modes, edge_own, edge, sums, inner, edge_touch, edge_diag, coefs, sums_out, out):
     rows, shared = edge.shape
-    per_elem, per_node = operator_parts(rows, per_dev, modes, coefs, diag)
+    factors = row_factors(rows, per_dev, modes)
+    rhs = edge_own[...] + edge[...]
+    full = sums[...] + product(edge[...], edge_touch[...], 0, 3)
+    sums_out[...] = full
+    spread = at_elems(factors, coefs) * full
+    image = at_nodes(factors, edge_diag) * rhs
+    norm = inner[:, 0:1] + 0.5 * row_sum(rhs * rhs)
+    curvature = inner[:, 1:2] + row_sum(image * rhs) + row_sum(spread * full)
+    out[:, :shared] = image + product(spread, edge_touch[...], 1, 3)
+    out[:, shared:] = lanes(norm, curvature)
+
+
+def image_kernel(per_dev, modes, local, edge, sums, touch, at_iface, diag, coefs, rhs_out, image_out, sums_out):
+    factors = row_factors(local.shape[0], per_dev, modes)
     rhs = local[...] + product(edge[...], at_iface[...], 1, 3)
     rhs_out[...] = rhs
-    sums = product(rhs, touch[...], 0)
-    sums_out[...] = sums
-    spread = per_elem * sums
-    image = per_node * rhs + product(spread, touch[...], 1)
+    image = at_nodes(factors, diag) * rhs + product(at_elems(factors, coefs) * sums[...], touch[...], 1)
     image_out[...] = image
-    norm = row_sum(diag[3:4, :] * rhs * rhs)
-    curvature = row_sum(per_node * rhs * rhs) + row_sum(spread * sums)
-    edge_out[:, :shared] = product(image, at_iface[...], 0, 3)
-    lane = lax.broadcasted_iota(jnp.int32, (rows, 128), 1)
-    edge_out[:, shared:] = jnp.where(lane == 0, norm, curvature)
-
-
-def second_kernel(per_dev, modes, image, edge, own, touch, at_iface, diag, coefs, rhs, sums, resid_out, norms_out):
-    rows = image.shape[0]
+    sums_out[...] = product(image, touch[...], 0)
+
+
+def resid_kernel(per_dev, modes, own, edge, rhs, image, sums, image_sums, at_iface, edge_touch, diag, coefs, resid_out, norms_out):
+    rows = rhs.shape[0]
     shared = edge.shape[1] - 128
-    per_elem, per_node = operator_parts(rows, per_dev, modes, coefs, diag)
+    factors = row_factors(rows, per_dev, modes)
+    per_elem, per_node = at_elems(factors, coefs), at_nodes(factors, diag)
     norm = own[:, shared : shared + 1] + edge[:, shared : shared + 1]
     curvature = own[:, shared + 1 : shared + 2] + edge[:, shared + 1 : shared + 2]
     alpha = norm / curvature
-    full = image[...] + product(edge[:, :shared], at_iface[...], 1, 3)
-    resid = rhs[...] - alpha * full
+    given = edge[:, :shared]
+    resid = rhs[...] - alpha * (image[...] + product(given, at_iface[...], 1, 3))
     resid_out[...] = resid
-    new = product(resid, touch[...], 0)
+    new = sums[...] - alpha * (image_sums[...] + product(given, edge_touch[...], 0, 3))
     after = row_sum(diag[3:4, :] * resid * resid)
     square = row_sum(per_node * resid * resid) + row_sum(per_elem * new * new)
     mixed = row_sum(per_node * resid * rhs[...]) + row_sum(per_elem * new * sums[...])
-    lane = lax.broadcasted_iota(jnp.int32, (rows, 128), 1)
-    norms_out[...] = jnp.where(lane == 0, after, jnp.where(lane == 1, square, mixed))
+    norms_out[...] = lanes(after, square, mixed)
 
 
 def last_kernel(edge, own, norms_own, norms, resid, rhs, vel_out, mag_out):
@@ -292,12 +324,14 @@
         shape(nodes, shared, kind=bf16),
         shape(8, nodes),
         shape(8, elems),
+        shape(shared, elems, kind=bf16),
+        shape(8, shared),
     )
     in_vmem = pl.BlockSpec(memory_space=pltpu.VMEM)
     built = pl.pallas_call(
         mesh_kernel,
         in_specs=[in_hbm] * 5,
-        out_specs=(in_hbm, in_vmem, in_vmem, in_vmem),
+        out_specs=(in_hbm, *[in_vmem] * 5),
         out_shape=tables,
         scratch_shapes=[
             pltpu.VMEM((nodes, elems), bf16),
@@ -314,7 +348,7 @@
         cost_estimate=pl.CostEstimate(flops=2**31, bytes_accessed=2**23, transcendentals=0),
     )(elem_nodes, mass, radial, stiff, iface)
     columns, *built = lax.optimization_barrier((columns, *built))
-    touch, at_iface, diag, coefs = built
+    touch, at_iface, diag, coefs, edge_touch, edge_diag = built
     terms = pl.pallas_call(
         nonlinear_kernel,
         out_shape=pltpu.VMEM((owners, rows, block), f32),
@@ -329,26 +363,37 @@
     def swap(array):
         return lax.ppermute(array, "mer", [(0, 1), (1, 0)])
 
-    local, edge = pl.pallas_call(
-        rhs_kernel, out_shape=(shape(rows, nodes), shape(rows, shared)), compiler_params=params(), name="rhs"
-    )(forcing, touch, at_iface, diag, coefs)
-    rhs, image, sums, edge_own = pl.pallas_call(
-        functools.partial(first_kernel, per_dev, modes),
-        out_shape=(shape(rows, nodes), shape(rows, nodes), shape(rows, elems), shape(rows, shared + 128)),
-        compiler_params=params(),
-        name="first",
-    )(local, swap(edge), touch, at_iface, diag, coefs)
-    edge_other = swap(edge_own)
-    resid, norms_own = pl.pallas_call(
-        functools.partial(second_kernel, per_dev, modes),
-        out_shape=(shape(rows, nodes), shape(rows, 128)),
-        compiler_params=params(),
-        name="second",
-    )(image, edge_other, edge_own, touch, at_iface, diag, coefs, rhs, sums)
+    def call(kernel, name, outs, work=0):
+        own = () if kernel is rhs_edge_kernel else (per_dev, modes)
+        cost = pl.CostEstimate(flops=work, bytes_accessed=work // 512, transcendentals=0) if work else None
+        return pl.pallas_call(
+            functools.partial(kernel, *own),
+            out_shape=tuple(outs),
+            compiler_params=params(),
+            name=name,
+            cost_estimate=cost,
+        )
+
+    full, part, small_row = shape(rows, nodes), shape(rows, elems), shape(rows, 128)
+    spread, edge_own = call(rhs_edge_kernel, "rhs_edge", (part, shape(rows, shared)))(
+        forcing, touch, at_iface, edge_touch, edge_diag, coefs
+    )
+    edge = swap(edge_own)
+    local, sums, inner = call(rhs_kernel, "rhs", (full, part, small_row), 2**30)(forcing, spread, touch, diag)
+    sums, image_edge_own = call(image_edge_kernel, "image_edge", (part, shape(rows, shared + 128)))(
+        edge_own, edge, sums, inner, edge_touch, edge_diag, coefs
+    )
+    image_edge = swap(image_edge_own)
+    rhs, image, image_sums = call(image_kernel, "image", (full, full, part), 2**30)(
+        local, edge, sums, touch, at_iface, diag, coefs
+    )
+    resid, norms_own = call(resid_kernel, "resid", (full, small_row))(
+        image_edge_own, image_edge, rhs, image, sums, image_sums, at_iface, edge_touch, diag, coefs
+    )
     out = shape(*velocity.shape)
     return pl.pallas_call(
         last_kernel, out_shape=(out, out), compiler_params=params(), name="last"
-    )(edge_other, edge_own, norms_own, swap(norms_own), resid, rhs)
+    )(image_edge, image_edge_own, norms_own, swap(norms_own), resid, rhs)
 
 
 def solution(mesh):

time: 44.3 us -> 43 us (0.971)
  waiting for transfers between devices: 9.75 us -> 7.62 us
  Pallas kernels: 14.1 us -> 14.7 us
    ppermute x3, waiting for transfers between devices: 3.21 us -> 1.16 us  [swap(): return lax.ppermute(array, 'mer', [(0, 1), (1, 0)])]
    pallas_call x4 -> x6, Pallas kernels: 11 us -> 11.5 us  [the longest x1 5.22 us: per_device(): pl.pallas_call(mesh_kernel, in_specs=[in_hbm] * 5, out_specs=(in_hbm, *[i...]
  transfers between devices with their start and end apart: 4 -> 4, of which waited for: 4 -> 2; matrix products, arithmetic and copies ran while one was open for 0% -> 0% of each run, Pallas kernels for 12% -> 23%
where the time goes in v3:
time: 43 us; the launch traced here: 42.6 us
  Pallas kernels  14.7 us (34%)
  blocking collectives  11.5 us (27%)
  starting transfers between devices  7.98 us (19%)
  waiting for transfers between devices  7.62 us (18%)
  between operations  0.78 us (2%)
    all_to_all x1, blocking collectives, per_device(): forcing = lax.all_to_all(terms, 'mode', 0, 0, tiled=True)  11.5 us
    all_to_all x1, starting transfers between devices, per_device(): columns = lax.all_to_all(packed, 'mode', 0, 0, tiled=True)  7.26 us
    all_to_all x1, waiting for transfers between devices, per_device(): columns = lax.all_to_all(packed, 'mode', 0, 0, tiled=True)  6.46 us
    pallas_call x1, Pallas kernels, per_device(): pl.pallas_call(mesh_kernel, in_specs=[in_hbm] * 5, out_specs=(in_hbm, *[i...  5.22 us
    pallas_call x1, Pallas kernels, per_device(): call(image_kernel, 'image', (full, full, part), 2 ** 30)  2.27 us
    pallas_call x1, Pallas kernels, per_device(): call(rhs_kernel, 'rhs', (full, part, small_row), 2 ** 30)  2.12 us
    pallas_call x1, Pallas kernels, per_device(): pl.pallas_call(pack_kernel, in_specs=[in_hbm] * 4, out_shape=shape(owners...  1.81 us
    ppermute x3, waiting for transfers between devices, swap(): return lax.ppermute(array, 'mer', [(0, 1), (1, 0)])  1.16 us
  transfers between devices with their start and end apart: 4, of which 2 were waited for; matrix products, arithmetic and copies ran while one was open for 0% of the time, Pallas kernels for 23%

profile of v3, /device:TPU:0, one launch (start us, length us, event | category | flops | bytes accessed | tf_op | source)
XLA Modules:
  0.0 42.6 jit_solution(1029873941328883464)
XLA Ops:
  0.6 1.8 %pack.1 = f32[8,48,256]{2,1,0:T(8,128)} custom-call(f32[3,2,2,2048]{3,2,1,0:T(2,128)} %vel.1, f32[3,2,2,2048]{3,2,1,0:T(2,128)} %mag.1, f32[3,2,2,2048]{3,2,1,0:T(2,128)} %vort.1, f32[3,2,2,2048]{3,2,1,0:T(2,128)} %cur.1), custom_call_target="tpu_custom_call" | custom-call | tf_op jit(solution)/shard_map/pack/pallas_call | solution.py:303
  2.4 0.0 copy-start.6
  2.5 0.0 copy-start.7
  2.5 7.3 %all-to-all-start = ((f32[8,48,256]{2,1,0:T(8,128)}), f32[8,48,256]{2,1,0:T(8,128)S(1)}, u32[]{:S(2)}, u32[]{:S(2)}) async-start(f32[8,48,256]{2,1,0:T(8,128)} %pack.1), calls=%async_computation | async-start | bytes 786432 | tf_op jit(solution)/shard_map/all_to_all | solution.py:321
  9.7 5.2 %incidence.1 = (bf16[2048,1024]{1,0:T(8,128)(2,1)}, bf16[2048,128]{1,0:T(8,128)(2,1)}, f32[8,2048]{1,0:T(8,128)}, f32[8,1024]{1,0:T(8,128)}, bf16[128,1024]{1,0:T(8,128)(2,1)}, /*index=5*/f32[8,128]{1,0:T(8,128)}) custom-call(s32[6,1024]{1,0:T(8,128)} %nodes_hbm.1, f32[1,1024]{1,0:T(1,128)} %bitcast.3, f32[1,1024]{1,0:T(1,128)} %bitcast.4, ...), custom_call_target="tpu_custom_call" | custom-call | flops 2147483648 | bytes 8388608 | tf_op jit(solution)/shard_map/incidence/pallas_call | solution.py:331
  15.0 6.5 %all-to-all-done.fields = f32[8,48,256]{2,1,0:T(8,128)S(1)} async-done(((f32[8,48,256]{2,1,0:T(8,128)}), f32[8,48,256]{2,1,0:T(8,128)S(1)}, u32[]{:S(2)}, u32[]{:S(2)}) %all-to-all-start) | async-done | bytes 393248 | tf_op jit(solution)/shard_map/all_to_all | solution.py:321
  21.4 0.0 copy-done.6
  21.4 0.0 copy-done.7
  21.4 0.0 copy-start
  21.4 0.0 copy-start.1
  21.4 0.0 copy-start.2
  21.5 0.0 copy-start.4
  21.5 0.0 copy-start.5
  21.5 0.4 nonlinear.1
  21.9 0.0 copy-start.3
  21.9 11.5 %all_to_all.10.forcing = f32[8,24,256]{2,1,0:T(8,128)S(1)} all-to-all(f32[8,24,256]{2,1,0:T(8,128)S(1)} %nonlinear.1), channel_id=1, replica_groups=mesh['runs'=2,'mode'=8,'mer'=2] {'mode'}, dimensions={0} | all-to-all | bytes 393216 | tf_op jit(solution)/shard_map/all_to_all | solution.py:359
  33.4 0.0 copy-done
  33.4 0.0 copy-done.1
  33.4 0.0 copy-done.2
  33.4 0.0 copy-done.4
  33.4 0.0 copy-done.5
  33.4 1.0 %rhs_edge.1 = (f32[24,1024]{1,0:T(8,128)S(1)}, f32[24,128]{1,0:T(8,128)S(1)}) custom-call(f32[8,24,256]{2,1,0:T(8,128)S(1)} %all_to_all.10.forcing, bf16[2048,1024]{1,0:T(8,128)(2,1)S(1)} %copy-done, bf16[2048,128]{1,0:T(8,128)(2,1)S(1)} %copy-done.1, bf16[128,1024]{1,0:T(8,128)(2,1)S(1)} %copy-done.2, f32[8,128]{1,0:T(8,128)S(1)} %copy-done.5, ...), custom_call_target="tpu_custom_call" | custom-call | tf_op jit(solution)/shard_map/rhs_edge/pallas_call | solution.py:378
  34.5 0.1 collective-permute-start
  34.5 0.0 copy-done.3
  34.6 2.1 %rhs.1 = (f32[24,2048]{1,0:T(8,128)S(1)}, f32[24,1024]{1,0:T(8,128)S(1)}, f32[24,128]{1,0:T(8,128)S(1)}) custom-call(f32[8,24,256]{2,1,0:T(8,128)S(1)} %all_to_all.10.forcing, f32[24,1024]{1,0:T(8,128)S(1)} %get-tuple-element.40.spread, bf16[2048,1024]{1,0:T(8,128)(2,1)S(1)} %copy-done, f32[8,2048]{1,0:T(8,128)S(1)} %copy-done.3), custom_call_target="tpu_custom_call" | custom-call | flops 1073741824 | bytes 2097152 | tf_op jit(solution)/shard_map/rhs/pallas_call | solution.py:382
  36.7 0.0 collective-permute-done.edge
  36.7 0.4 image_edge.1
  37.1 0.6 %collective-permute-start.1 = (f32[24,256]{1,0:T(8,128)S(1)}, f32[24,256]{1,0:T(8,128)S(1)}, u32[]{:S(2)}, u32[]{:S(2)}) collective-permute-start(f32[24,256]{1,0:T(8,128)S(1)} %get-tuple-element.44.own), channel_id=1, source_target_pairs={{0,1},{1,0},{2,3},{3,2},{4,5},{5,4},{6,7},{7,6},{8,9},{9,8},{10,11... | collective-permute-start | bytes 73736 | tf_op jit(solution)/shard_map/ppermute | solution.py:364
  37.6 2.3 %image.1 = (f32[24,2048]{1,0:T(8,128)S(1)}, f32[24,2048]{1,0:T(8,128)S(1)}, f32[24,1024]{1,0:T(8,128)S(1)}) custom-call(f32[24,2048]{1,0:T(8,128)S(1)} %get-tuple-element.45.local, f32[24,128]{1,0:T(8,128)S(1)} %collective-permute-done.edge, f32[24,1024]{1,0:T(8,128)S(1)} %get-tuple-element.46.sums, bf16[2048,1024]{1,0:T(8,128)(2,1)S(1)} %copy-done, ...), custom_call_target="tpu_custom_call" | custom-call | flops 1073741824 | bytes 2097152 | tf_op jit(solution)/shard_map/image/pallas_call | solution.py:387
  39.9 0.0 collective-permute-done.1.edge
  39.9 0.4 %resid.1 = (f32[24,2048]{1,0:T(8,128)S(1)}, f32[24,128]{1,0:T(8,128)S(1)}) custom-call(f32[24,256]{1,0:T(8,128)S(1)} %get-tuple-element.44.own, f32[24,256]{1,0:T(8,128)S(1)} %collective-permute-done.1.edge, f32[24,2048]{1,0:T(8,128)S(1)} %get-tuple-element.47.rhs, f32[24,2048]{1,0:T(8,128)S(1)} %get-tuple-element.48.image, ...), custom_call_target="tpu_custom_call" | custom-call | tf_op jit(solution)/shard_map/resid/pallas_call | solution.py:390
  40.3 0.1 collective-permute-start.2
  40.4 1.2 %collective-permute-done.2.norms = f32[24,128]{1,0:T(8,128)S(1)} collective-permute-done((f32[24,128]{1,0:T(8,128)S(1)}, f32[24,128]{1,0:T(8,128)S(1)}, u32[]{:S(2)}, u32[]{:S(2)}) %collective-permute-start.2) | collective-permute-done | bytes 12320 | tf_op jit(solution)/shard_map/ppermute | solution.py:364
  41.6 1.0 %last.1 = (f32[3,2,2,2048]{3,2,1,0:T(2,128)}, f32[3,2,2,2048]{3,2,1,0:T(2,128)}) custom-call(f32[24,256]{1,0:T(8,128)S(1)} %collective-permute-done.1.edge, f32[24,256]{1,0:T(8,128)S(1)} %get-tuple-element.44.own, f32[24,128]{1,0:T(8,128)S(1)} %get-tuple-element.50.norms_own, f32[24,128]{1,0:T(8,128)S(1)} %collective-permute-done.2.norms, ...), custom_call_target="tpu_custom_call" | custom-call | tf_op jit(solution)/shard_map/last/pallas_call | solution.py:394
Async XLA Ops:
  2.4 19.0 %copy-start.6 = (bf16[64,192]{1,0:T(8,128)(2,1)S(1)}, bf16[64,192]{1,0:T(8,128)(2,1)}, u32[]{:S(2)}) copy-start(bf16[64,192]{1,0:T(8,128)(2,1)} %constant.5.clone.analysis) | copy-start | bytes 73732
  2.5 19.0 %copy-start.7 = (bf16[64,192]{1,0:T(8,128)(2,1)S(1)}, bf16[64,192]{1,0:T(8,128)(2,1)}, u32[]{:S(2)}) copy-start(bf16[64,192]{1,0:T(8,128)(2,1)} %constant.4.clone.synthesis) | copy-start | bytes 73732
  2.5 19.0 %all-to-all-start = ((f32[8,48,256]{2,1,0:T(8,128)}), f32[8,48,256]{2,1,0:T(8,128)S(1)}, u32[]{:S(2)}, u32[]{:S(2)}) async-start(f32[8,48,256]{2,1,0:T(8,128)} %pack.1), calls=%async_computation | async-start | bytes 786432 | tf_op jit(solution)/shard_map/all_to_all | solution.py:321
  21.4 12.0 %copy-start = (bf16[2048,1024]{1,0:T(8,128)(2,1)S(1)}, bf16[2048,1024]{1,0:T(8,128)(2,1)}, u32[]{:S(2)}) copy-start(bf16[2048,1024]{1,0:T(8,128)(2,1)} %get-tuple-element.34.touch) | copy-start | bytes 12582916
  21.4 12.0 %copy-start.1 = (bf16[2048,128]{1,0:T(8,128)(2,1)S(1)}, bf16[2048,128]{1,0:T(8,128)(2,1)}, u32[]{:S(2)}) copy-start(bf16[2048,128]{1,0:T(8,128)(2,1)} %get-tuple-element.35.at_iface) | copy-start | bytes 1572868
  21.4 12.0 %copy-start.2 = (bf16[128,1024]{1,0:T(8,128)(2,1)S(1)}, bf16[128,1024]{1,0:T(8,128)(2,1)}, u32[]{:S(2)}) copy-start(bf16[128,1024]{1,0:T(8,128)(2,1)} %get-tuple-element.36.edge_touch) | copy-start | bytes 786436
  21.5 11.9 %copy-start.4 = (f32[8,1024]{1,0:T(8,128)S(1)}, f32[8,1024]{1,0:T(8,128)}, u32[]{:S(2)}) copy-start(f32[8,1024]{1,0:T(8,128)} %get-tuple-element.38.coefs) | copy-start | bytes 98308
  21.5 11.9 %copy-start.5 = (f32[8,128]{1,0:T(8,128)S(1)}, f32[8,128]{1,0:T(8,128)}, u32[]{:S(2)}) copy-start(f32[8,128]{1,0:T(8,128)} %get-tuple-element.37.edge_diag) | copy-start | bytes 12292
  21.9 12.7 %copy-start.3 = (f32[8,2048]{1,0:T(8,128)S(1)}, f32[8,2048]{1,0:T(8,128)}, u32[]{:S(2)}) copy-start(f32[8,2048]{1,0:T(8,128)} %get-tuple-element.41.diag) | copy-start | bytes 196612
  34.5 2.2 %collective-permute-start = (f32[24,128]{1,0:T(8,128)S(1)}, f32[24,128]{1,0:T(8,128)S(1)}, u32[]{:S(2)}, u32[]{:S(2)}) collective-permute-start(f32[24,128]{1,0:T(8,128)S(1)} %get-tuple-element.39.edge_own), channel_id=1, source_target_pairs={{0,1},{1,0},{2,3},{3,2},{4,5},{5,4},{6,7},{7,6},{8,9},{9,8},{10,11... | collective-permute-start | bytes 36872 | tf_op jit(solution)/shard_map/ppermute | solution.py:364
  37.1 2.8 %collective-permute-start.1 = (f32[24,256]{1,0:T(8,128)S(1)}, f32[24,256]{1,0:T(8,128)S(1)}, u32[]{:S(2)}, u32[]{:S(2)}) collective-permute-start(f32[24,256]{1,0:T(8,128)S(1)} %get-tuple-element.44.own), channel_id=1, source_target_pairs={{0,1},{1,0},{2,3},{3,2},{4,5},{5,4},{6,7},{7,6},{8,9},{9,8},{10,11... | collective-permute-start | bytes 73736 | tf_op jit(solution)/shard_map/ppermute | solution.py:364
  40.3 1.3 %collective-permute-start.2 = (f32[24,128]{1,0:T(8,128)S(1)}, f32[24,128]{1,0:T(8,128)S(1)}, u32[]{:S(2)}, u32[]{:S(2)}) collective-permute-start(f32[24,128]{1,0:T(8,128)S(1)} %get-tuple-element.50.norms_own), channel_id=1, source_target_pairs={{0,1},{1,0},{2,3},{3,2},{4,5},{5,4},{6,7},{7,6},{8,9},{9,8},{10,11... | collective-permute-start | bytes 36872 | tf_op jit(solution)/shard_map/ppermute | solution.py:364

commit v4 on v3

--- a/solution.py
+++ b/solution.py
@@ -54,11 +54,9 @@
     return jnp.concatenate(parts, axis=0).astype(bf16)
 
 
-def product(array, exact, contract, count=2):
+def product(array, exact, count=2):
     rows = array.shape[0]
-    out = lax.dot_general(
-        pieces(array, count), exact, (((1,), (contract,)), ((), ())), preferred_element_type=f32
-    )
+    out = jnp.dot(pieces(array, count), exact[...], preferred_element_type=f32)
     total = out[:rows]
     for i in range(1, count):
         total = total + out[i * rows : (i + 1) * rows]
@@ -128,7 +126,7 @@
             out[j, span, :] = fields[j, span, :] + coef[j * pair : (j + 1) * pair]
 
 
-def mesh_kernel(nodes_hbm, mass_hbm, radial_hbm, stiff_hbm, iface_hbm, touch_out, at_iface, diag, coefs, edge_touch, edge_diag, touch, elem_nodes, mass, radial, stiff, iface, in_sems, out_sems):
+def mesh_kernel(nodes_hbm, mass_hbm, radial_hbm, stiff_hbm, iface_hbm, touch_out, back_out, at_iface, from_iface, diag, coefs, edge_touch, edge_back, edge_diag, touch, back, elem_nodes, mass, radial, stiff, iface, in_sems, out_sems):
     loads = start_all(
         (nodes_hbm, mass_hbm, radial_hbm, stiff_hbm, iface_hbm), (elem_nodes, mass, radial, stiff, iface), in_sems
     )
@@ -155,19 +153,24 @@
         column = pl.ds(c * width, width)
         sent.append(pltpu.make_async_copy(touch.at[:, column], touch_out.at[:, column], out_sems.at[c]))
         sent[-1].start()
+        back[span, :] = touch[:, span].T
+        sent.append(pltpu.make_async_copy(back.at[column, :], back_out.at[column, :], out_sems.at[elems // width + c]))
+        sent[-1].start()
     node = lax.broadcasted_iota(jnp.int32, (nodes, shared), 0)
-    at_iface[...] = jnp.where(iface[...] == node, 1.0, 0.0).astype(bf16)
+    hit = jnp.where(iface[...] == node, 1.0, 0.0)
+    at_iface[...] = hit.astype(bf16)
+    from_iface[...] = hit.T.astype(bf16)
     zero = jnp.zeros((5, elems), f32)
     coefs[...] = jnp.concatenate([mass[...] / 12.0, radial[...] / 12.0, stiff[...], zero], axis=0)
     scaled = jnp.concatenate([mass[...] / 12.0, radial[...] / 12.0, 6.0 * stiff[...], zero], axis=0)
-    sums = product(scaled, touch[...], 1, 3)
-    ones = jnp.ones((16, shared), bf16)
-    hits = lax.dot_general(ones, at_iface[...], (((1,), (1,)), ((), ())), preferred_element_type=f32)
+    sums = product(scaled, back, 3)
+    hits = jnp.dot(jnp.ones((16, shared), bf16), from_iface[...], preferred_element_type=f32)
     row = lax.broadcasted_iota(jnp.int32, (8, nodes), 0)
     diag[...] = jnp.where(row == 3, 1.0 - 0.5 * hits[:8], sums)
-    edge_diag[...] = product(sums, at_iface[...], 0, 3)
-    counts = lax.dot_general(at_iface[...], touch[...], (((0,), (0,)), ((), ())), preferred_element_type=f32)
+    edge_diag[...] = product(sums, at_iface, 3)
+    counts = jnp.dot(from_iface[...], touch[...], preferred_element_type=f32)
     edge_touch[...] = counts.astype(bf16)
+    edge_back[...] = counts.T.astype(bf16)
     for copy in sent:
         copy.wait()
 
@@ -207,46 +210,46 @@
     return jnp.concatenate([forcing[b] for b in range(forcing.shape[0])], axis=1)
 
 
-def rhs_edge_kernel(forcing, touch, at_iface, edge_touch, edge_diag, coefs, spread_out, edge):
+def rhs_edge_kernel(forcing, touch, at_iface, edge_back, edge_diag, coefs, spread_out, edge):
     given = together(forcing)
-    spread = product(given, touch[...], 0) * coefs[0:1, :]
+    spread = product(given, touch) * coefs[0:1, :]
     spread_out[...] = spread
-    edge[...] = edge_diag[0:1, :] * product(given, at_iface[...], 0, 3) + product(spread, edge_touch[...], 1, 3)
-
-
-def rhs_kernel(per_dev, modes, forcing, spread, touch, diag, local, sums, inner):
+    edge[...] = edge_diag[0:1, :] * product(given, at_iface, 3) + product(spread, edge_back, 3)
+
+
+def rhs_kernel(per_dev, modes, forcing, spread, touch, back, diag, local, sums, inner):
     rows = spread.shape[0]
-    image = diag[0:1, :] * together(forcing) + product(spread[...], touch[...], 1)
+    image = diag[0:1, :] * together(forcing) + product(spread[...], back)
     local[...] = image
-    sums[...] = product(image, touch[...], 0)
+    sums[...] = product(image, touch)
     square = (2.0 * diag[3:4, :] - 1.0) * image * image
     inner[...] = lanes(row_sum(square), row_sum(at_nodes(row_factors(rows, per_dev, modes), diag) * square))
 
 
-def image_edge_kernel(per_dev, modes, edge_own, edge, sums, inner, edge_touch, edge_diag, coefs, sums_out, out):
+def image_edge_kernel(per_dev, modes, edge_own, edge, sums, inner, edge_touch, edge_back, edge_diag, coefs, sums_out, out):
     rows, shared = edge.shape
     factors = row_factors(rows, per_dev, modes)
     rhs = edge_own[...] + edge[...]
-    full = sums[...] + product(edge[...], edge_touch[...], 0, 3)
+    full = sums[...] + product(edge[...], edge_touch, 3)
     sums_out[...] = full
     spread = at_elems(factors, coefs) * full
     image = at_nodes(factors, edge_diag) * rhs
     norm = inner[:, 0:1] + 0.5 * row_sum(rhs * rhs)
     curvature = inner[:, 1:2] + row_sum(image * rhs) + row_sum(spread * full)
-    out[:, :shared] = image + product(spread, edge_touch[...], 1, 3)
+    out[:, :shared] = image + product(spread, edge_back, 3)
     out[:, shared:] = lanes(norm, curvature)
 
 
-def image_kernel(per_dev, modes, local, edge, sums, touch, at_iface, diag, coefs, rhs_out, image_out, sums_out):
+def image_kernel(per_dev, modes, local, edge, sums, touch, back, from_iface, diag, coefs, rhs_out, image_out, sums_out):
     factors = row_factors(local.shape[0], per_dev, modes)
-    rhs = local[...] + product(edge[...], at_iface[...], 1, 3)
+    rhs = local[...] + product(edge[...], from_iface, 3)
     rhs_out[...] = rhs
-    image = at_nodes(factors, diag) * rhs + product(at_elems(factors, coefs) * sums[...], touch[...], 1)
+    image = at_nodes(factors, diag) * rhs + product(at_elems(factors, coefs) * sums[...], back)
     image_out[...] = image
-    sums_out[...] = product(image, touch[...], 0)
-
-
-def resid_kernel(per_dev, modes, own, edge, rhs, image, sums, image_sums, at_iface, edge_touch, diag, coefs, resid_out, norms_out):
+    sums_out[...] = product(image, touch)
+
+
+def resid_kernel(per_dev, modes, own, edge, rhs, image, sums, image_sums, from_iface, edge_touch, diag, coefs, resid_out, norms_out):
     rows = rhs.shape[0]
     shared = edge.shape[1] - 128
     factors = row_factors(rows, per_dev, modes)
@@ -255,9 +258,9 @@
     curvature = own[:, shared + 1 : shared + 2] + edge[:, shared + 1 : shared + 2]
     alpha = norm / curvature
     given = edge[:, :shared]
-    resid = rhs[...] - alpha * (image[...] + product(given, at_iface[...], 1, 3))
+    resid = rhs[...] - alpha * (image[...] + product(given, from_iface, 3))
     resid_out[...] = resid
-    new = sums[...] - alpha * (image_sums[...] + product(given, edge_touch[...], 0, 3))
+    new = sums[...] - alpha * (image_sums[...] + product(given, edge_touch, 3))
     after = row_sum(diag[3:4, :] * resid * resid)
     square = row_sum(per_node * resid * resid) + row_sum(per_elem * new * new)
     mixed = row_sum(per_node * resid * rhs[...]) + row_sum(per_elem * new * sums[...])
@@ -321,34 +324,38 @@
     columns = lax.all_to_all(packed, "mode", 0, 0, tiled=True)
     tables = (
         shape(nodes, elems, kind=bf16),
+        shape(elems, nodes, kind=bf16),
         shape(nodes, shared, kind=bf16),
+        shape(shared, nodes, kind=bf16),
         shape(8, nodes),
         shape(8, elems),
         shape(shared, elems, kind=bf16),
+        shape(elems, shared, kind=bf16),
         shape(8, shared),
     )
     in_vmem = pl.BlockSpec(memory_space=pltpu.VMEM)
     built = pl.pallas_call(
         mesh_kernel,
         in_specs=[in_hbm] * 5,
-        out_specs=(in_hbm, *[in_vmem] * 5),
+        out_specs=(in_hbm, in_hbm, *[in_vmem] * 7),
         out_shape=tables,
         scratch_shapes=[
             pltpu.VMEM((nodes, elems), bf16),
+            pltpu.VMEM((elems, nodes), bf16),
             pltpu.VMEM(elem_nodes.shape, jnp.int32),
             pltpu.VMEM((1, elems), f32),
             pltpu.VMEM((1, elems), f32),
             pltpu.VMEM((1, elems), f32),
             pltpu.VMEM(iface.shape, jnp.int32),
             pltpu.SemaphoreType.DMA((5,)),
-            pltpu.SemaphoreType.DMA((elems // math.gcd(elems, 256),)),
+            pltpu.SemaphoreType.DMA((2 * elems // math.gcd(elems, 256),)),
         ],
         compiler_params=params(large),
         name="incidence",
         cost_estimate=pl.CostEstimate(flops=2**31, bytes_accessed=2**23, transcendentals=0),
     )(elem_nodes, mass, radial, stiff, iface)
     columns, *built = lax.optimization_barrier((columns, *built))
-    touch, at_iface, diag, coefs, edge_touch, edge_diag = built
+    touch, back, at_iface, from_iface, diag, coefs, edge_touch, edge_back, edge_diag = built
     terms = pl.pallas_call(
         nonlinear_kernel,
         out_shape=pltpu.VMEM((owners, rows, block), f32),
@@ -376,19 +383,21 @@
 
     full, part, small_row = shape(rows, nodes), shape(rows, elems), shape(rows, 128)
     spread, edge_own = call(rhs_edge_kernel, "rhs_edge", (part, shape(rows, shared)))(
-        forcing, touch, at_iface, edge_touch, edge_diag, coefs
+        forcing, touch, at_iface, edge_back, edge_diag, coefs
     )
     edge = swap(edge_own)
-    local, sums, inner = call(rhs_kernel, "rhs", (full, part, small_row), 2**30)(forcing, spread, touch, diag)
+    local, sums, inner = call(rhs_kernel, "rhs", (full, part, small_row), 2**30)(
+        forcing, spread, touch, back, diag
+    )
     sums, image_edge_own = call(image_edge_kernel, "image_edge", (part, shape(rows, shared + 128)))(
-        edge_own, edge, sums, inner, edge_touch, edge_diag, coefs
+        edge_own, edge, sums, inner, edge_touch, edge_back, edge_diag, coefs
     )
     image_edge = swap(image_edge_own)
     rhs, image, image_sums = call(image_kernel, "image", (full, full, part), 2**30)(
-        local, edge, sums, touch, at_iface, diag, coefs
+        local, edge, sums, touch, back, from_iface, diag, coefs
     )
     resid, norms_own = call(resid_kernel, "resid", (full, small_row))(
-        image_edge_own, image_edge, rhs, image, sums, image_sums, at_iface, edge_touch, diag, coefs
+        image_edge_own, image_edge, rhs, image, sums, image_sums, from_iface, edge_touch, diag, coefs
     )
     out = shape(*velocity.shape)
     return pl.pallas_call(

time: 43 us -> 41.8 us (0.972)
  waiting for transfers between devices: 7.62 us -> 6.93 us
  Pallas kernels: 14.7 us -> 14.2 us
    all_to_all x1, waiting for transfers between devices: 6.46 us -> 5.8 us  [per_device(): columns = lax.all_to_all(packed, 'mode', 0, 0, tiled=True)]
    pallas_call x1, Pallas kernels: 5.22 us -> 5.89 us  [per_device(): pl.pallas_call(mesh_kernel, in_specs=[in_hbm] * 5, out_specs=(in_hbm, in_...]
    pallas_call x1, Pallas kernels: 2.27 us -> 1.7 us  [per_device(): call(image_kernel, 'image', (full, full, part), 2 ** 30)]
    pallas_call x1, Pallas kernels: 2.12 us -> 1.61 us  [per_device(): call(rhs_kernel, 'rhs', (full, part, small_row), 2 ** 30)]
  transfers between devices with their start and end apart: 4 -> 4, of which waited for: 2 -> 2; matrix products, arithmetic and copies ran while one was open for 0% -> 0% of each run, Pallas kernels for 23% -> 22%
where the time goes in v4:
time: 41.8 us; the launch traced here: 41.4 us
  Pallas kernels  14.2 us (34%)
  blocking collectives  11.5 us (28%)
  starting transfers between devices  7.98 us (19%)
  waiting for transfers between devices  6.93 us (17%)
  between operations  0.83 us (2%)
    all_to_all x1, blocking collectives, per_device(): forcing = lax.all_to_all(terms, 'mode', 0, 0, tiled=True)  11.5 us
    all_to_all x1, starting transfers between devices, per_device(): columns = lax.all_to_all(packed, 'mode', 0, 0, tiled=True)  7.26 us
    pallas_call x1, Pallas kernels, per_device(): pl.pallas_call(mesh_kernel, in_specs=[in_hbm] * 5, out_specs=(in_hbm, in_...  5.89 us
    all_to_all x1, waiting for transfers between devices, per_device(): columns = lax.all_to_all(packed, 'mode', 0, 0, tiled=True)  5.8 us
    pallas_call x1, Pallas kernels, per_device(): pl.pallas_call(pack_kernel, in_specs=[in_hbm] * 4, out_shape=shape(owners...  1.8 us
    pallas_call x1, Pallas kernels, per_device(): call(image_kernel, 'image', (full, full, part), 2 ** 30)  1.7 us
    pallas_call x1, Pallas kernels, per_device(): call(rhs_kernel, 'rhs', (full, part, small_row), 2 ** 30)  1.61 us
    ppermute x3, waiting for transfers between devices, swap(): return lax.ppermute(array, 'mer', [(0, 1), (1, 0)])  1.14 us
  transfers between devices with their start and end apart: 4, of which 2 were waited for; matrix products, arithmetic and copies ran while one was open for 0% of the time, Pallas kernels for 22%

profile of v4, /device:TPU:0, one launch (start us, length us, event | category | flops | bytes accessed | tf_op | source)
XLA Modules:
  0.0 41.4 jit_solution(7037207319157563811)
XLA Ops:
  0.6 1.8 %pack.1 = f32[8,48,256]{2,1,0:T(8,128)} custom-call(f32[3,2,2,2048]{3,2,1,0:T(2,128)} %vel.1, f32[3,2,2,2048]{3,2,1,0:T(2,128)} %mag.1, f32[3,2,2,2048]{3,2,1,0:T(2,128)} %vort.1, f32[3,2,2,2048]{3,2,1,0:T(2,128)} %cur.1), custom_call_target="tpu_custom_call" | custom-call | tf_op jit(solution)/shard_map/pack/pallas_call | solution.py:306
  2.4 0.0 copy-start.9
  2.5 0.0 copy-start.10
  2.5 7.3 %all-to-all-start = ((f32[8,48,256]{2,1,0:T(8,128)}), f32[8,48,256]{2,1,0:T(8,128)S(1)}, u32[]{:S(2)}, u32[]{:S(2)}) async-start(f32[8,48,256]{2,1,0:T(8,128)} %pack.1), calls=%async_computation | async-start | bytes 786432 | tf_op jit(solution)/shard_map/all_to_all | solution.py:324
  9.7 5.9 %incidence.1 = (bf16[2048,1024]{1,0:T(8,128)(2,1)}, bf16[1024,2048]{1,0:T(8,128)(2,1)}, bf16[2048,128]{1,0:T(8,128)(2,1)}, bf16[128,2048]{1,0:T(8,128)(2,1)}, f3...) custom-call(s32[6,1024]{1,0:T(8,128)} %nodes_hbm.1, ...), custom_call_target="tpu_custom_call" | custom-call | flops 2147483648 | bytes 8388608 | tf_op jit(solution)/shard_map/incidence/pallas_call | solution.py:337
  15.6 5.8 %all-to-all-done.fields = f32[8,48,256]{2,1,0:T(8,128)S(1)} async-done(((f32[8,48,256]{2,1,0:T(8,128)}), f32[8,48,256]{2,1,0:T(8,128)S(1)}, u32[]{:S(2)}, u32[]{:S(2)}) %all-to-all-start) | async-done | bytes 393248 | tf_op jit(solution)/shard_map/all_to_all | solution.py:324
  21.4 0.0 copy-done.9
  21.4 0.0 copy-done.10
  21.4 0.0 copy-start
  21.4 0.0 copy-start.3
  21.4 0.0 copy-start.6
  21.4 0.0 copy-start.7
  21.5 0.0 copy-start.8
  21.5 0.4 %nonlinear.1 = f32[8,24,256]{2,1,0:T(8,128)S(1)} custom-call(f32[8,48,256]{2,1,0:T(8,128)S(1)} %all-to-all-done.fields, bf16[64,192]{1,0:T(8,128)(2,1)S(1)} %copy-done.10, bf16[64,192]{1,0:T(8,128)(2,1)S(1)} %copy-done.9), custom_call_target="tpu_custom_call" | custom-call | flops 8589934592 | bytes 16777216 | tf_op jit(solution)/shard_map/nonlinear/pallas_call | solution.py:359
  21.9 0.0 copy-start.1
  21.9 0.0 copy-start.5
  21.9 11.5 %all_to_all.10.forcing = f32[8,24,256]{2,1,0:T(8,128)S(1)} all-to-all(f32[8,24,256]{2,1,0:T(8,128)S(1)} %nonlinear.1), channel_id=1, replica_groups=mesh['runs'=2,'mode'=8,'mer'=2] {'mode'}, dimensions={0} | all-to-all | bytes 393216 | tf_op jit(solution)/shard_map/all_to_all | solution.py:366
  33.4 0.0 copy-done
  33.4 0.0 copy-done.3
  33.4 0.0 copy-done.6
  33.4 0.0 copy-done.7
  33.4 0.0 copy-done.8
  33.4 1.0 %rhs_edge.1 = (f32[24,1024]{1,0:T(8,128)S(1)}, f32[24,128]{1,0:T(8,128)S(1)}) custom-call(f32[8,24,256]{2,1,0:T(8,128)S(1)} %all_to_all.10.forcing, bf16[2048,1024]{1,0:T(8,128)(2,1)S(1)} %copy-done, bf16[2048,128]{1,0:T(8,128)(2,1)S(1)} %copy-done.7, bf16[1024,128]{1,0:T(8,128)(2,1)S(1)} %copy-done.3, f32[8,128]{1,0:T(8,128)S(1)} %copy-done.8, ...), custom_call_target="tpu_custom_call" | custom-call | tf_op jit(solution)/shard_map/rhs_edge/pallas_call | solution.py:385
  34.5 0.1 collective-permute-start
  34.5 0.0 copy-done.1
  34.5 0.0 copy-done.5
  34.6 0.0 copy-start.4
  34.6 0.0 copy-start.2
  34.6 1.6 %rhs.1 = (f32[24,2048]{1,0:T(8,128)S(1)}, f32[24,1024]{1,0:T(8,128)S(1)}, f32[24,128]{1,0:T(8,128)S(1)}) custom-call(f32[8,24,256]{2,1,0:T(8,128)S(1)} %all_to_all.10.forcing, f32[24,1024]{1,0:T(8,128)S(1)} %get-tuple-element.49.spread, bf16[2048,1024]{1,0:T(8,128)(2,1)S(1)} %copy-done, bf16[1024,2048]{1,0:T(8,128)(2,1)S(1)} %copy-done.1, ...), custom_call_target="tpu_custom_call" | custom-call | flops 1073741824 | bytes 2097152 | tf_op jit(solution)/shard_map/rhs/pallas_call | solution.py:389
  36.2 0.0 collective-permute-done.edge
  36.2 0.0 copy-done.4
  36.2 0.4 image_edge.1
  36.6 0.5 %collective-permute-start.1 = (f32[24,256]{1,0:T(8,128)S(1)}, f32[24,256]{1,0:T(8,128)S(1)}, u32[]{:S(2)}, u32[]{:S(2)}) collective-permute-start(f32[24,256]{1,0:T(8,128)S(1)} %get-tuple-element.55.own), channel_id=1, source_target_pairs={{0,1},{1,0},{2,3},{3,2},{4,5},{5,4},{6,7},{7,6},{8,9},{9,8},{10,11... | collective-permute-start | bytes 73736 | tf_op jit(solution)/shard_map/ppermute | solution.py:371
  37.1 0.0 copy-done.2
  37.1 1.7 %image.1 = (f32[24,2048]{1,0:T(8,128)S(1)}, f32[24,2048]{1,0:T(8,128)S(1)}, f32[24,1024]{1,0:T(8,128)S(1)}) custom-call(f32[24,2048]{1,0:T(8,128)S(1)} %get-tuple-element.56.local, f32[24,128]{1,0:T(8,128)S(1)} %collective-permute-done.edge, f32[24,1024]{1,0:T(8,128)S(1)} %get-tuple-element.57.sums, bf16[2048,1024]{1,0:T(8,128)(2,1)S(1)} %copy-done, ...), custom_call_target="tpu_custom_call" | custom-call | flops 1073741824 | bytes 2097152 | tf_op jit(solution)/shard_map/image/pallas_call | solution.py:396
  38.8 0.0 collective-permute-done.1.edge
  38.8 0.4 resid.1
  39.2 0.1 collective-permute-start.2
  39.3 1.1 %collective-permute-done.2.norms = f32[24,128]{1,0:T(8,128)S(1)} collective-permute-done((f32[24,128]{1,0:T(8,128)S(1)}, f32[24,128]{1,0:T(8,128)S(1)}, u32[]{:S(2)}, u32[]{:S(2)}) %collective-permute-start.2) | collective-permute-done | bytes 12320 | tf_op jit(solution)/shard_map/ppermute | solution.py:371
  40.5 1.0 %last.1 = (f32[3,2,2,2048]{3,2,1,0:T(2,128)}, f32[3,2,2,2048]{3,2,1,0:T(2,128)}) custom-call(f32[24,256]{1,0:T(8,128)S(1)} %collective-permute-done.1.edge, f32[24,256]{1,0:T(8,128)S(1)} %get-tuple-element.55.own, f32[24,128]{1,0:T(8,128)S(1)} %get-tuple-element.62.norms_own, f32[24,128]{1,0:T(8,128)S(1)} %collective-permute-done.2.norms, ...), custom_call_target="tpu_custom_call" | custom-call | tf_op jit(solution)/shard_map/last/pallas_call | solution.py:403
Async XLA Ops:
  2.4 19.0 %copy-start.9 = (bf16[64,192]{1,0:T(8,128)(2,1)S(1)}, bf16[64,192]{1,0:T(8,128)(2,1)}, u32[]{:S(2)}) copy-start(bf16[64,192]{1,0:T(8,128)(2,1)} %constant.5.clone.analysis) | copy-start | bytes 73732
  2.5 19.0 %copy-start.10 = (bf16[64,192]{1,0:T(8,128)(2,1)S(1)}, bf16[64,192]{1,0:T(8,128)(2,1)}, u32[]{:S(2)}) copy-start(bf16[64,192]{1,0:T(8,128)(2,1)} %constant.4.clone.synthesis) | copy-start | bytes 73732
  2.5 19.0 %all-to-all-start = ((f32[8,48,256]{2,1,0:T(8,128)}), f32[8,48,256]{2,1,0:T(8,128)S(1)}, u32[]{:S(2)}, u32[]{:S(2)}) async-start(f32[8,48,256]{2,1,0:T(8,128)} %pack.1), calls=%async_computation | async-start | bytes 786432 | tf_op jit(solution)/shard_map/all_to_all | solution.py:324
  21.4 12.0 %copy-start = (bf16[2048,1024]{1,0:T(8,128)(2,1)S(1)}, bf16[2048,1024]{1,0:T(8,128)(2,1)}, u32[]{:S(2)}) copy-start(bf16[2048,1024]{1,0:T(8,128)(2,1)} %get-tuple-element.43.touch) | copy-start | bytes 12582916
  21.4 12.0 %copy-start.3 = (bf16[1024,128]{1,0:T(8,128)(2,1)S(1)}, bf16[1024,128]{1,0:T(8,128)(2,1)}, u32[]{:S(2)}) copy-start(bf16[1024,128]{1,0:T(8,128)(2,1)} %get-tuple-element.45.edge_back) | copy-start | bytes 786436
  21.4 12.0 %copy-start.6 = (f32[8,1024]{1,0:T(8,128)S(1)}, f32[8,1024]{1,0:T(8,128)}, u32[]{:S(2)}) copy-start(f32[8,1024]{1,0:T(8,128)} %get-tuple-element.47.coefs) | copy-start | bytes 98308
  21.4 12.0 %copy-start.7 = (bf16[2048,128]{1,0:T(8,128)(2,1)S(1)}, bf16[2048,128]{1,0:T(8,128)(2,1)}, u32[]{:S(2)}) copy-start(bf16[2048,128]{1,0:T(8,128)(2,1)} %get-tuple-element.44.at_iface) | copy-start | bytes 1572868
  21.5 12.0 %copy-start.8 = (f32[8,128]{1,0:T(8,128)S(1)}, f32[8,128]{1,0:T(8,128)}, u32[]{:S(2)}) copy-start(f32[8,128]{1,0:T(8,128)} %get-tuple-element.46.edge_diag) | copy-start | bytes 12292
  21.9 12.6 %copy-start.1 = (bf16[1024,2048]{1,0:T(8,128)(2,1)S(1)}, bf16[1024,2048]{1,0:T(8,128)(2,1)}, u32[]{:S(2)}) copy-start(bf16[1024,2048]{1,0:T(8,128)(2,1)} %get-tuple-element.50.back) | copy-start | bytes 12582916
  21.9 12.7 %copy-start.5 = (f32[8,2048]{1,0:T(8,128)S(1)}, f32[8,2048]{1,0:T(8,128)}, u32[]{:S(2)}) copy-start(f32[8,2048]{1,0:T(8,128)} %get-tuple-element.51.diag) | copy-start | bytes 196612
  34.5 1.7 %collective-permute-start = (f32[24,128]{1,0:T(8,128)S(1)}, f32[24,128]{1,0:T(8,128)S(1)}, u32[]{:S(2)}, u32[]{:S(2)}) collective-permute-start(f32[24,128]{1,0:T(8,128)S(1)} %get-tuple-element.48.edge_own), channel_id=1, source_target_pairs={{0,1},{1,0},{2,3},{3,2},{4,5},{5,4},{6,7},{7,6},{8,9},{9,8},{10,11... | collective-permute-start | bytes 36872 | tf_op jit(solution)/shard_map/ppermute | solution.py:371
  34.6 1.6 %copy-start.4 = (bf16[128,1024]{1,0:T(8,128)(2,1)S(1)}, bf16[128,1024]{1,0:T(8,128)(2,1)}, u32[]{:S(2)}) copy-start(bf16[128,1024]{1,0:T(8,128)(2,1)} %get-tuple-element.54.edge_touch) | copy-start | bytes 786436
  34.6 2.5 %copy-start.2 = (bf16[128,2048]{1,0:T(8,128)(2,1)S(1)}, bf16[128,2048]{1,0:T(8,128)(2,1)}, u32[]{:S(2)}) copy-start(bf16[128,2048]{1,0:T(8,128)(2,1)} %get-tuple-element.58.from_iface) | copy-start | bytes 1572868
  36.6 2.2 %collective-permute-start.1 = (f32[24,256]{1,0:T(8,128)S(1)}, f32[24,256]{1,0:T(8,128)S(1)}, u32[]{:S(2)}, u32[]{:S(2)}) collective-permute-start(f32[24,256]{1,0:T(8,128)S(1)} %get-tuple-element.55.own), channel_id=1, source_target_pairs={{0,1},{1,0},{2,3},{3,2},{4,5},{5,4},{6,7},{7,6},{8,9},{9,8},{10,11... | collective-permute-start | bytes 73736 | tf_op jit(solution)/shard_map/ppermute | solution.py:371
  39.2 1.2 %collective-permute-start.2 = (f32[24,128]{1,0:T(8,128)S(1)}, f32[24,128]{1,0:T(8,128)S(1)}, u32[]{:S(2)}, u32[]{:S(2)}) collective-permute-start(f32[24,128]{1,0:T(8,128)S(1)} %get-tuple-element.62.norms_own), channel_id=1, source_target_pairs={{0,1},{1,0},{2,3},{3,2},{4,5},{5,4},{6,7},{7,6},{8,9},{9,8},{10,11... | collective-permute-start | bytes 36872 | tf_op jit(solution)/shard_map/ppermute | solution.py:371

commit v5 on v4

--- a/solution.py
+++ b/solution.py
@@ -13,6 +13,7 @@
 diffusion_ratio = 2.0
 f32 = jnp.float32
 bf16 = jnp.bfloat16
+f8 = jnp.float8_e4m3fn
 small, medium, large = 16 * 2**20, 54 * 2**20, 60 * 2**20
 
 
@@ -126,7 +127,7 @@
             out[j, span, :] = fields[j, span, :] + coef[j * pair : (j + 1) * pair]
 
 
-def mesh_kernel(nodes_hbm, mass_hbm, radial_hbm, stiff_hbm, iface_hbm, touch_out, back_out, at_iface, from_iface, diag, coefs, edge_touch, edge_back, edge_diag, touch, back, elem_nodes, mass, radial, stiff, iface, in_sems, out_sems):
+def mesh_kernel(nodes_hbm, mass_hbm, radial_hbm, stiff_hbm, iface_hbm, touch_out, back_out, at_iface, from_iface, diag, coefs, edge_touch, edge_back, edge_diag, gram, touch, back, elem_nodes, mass, radial, stiff, iface, in_sems, out_sems):
     loads = start_all(
         (nodes_hbm, mass_hbm, radial_hbm, stiff_hbm, iface_hbm), (elem_nodes, mass, radial, stiff, iface), in_sems
     )
@@ -171,6 +172,15 @@
     counts = jnp.dot(from_iface[...], touch[...], preferred_element_type=f32)
     edge_touch[...] = counts.astype(bf16)
     edge_back[...] = counts.T.astype(bf16)
+    short = touch[...].astype(f32).astype(f8)
+    for c in range(elems // width):
+        span = slice(c * width, (c + 1) * width)
+        left = back[span, :].astype(f32).astype(f8)
+        counts = jnp.dot(left, short[:, c * width :], preferred_element_type=f32)
+        gram[span, c * width :] = counts.astype(bf16)
+        for d in range(c + 1, elems // width):
+            block = counts[:, (d - c) * width : (d - c + 1) * width]
+            gram[d * width : (d + 1) * width, span] = block.T.astype(bf16)
     for copy in sent:
         copy.wait()
 
@@ -217,13 +227,16 @@
     edge[...] = edge_diag[0:1, :] * product(given, at_iface, 3) + product(spread, edge_back, 3)
 
 
-def rhs_kernel(per_dev, modes, forcing, spread, touch, back, diag, local, sums, inner):
+def rhs_kernel(per_dev, modes, forcing, spread, touch, back, diag, local, sums, scaled_sums, inner):
     rows = spread.shape[0]
     image = diag[0:1, :] * together(forcing) + product(spread[...], back)
     local[...] = image
-    sums[...] = product(image, touch)
-    square = (2.0 * diag[3:4, :] - 1.0) * image * image
-    inner[...] = lanes(row_sum(square), row_sum(at_nodes(row_factors(rows, per_dev, modes), diag) * square))
+    scaled = at_nodes(row_factors(rows, per_dev, modes), diag) * image
+    both = product(jnp.concatenate([image, scaled], axis=0), touch)
+    sums[...] = both[:rows]
+    scaled_sums[...] = both[rows:]
+    own = 2.0 * diag[3:4, :] - 1.0
+    inner[...] = lanes(row_sum(own * image * image), row_sum(own * image * scaled))
 
 
 def image_edge_kernel(per_dev, modes, edge_own, edge, sums, inner, edge_touch, edge_back, edge_diag, coefs, sums_out, out):
@@ -240,13 +253,14 @@
     out[:, shared:] = lanes(norm, curvature)
 
 
-def image_kernel(per_dev, modes, local, edge, sums, touch, back, from_iface, diag, coefs, rhs_out, image_out, sums_out):
+def image_kernel(per_dev, modes, local, edge, sums, scaled_sums, back, from_iface, edge_touch, edge_diag, gram, diag, coefs, rhs_out, image_out, sums_out):
     factors = row_factors(local.shape[0], per_dev, modes)
     rhs = local[...] + product(edge[...], from_iface, 3)
     rhs_out[...] = rhs
-    image = at_nodes(factors, diag) * rhs + product(at_elems(factors, coefs) * sums[...], back)
-    image_out[...] = image
-    sums_out[...] = product(image, touch)
+    spread = at_elems(factors, coefs) * sums[...]
+    image_out[...] = at_nodes(factors, diag) * rhs + product(spread, back)
+    arrived = product(at_nodes(factors, edge_diag) * edge[...], edge_touch, 3)
+    sums_out[...] = scaled_sums[...] + arrived + product(spread, gram)
 
 
 def resid_kernel(per_dev, modes, own, edge, rhs, image, sums, image_sums, from_iface, edge_touch, diag, coefs, resid_out, norms_out):
@@ -332,12 +346,13 @@
         shape(shared, elems, kind=bf16),
         shape(elems, shared, kind=bf16),
         shape(8, shared),
+        shape(elems, elems, kind=bf16),
     )
     in_vmem = pl.BlockSpec(memory_space=pltpu.VMEM)
     built = pl.pallas_call(
         mesh_kernel,
         in_specs=[in_hbm] * 5,
-        out_specs=(in_hbm, in_hbm, *[in_vmem] * 7),
+        out_specs=(in_hbm, in_hbm, *[in_vmem] * 8),
         out_shape=tables,
         scratch_shapes=[
             pltpu.VMEM((nodes, elems), bf16),
@@ -355,7 +370,7 @@
         cost_estimate=pl.CostEstimate(flops=2**31, bytes_accessed=2**23, transcendentals=0),
     )(elem_nodes, mass, radial, stiff, iface)
     columns, *built = lax.optimization_barrier((columns, *built))
-    touch, back, at_iface, from_iface, diag, coefs, edge_touch, edge_back, edge_diag = built
+    touch, back, at_iface, from_iface, diag, coefs, edge_touch, edge_back, edge_diag, gram = built
     terms = pl.pallas_call(
         nonlinear_kernel,
         out_shape=pltpu.VMEM((owners, rows, block), f32),
@@ -386,7 +401,7 @@
         forcing, touch, at_iface, edge_back, edge_diag, coefs
     )
     edge = swap(edge_own)
-    local, sums, inner = call(rhs_kernel, "rhs", (full, part, small_row), 2**30)(
+    local, sums, scaled_sums, inner = call(rhs_kernel, "rhs", (full, part, part, small_row), 2**30)(
         forcing, spread, touch, back, diag
     )
     sums, image_edge_own = call(image_edge_kernel, "image_edge", (part, shape(rows, shared + 128)))(
@@ -394,7 +409,7 @@
     )
     image_edge = swap(image_edge_own)
     rhs, image, image_sums = call(image_kernel, "image", (full, full, part), 2**30)(
-        local, edge, sums, touch, back, from_iface, diag, coefs
+        local, edge, sums, scaled_sums, back, from_iface, edge_touch, edge_diag, gram, diag, coefs
     )
     resid, norms_own = call(resid_kernel, "resid", (full, small_row))(
         image_edge_own, image_edge, rhs, image, sums, image_sums, from_iface, edge_touch, diag, coefs

time: 41.8 us -> 41.4 us (level)
  waiting for transfers between devices: 6.93 us -> 5.1 us
  Pallas kernels: 14.2 us -> 15.6 us
    pallas_call x1, Pallas kernels: 5.89 us -> 7.72 us  [per_device(): pl.pallas_call(mesh_kernel, in_specs=[in_hbm] * 5, out_specs=(in_hbm, in_...]
    all_to_all x1, waiting for transfers between devices: 5.8 us -> 3.96 us  [per_device(): columns = lax.all_to_all(packed, 'mode', 0, 0, tiled=True)]
  transfers between devices with their start and end apart: 4 -> 4, of which waited for: 2 -> 2; matrix products, arithmetic and copies ran while one was open for 0% -> 0% of each run, Pallas kernels for 22% -> 26%
where the time goes in v5:
time: 41.4 us; the launch traced here: 41.1 us
  Pallas kernels  15.6 us (38%)
  blocking collectives  11.5 us (28%)
  starting transfers between devices  7.98 us (19%)
  waiting for transfers between devices  5.1 us (12%)
  between operations  0.84 us (2%)
    all_to_all x1, blocking collectives, per_device(): forcing = lax.all_to_all(terms, 'mode', 0, 0, tiled=True)  11.5 us
    pallas_call x1, Pallas kernels, per_device(): pl.pallas_call(mesh_kernel, in_specs=[in_hbm] * 5, out_specs=(in_hbm, in_...  7.72 us
    all_to_all x1, starting transfers between devices, per_device(): columns = lax.all_to_all(packed, 'mode', 0, 0, tiled=True)  7.26 us
    all_to_all x1, waiting for transfers between devices, per_device(): columns = lax.all_to_all(packed, 'mode', 0, 0, tiled=True)  3.96 us
    pallas_call x1, Pallas kernels, per_device(): pl.pallas_call(pack_kernel, in_specs=[in_hbm] * 4, out_shape=shape(owners...  1.82 us
    pallas_call x1, Pallas kernels, per_device(): call(rhs_kernel, 'rhs', (full, part, part, small_row), 2 ** 30)  1.55 us
    pallas_call x1, Pallas kernels, per_device(): call(image_kernel, 'image', (full, full, part), 2 ** 30)  1.37 us
    ppermute x3, waiting for transfers between devices, swap(): return lax.ppermute(array, 'mer', [(0, 1), (1, 0)])  1.14 us
  transfers between devices with their start and end apart: 4, of which 2 were waited for; matrix products, arithmetic and copies ran while one was open for 0% of the time, Pallas kernels for 26%

profile of v5, /device:TPU:0, one launch (start us, length us, event | category | flops | bytes accessed | tf_op | source)
XLA Modules:
  0.0 41.1 jit_solution(9267257013347770262)
XLA Ops:
  0.6 1.8 %pack.1 = f32[8,48,256]{2,1,0:T(8,128)} custom-call(f32[3,2,2,2048]{3,2,1,0:T(2,128)} %vel.1, f32[3,2,2,2048]{3,2,1,0:T(2,128)} %mag.1, f32[3,2,2,2048]{3,2,1,0:T(2,128)} %vort.1, f32[3,2,2,2048]{3,2,1,0:T(2,128)} %cur.1), custom_call_target="tpu_custom_call" | custom-call | tf_op jit(solution)/shard_map/pack/pallas_call | solution.py:320
  2.5 0.0 copy-start.10
  2.5 0.0 copy-start.11
  2.5 7.3 %all-to-all-start = ((f32[8,48,256]{2,1,0:T(8,128)}), f32[8,48,256]{2,1,0:T(8,128)S(1)}, u32[]{:S(2)}, u32[]{:S(2)}) async-start(f32[8,48,256]{2,1,0:T(8,128)} %pack.1), calls=%async_computation | async-start | bytes 786432 | tf_op jit(solution)/shard_map/all_to_all | solution.py:338
  9.8 7.7 %incidence.1 = (bf16[2048,1024]{1,0:T(8,128)(2,1)}, bf16[1024,2048]{1,0:T(8,128)(2,1)}, bf16[2048,128]{1,0:T(8,128)(2,1)}, bf16[128,2048]{1,0:T(8,128)(2,1)}, f3...) custom-call(s32[6,1024]{1,0:T(8,128)} %nodes_hbm.1, ...), custom_call_target="tpu_custom_call" | custom-call | flops 2147483648 | bytes 8388608 | tf_op jit(solution)/shard_map/incidence/pallas_call | solution.py:352
  17.5 4.0 %all-to-all-done.fields = f32[8,48,256]{2,1,0:T(8,128)S(1)} async-done(((f32[8,48,256]{2,1,0:T(8,128)}), f32[8,48,256]{2,1,0:T(8,128)S(1)}, u32[]{:S(2)}, u32[]{:S(2)}) %all-to-all-start) | async-done | bytes 393248 | tf_op jit(solution)/shard_map/all_to_all | solution.py:338
  21.4 0.0 copy-done.10
  21.4 0.0 copy-done.11
  21.4 0.0 copy-start
  21.5 0.0 copy-start.5
  21.5 0.0 copy-start.7
  21.5 0.0 copy-start.8
  21.5 0.0 copy-start.9
  21.5 0.4 %nonlinear.1 = f32[8,24,256]{2,1,0:T(8,128)S(1)} custom-call(f32[8,48,256]{2,1,0:T(8,128)S(1)} %all-to-all-done.fields, bf16[64,192]{1,0:T(8,128)(2,1)S(1)} %copy-done.11, bf16[64,192]{1,0:T(8,128)(2,1)S(1)} %copy-done.10), custom_call_target="tpu_custom_call" | custom-call | flops 8589934592 | bytes 16777216 | tf_op jit(solution)/shard_map/nonlinear/pallas_call | solution.py:374
  21.9 0.0 copy-start.1
  21.9 0.0 copy-start.6
  21.9 11.5 %all_to_all.10.forcing = f32[8,24,256]{2,1,0:T(8,128)S(1)} all-to-all(f32[8,24,256]{2,1,0:T(8,128)S(1)} %nonlinear.1), channel_id=1, replica_groups=mesh['runs'=2,'mode'=8,'mer'=2] {'mode'}, dimensions={0} | all-to-all | bytes 393216 | tf_op jit(solution)/shard_map/all_to_all | solution.py:381
  33.4 0.0 copy-done
  33.4 0.0 copy-done.5
  33.4 0.0 copy-done.7
  33.4 0.0 copy-done.8
  33.4 0.0 copy-done.9
  33.4 1.0 %rhs_edge.1 = (f32[24,1024]{1,0:T(8,128)S(1)}, f32[24,128]{1,0:T(8,128)S(1)}) custom-call(f32[8,24,256]{2,1,0:T(8,128)S(1)} %all_to_all.10.forcing, bf16[2048,1024]{1,0:T(8,128)(2,1)S(1)} %copy-done, bf16[2048,128]{1,0:T(8,128)(2,1)S(1)} %copy-done.7, bf16[1024,128]{1,0:T(8,128)(2,1)S(1)} %copy-done.5, f32[8,128]{1,0:T(8,128)S(1)} %copy-done.9, ...), custom_call_target="tpu_custom_call" | custom-call | tf_op jit(solution)/shard_map/rhs_edge/pallas_call | solution.py:400
  34.5 0.1 collective-permute-start
  34.5 0.0 copy-done.1
  34.5 0.0 copy-done.6
  34.6 0.0 copy-start.2
  34.6 0.0 copy-start.3
  34.6 0.0 copy-start.4
  34.6 1.6 %rhs.1 = (f32[24,2048]{1,0:T(8,128)S(1)}, f32[24,1024]{1,0:T(8,128)S(1)}, f32[24,1024]{1,0:T(8,128)S(1)}, f32[24,128]{1,0:T(8,128)S(1)}) custom-call(f32[8,24,256]{2,1,0:T(8,128)S(1)} %all_to_all.10.forcing, f32[24,1024]{1,0:T(8,128)S(1)} %get-tuple-element.53.spread, bf16[2048,1024]{1,0:T(8,128)(2,1)S(1)} %copy-done, bf16[1024,2048]{1,0:T(8,128)(2,1)S(1)} %copy-done.1, ...), custom_call_target="tpu_custom_call" | custom-call | flops 1073741824 | bytes 2097152 | tf_op jit(solution)/shard_map/rhs/pallas_call | solution.py:404
  36.1 0.0 collective-permute-done.edge
  36.2 0.0 copy-done.2
  36.2 0.4 image_edge.1
  36.5 0.5 %collective-permute-start.1 = (f32[24,256]{1,0:T(8,128)S(1)}, f32[24,256]{1,0:T(8,128)S(1)}, u32[]{:S(2)}, u32[]{:S(2)}) collective-permute-start(f32[24,256]{1,0:T(8,128)S(1)} %get-tuple-element.59.own), channel_id=1, source_target_pairs={{0,1},{1,0},{2,3},{3,2},{4,5},{5,4},{6,7},{7,6},{8,9},{9,8},{10,11... | collective-permute-start | bytes 73736 | tf_op jit(solution)/shard_map/ppermute | solution.py:386
  37.1 0.0 copy-done.3
  37.1 0.0 copy-done.4
  37.1 1.4 %image.1 = (f32[24,2048]{1,0:T(8,128)S(1)}, f32[24,2048]{1,0:T(8,128)S(1)}, f32[24,1024]{1,0:T(8,128)S(1)}) custom-call(f32[24,2048]{1,0:T(8,128)S(1)} %get-tuple-element.60.local, f32[24,128]{1,0:T(8,128)S(1)} %collective-permute-done.edge, f32[24,1024]{1,0:T(8,128)S(1)} %get-tuple-element.61.sums, f32[24,1024]{1,0:T(8,128)S(1)} %get-tuple-element.62.scaled_sums, ...), custom_call_target="tpu_custom_call" | custom-call | flops 1073741824 | bytes 2097152 | tf_op jit(solution)/shard_map/image/pallas_call | solution.py:411
  38.4 0.0 collective-permute-done.1.edge
  38.5 0.4 resid.1
  38.9 0.1 collective-permute-start.2
  39.0 1.1 %collective-permute-done.2.norms = f32[24,128]{1,0:T(8,128)S(1)} collective-permute-done((f32[24,128]{1,0:T(8,128)S(1)}, f32[24,128]{1,0:T(8,128)S(1)}, u32[]{:S(2)}, u32[]{:S(2)}) %collective-permute-start.2) | collective-permute-done | bytes 12320 | tf_op jit(solution)/shard_map/ppermute | solution.py:386
  40.1 1.0 %last.1 = (f32[3,2,2,2048]{3,2,1,0:T(2,128)}, f32[3,2,2,2048]{3,2,1,0:T(2,128)}) custom-call(f32[24,256]{1,0:T(8,128)S(1)} %collective-permute-done.1.edge, f32[24,256]{1,0:T(8,128)S(1)} %get-tuple-element.59.own, f32[24,128]{1,0:T(8,128)S(1)} %get-tuple-element.68.norms_own, f32[24,128]{1,0:T(8,128)S(1)} %collective-permute-done.2.norms, ...), custom_call_target="tpu_custom_call" | custom-call | tf_op jit(solution)/shard_map/last/pallas_call | solution.py:418
Async XLA Ops:
  2.5 19.0 %copy-start.10 = (bf16[64,192]{1,0:T(8,128)(2,1)S(1)}, bf16[64,192]{1,0:T(8,128)(2,1)}, u32[]{:S(2)}) copy-start(bf16[64,192]{1,0:T(8,128)(2,1)} %constant.5.clone.analysis) | copy-start | bytes 73732
  2.5 19.0 %copy-start.11 = (bf16[64,192]{1,0:T(8,128)(2,1)S(1)}, bf16[64,192]{1,0:T(8,128)(2,1)}, u32[]{:S(2)}) copy-start(bf16[64,192]{1,0:T(8,128)(2,1)} %constant.4.clone.synthesis) | copy-start | bytes 73732
  2.5 19.0 %all-to-all-start = ((f32[8,48,256]{2,1,0:T(8,128)}), f32[8,48,256]{2,1,0:T(8,128)S(1)}, u32[]{:S(2)}, u32[]{:S(2)}) async-start(f32[8,48,256]{2,1,0:T(8,128)} %pack.1), calls=%async_computation | async-start | bytes 786432 | tf_op jit(solution)/shard_map/all_to_all | solution.py:338
  21.4 12.0 %copy-start = (bf16[2048,1024]{1,0:T(8,128)(2,1)S(1)}, bf16[2048,1024]{1,0:T(8,128)(2,1)}, u32[]{:S(2)}) copy-start(bf16[2048,1024]{1,0:T(8,128)(2,1)} %get-tuple-element.47.touch) | copy-start | bytes 12582916
  21.5 12.0 %copy-start.5 = (bf16[1024,128]{1,0:T(8,128)(2,1)S(1)}, bf16[1024,128]{1,0:T(8,128)(2,1)}, u32[]{:S(2)}) copy-start(bf16[1024,128]{1,0:T(8,128)(2,1)} %get-tuple-element.49.edge_back) | copy-start | bytes 786436
  21.5 12.0 %copy-start.7 = (bf16[2048,128]{1,0:T(8,128)(2,1)S(1)}, bf16[2048,128]{1,0:T(8,128)(2,1)}, u32[]{:S(2)}) copy-start(bf16[2048,128]{1,0:T(8,128)(2,1)} %get-tuple-element.48.at_iface) | copy-start | bytes 1572868
  21.5 12.0 %copy-start.8 = (f32[8,1024]{1,0:T(8,128)S(1)}, f32[8,1024]{1,0:T(8,128)}, u32[]{:S(2)}) copy-start(f32[8,1024]{1,0:T(8,128)} %get-tuple-element.51.coefs) | copy-start | bytes 98308
  21.5 12.0 %copy-start.9 = (f32[8,128]{1,0:T(8,128)S(1)}, f32[8,128]{1,0:T(8,128)}, u32[]{:S(2)}) copy-start(f32[8,128]{1,0:T(8,128)} %get-tuple-element.50.edge_diag) | copy-start | bytes 12292
  21.9 12.6 %copy-start.1 = (bf16[1024,2048]{1,0:T(8,128)(2,1)S(1)}, bf16[1024,2048]{1,0:T(8,128)(2,1)}, u32[]{:S(2)}) copy-start(bf16[1024,2048]{1,0:T(8,128)(2,1)} %get-tuple-element.54.back) | copy-start | bytes 12582916
  21.9 12.6 %copy-start.6 = (f32[8,2048]{1,0:T(8,128)S(1)}, f32[8,2048]{1,0:T(8,128)}, u32[]{:S(2)}) copy-start(f32[8,2048]{1,0:T(8,128)} %get-tuple-element.55.diag) | copy-start | bytes 196612
  34.5 1.7 %collective-permute-start = (f32[24,128]{1,0:T(8,128)S(1)}, f32[24,128]{1,0:T(8,128)S(1)}, u32[]{:S(2)}, u32[]{:S(2)}) collective-permute-start(f32[24,128]{1,0:T(8,128)S(1)} %get-tuple-element.52.edge_own), channel_id=1, source_target_pairs={{0,1},{1,0},{2,3},{3,2},{4,5},{5,4},{6,7},{7,6},{8,9},{9,8},{10,11... | collective-permute-start | bytes 36872 | tf_op jit(solution)/shard_map/ppermute | solution.py:386
  34.6 1.6 %copy-start.2 = (bf16[128,1024]{1,0:T(8,128)(2,1)S(1)}, bf16[128,1024]{1,0:T(8,128)(2,1)}, u32[]{:S(2)}) copy-start(bf16[128,1024]{1,0:T(8,128)(2,1)} %get-tuple-element.58.edge_touch) | copy-start | bytes 786436
  34.6 2.5 %copy-start.3 = (bf16[1024,1024]{1,0:T(8,128)(2,1)S(1)}, bf16[1024,1024]{1,0:T(8,128)(2,1)}, u32[]{:S(2)}) copy-start(bf16[1024,1024]{1,0:T(8,128)(2,1)} %get-tuple-element.64.gram) | copy-start | bytes 6291460
  34.6 2.5 %copy-start.4 = (bf16[128,2048]{1,0:T(8,128)(2,1)S(1)}, bf16[128,2048]{1,0:T(8,128)(2,1)}, u32[]{:S(2)}) copy-start(bf16[128,2048]{1,0:T(8,128)(2,1)} %get-tuple-element.63.from_iface) | copy-start | bytes 1572868
  36.5 1.9 %collective-permute-start.1 = (f32[24,256]{1,0:T(8,128)S(1)}, f32[24,256]{1,0:T(8,128)S(1)}, u32[]{:S(2)}, u32[]{:S(2)}) collective-permute-start(f32[24,256]{1,0:T(8,128)S(1)} %get-tuple-element.59.own), channel_id=1, source_target_pairs={{0,1},{1,0},{2,3},{3,2},{4,5},{5,4},{6,7},{7,6},{8,9},{9,8},{10,11... | collective-permute-start | bytes 73736 | tf_op jit(solution)/shard_map/ppermute | solution.py:386
  38.9 1.2 %collective-permute-start.2 = (f32[24,128]{1,0:T(8,128)S(1)}, f32[24,128]{1,0:T(8,128)S(1)}, u32[]{:S(2)}, u32[]{:S(2)}) collective-permute-start(f32[24,128]{1,0:T(8,128)S(1)} %get-tuple-element.68.norms_own), channel_id=1, source_target_pairs={{0,1},{1,0},{2,3},{3,2},{4,5},{5,4},{6,7},{7,6},{8,9},{9,8},{10,11... | collective-permute-start | bytes 36872 | tf_op jit(solution)/shard_map/ppermute | solution.py:386

commit v6 on v4

--- a/solution.py
+++ b/solution.py
@@ -13,6 +13,7 @@
 diffusion_ratio = 2.0
 f32 = jnp.float32
 bf16 = jnp.bfloat16
+f8 = jnp.float8_e4m3fn
 small, medium, large = 16 * 2**20, 54 * 2**20, 60 * 2**20
 
 
@@ -44,23 +45,20 @@
     return out
 
 
-def pieces(array, count):
+def product(array, exact, count=5):
+    rows = array.shape[0]
+    top = jnp.maximum(jnp.max(jnp.abs(array), axis=1, keepdims=True), 1e-30)
     parts = []
-    rest = array
-    for i in range(count):
-        part = rest.astype(bf16).astype(f32)
+    rest = array * (200.0 / top)
+    for _ in range(count):
+        part = rest.astype(f8).astype(f32)
         parts.append(part)
-        rest = rest - part
-    return jnp.concatenate(parts, axis=0).astype(bf16)
-
-
-def product(array, exact, count=2):
-    rows = array.shape[0]
-    out = jnp.dot(pieces(array, count), exact[...], preferred_element_type=f32)
-    total = out[:rows]
-    for i in range(1, count):
-        total = total + out[i * rows : (i + 1) * rows]
-    return total
+        rest = (rest - part) * 16.0
+    out = jnp.dot(jnp.concatenate(parts, axis=0).astype(f8), exact[...], preferred_element_type=f32)
+    total = out[(count - 1) * rows :]
+    for i in reversed(range(count - 1)):
+        total = total * (1.0 / 16.0) + out[i * rows : (i + 1) * rows]
+    return total * (top / 200.0)
 
 
 def table_product(table, values):
@@ -148,29 +146,29 @@
             value = jnp.left_shift(1, field * 4)
             total = total + jnp.where(ids - field * words == word, value, 0)
         for q in range(fields):
-            count = jnp.right_shift(total, 4 * q) & 15
-            touch[q * words : (q + 1) * words, span] = count.astype(f32).astype(bf16)
+            count = (jnp.right_shift(total, 4 * q) & 15).astype(f32)
+            touch[q * words : (q + 1) * words, span] = count.astype(f8)
+            back[span, q * words : (q + 1) * words] = count.T.astype(f8)
         column = pl.ds(c * width, width)
         sent.append(pltpu.make_async_copy(touch.at[:, column], touch_out.at[:, column], out_sems.at[c]))
         sent[-1].start()
-        back[span, :] = touch[:, span].T
         sent.append(pltpu.make_async_copy(back.at[column, :], back_out.at[column, :], out_sems.at[elems // width + c]))
         sent[-1].start()
     node = lax.broadcasted_iota(jnp.int32, (nodes, shared), 0)
     hit = jnp.where(iface[...] == node, 1.0, 0.0)
-    at_iface[...] = hit.astype(bf16)
-    from_iface[...] = hit.T.astype(bf16)
+    at_iface[...] = hit.astype(f8)
+    from_iface[...] = hit.T.astype(f8)
     zero = jnp.zeros((5, elems), f32)
     coefs[...] = jnp.concatenate([mass[...] / 12.0, radial[...] / 12.0, stiff[...], zero], axis=0)
     scaled = jnp.concatenate([mass[...] / 12.0, radial[...] / 12.0, 6.0 * stiff[...], zero], axis=0)
-    sums = product(scaled, back, 3)
-    hits = jnp.dot(jnp.ones((16, shared), bf16), from_iface[...], preferred_element_type=f32)
+    sums = product(scaled, back)
+    hits = jnp.dot(jnp.ones((32, shared), f8), from_iface[...], preferred_element_type=f32)
     row = lax.broadcasted_iota(jnp.int32, (8, nodes), 0)
     diag[...] = jnp.where(row == 3, 1.0 - 0.5 * hits[:8], sums)
-    edge_diag[...] = product(sums, at_iface, 3)
+    edge_diag[...] = product(sums, at_iface)
     counts = jnp.dot(from_iface[...], touch[...], preferred_element_type=f32)
-    edge_touch[...] = counts.astype(bf16)
-    edge_back[...] = counts.T.astype(bf16)
+    edge_touch[...] = counts.astype(f8)
+    edge_back[...] = counts.T.astype(f8)
     for copy in sent:
         copy.wait()
 
@@ -214,7 +212,7 @@
     given = together(forcing)
     spread = product(given, touch) * coefs[0:1, :]
     spread_out[...] = spread
-    edge[...] = edge_diag[0:1, :] * product(given, at_iface, 3) + product(spread, edge_back, 3)
+    edge[...] = edge_diag[0:1, :] * product(given, at_iface) + product(spread, edge_back)
 
 
 def rhs_kernel(per_dev, modes, forcing, spread, touch, back, diag, local, sums, inner):
@@ -230,19 +228,19 @@
     rows, shared = edge.shape
     factors = row_factors(rows, per_dev, modes)
     rhs = edge_own[...] + edge[...]
-    full = sums[...] + product(edge[...], edge_touch, 3)
+    full = sums[...] + product(edge[...], edge_touch)
     sums_out[...] = full
     spread = at_elems(factors, coefs) * full
     image = at_nodes(factors, edge_diag) * rhs
     norm = inner[:, 0:1] + 0.5 * row_sum(rhs * rhs)
     curvature = inner[:, 1:2] + row_sum(image * rhs) + row_sum(spread * full)
-    out[:, :shared] = image + product(spread, edge_back, 3)
+    out[:, :shared] = image + product(spread, edge_back)
     out[:, shared:] = lanes(norm, curvature)
 
 
 def image_kernel(per_dev, modes, local, edge, sums, touch, back, from_iface, diag, coefs, rhs_out, image_out, sums_out):
     factors = row_factors(local.shape[0], per_dev, modes)
-    rhs = local[...] + product(edge[...], from_iface, 3)
+    rhs = local[...] + product(edge[...], from_iface)
     rhs_out[...] = rhs
     image = at_nodes(factors, diag) * rhs + product(at_elems(factors, coefs) * sums[...], back)
     image_out[...] = image
@@ -258,9 +256,9 @@
     curvature = own[:, shared + 1 : shared + 2] + edge[:, shared + 1 : shared + 2]
     alpha = norm / curvature
     given = edge[:, :shared]
-    resid = rhs[...] - alpha * (image[...] + product(given, from_iface, 3))
+    resid = rhs[...] - alpha * (image[...] + product(given, from_iface))
     resid_out[...] = resid
-    new = sums[...] - alpha * (image_sums[...] + product(given, edge_touch, 3))
+    new = sums[...] - alpha * (image_sums[...] + product(given, edge_touch))
     after = row_sum(diag[3:4, :] * resid * resid)
     square = row_sum(per_node * resid * resid) + row_sum(per_elem * new * new)
     mixed = row_sum(per_node * resid * rhs[...]) + row_sum(per_elem * new * sums[...])
@@ -323,14 +321,14 @@
         ).transpose(1, 0, 2)
     columns = lax.all_to_all(packed, "mode", 0, 0, tiled=True)
     tables = (
-        shape(nodes, elems, kind=bf16),
-        shape(elems, nodes, kind=bf16),
-        shape(nodes, shared, kind=bf16),
-        shape(shared, nodes, kind=bf16),
+        shape(nodes, elems, kind=f8),
+        shape(elems, nodes, kind=f8),
+        shape(nodes, shared, kind=f8),
+        shape(shared, nodes, kind=f8),
         shape(8, nodes),
         shape(8, elems),
-        shape(shared, elems, kind=bf16),
-        shape(elems, shared, kind=bf16),
+        shape(shared, elems, kind=f8),
+        shape(elems, shared, kind=f8),
         shape(8, shared),
     )
     in_vmem = pl.BlockSpec(memory_space=pltpu.VMEM)
@@ -340,8 +338,8 @@
         out_specs=(in_hbm, in_hbm, *[in_vmem] * 7),
         out_shape=tables,
         scratch_shapes=[
-            pltpu.VMEM((nodes, elems), bf16),
-            pltpu.VMEM((elems, nodes), bf16),
+            pltpu.VMEM((nodes, elems), f8),
+            pltpu.VMEM((elems, nodes), f8),
             pltpu.VMEM(elem_nodes.shape, jnp.int32),
             pltpu.VMEM((1, elems), f32),
             pltpu.VMEM((1, elems), f32),

time: 41.8 us -> 40.9 us (0.978)
  Pallas kernels: 14.2 us -> 12.9 us
    pallas_call x1, Pallas kernels: 1.7 us -> 1.14 us  [per_device(): call(image_kernel, 'image', (full, full, part), 2 ** 30)]
    pallas_call x1, Pallas kernels: 1.61 us -> 1.05 us  [per_device(): call(rhs_kernel, 'rhs', (full, part, small_row), 2 ** 30)]
  transfers between devices with their start and end apart: 4 -> 4, of which waited for: 2 -> 3; matrix products, arithmetic and copies ran while one was open for 0% -> 0% of each run, Pallas kernels for 22% -> 19%
where the time goes in v6:
time: 40.9 us; the launch traced here: 40.5 us
  Pallas kernels  12.9 us (32%)
  blocking collectives  11.5 us (28%)
  starting transfers between devices  7.97 us (19%)
  waiting for transfers between devices  7.33 us (18%)
  between operations  0.8 us (2%)
    all_to_all x1, blocking collectives, per_device(): forcing = lax.all_to_all(terms, 'mode', 0, 0, tiled=True)  11.5 us
    all_to_all x1, starting transfers between devices, per_device(): columns = lax.all_to_all(packed, 'mode', 0, 0, tiled=True)  7.26 us
    all_to_all x1, waiting for transfers between devices, per_device(): columns = lax.all_to_all(packed, 'mode', 0, 0, tiled=True)  6.17 us
    pallas_call x1, Pallas kernels, per_device(): pl.pallas_call(mesh_kernel, in_specs=[in_hbm] * 5, out_specs=(in_hbm, in_...  5.49 us
    pallas_call x1, Pallas kernels, per_device(): pl.pallas_call(pack_kernel, in_specs=[in_hbm] * 4, out_shape=shape(owners...  1.83 us
    ppermute x3, waiting for transfers between devices, swap(): return lax.ppermute(array, 'mer', [(0, 1), (1, 0)])  1.16 us
    pallas_call x1, Pallas kernels, per_device(): call(image_kernel, 'image', (full, full, part), 2 ** 30)  1.14 us
    pallas_call x1, Pallas kernels, per_device(): call(rhs_kernel, 'rhs', (full, part, small_row), 2 ** 30)  1.05 us
  transfers between devices with their start and end apart: 4, of which 3 were waited for; matrix products, arithmetic and copies ran while one was open for 0% of the time, Pallas kernels for 19%

profile of v6, /device:TPU:0, one launch (start us, length us, event | category | flops | bytes accessed | tf_op | source)
XLA Modules:
  0.0 40.5 jit_solution(1272414956389282484)
XLA Ops:
  0.6 1.8 %pack.1 = f32[8,48,256]{2,1,0:T(8,128)} custom-call(f32[3,2,2,2048]{3,2,1,0:T(2,128)} %vel.1, f32[3,2,2,2048]{3,2,1,0:T(2,128)} %mag.1, f32[3,2,2,2048]{3,2,1,0:T(2,128)} %vort.1, f32[3,2,2,2048]{3,2,1,0:T(2,128)} %cur.1), custom_call_target="tpu_custom_call" | custom-call | tf_op jit(solution)/shard_map/pack/pallas_call | solution.py:304
  2.5 7.3 %all-to-all-start = ((f32[8,48,256]{2,1,0:T(8,128)}), f32[8,48,256]{2,1,0:T(8,128)S(1)}, u32[]{:S(2)}, u32[]{:S(2)}) async-start(f32[8,48,256]{2,1,0:T(8,128)} %pack.1), calls=%async_computation | async-start | bytes 786432 | tf_op jit(solution)/shard_map/all_to_all | solution.py:322
  9.7 0.0 copy-start.9
  9.7 0.0 copy-start.10
  9.8 5.5 %incidence.1 = (f8e4m3fn[2048,1024]{1,0:T(32,128)(4,1)}, f8e4m3fn[1024,2048]{1,0:T(32,128)(4,1)}, f8e4m3fn[2048,128]{1,0:T(32,128)(4,1)}, f8e4m3fn[128,2048]{1,0...) custom-call(s32[6,1024]{1,0:T(8,128)} %nodes_hbm.1, ...), custom_call_target="tpu_custom_call" | custom-call | flops 2147483648 | bytes 8388608 | tf_op jit(solution)/shard_map/incidence/pallas_call | solution.py:335
  15.3 6.2 %all-to-all-done.fields = f32[8,48,256]{2,1,0:T(8,128)S(1)} async-done(((f32[8,48,256]{2,1,0:T(8,128)}), f32[8,48,256]{2,1,0:T(8,128)S(1)}, u32[]{:S(2)}, u32[]{:S(2)}) %all-to-all-start) | async-done | bytes 393248 | tf_op jit(solution)/shard_map/all_to_all | solution.py:322
  21.4 0.0 copy-done.9
  21.4 0.0 copy-done.10
  21.4 0.0 copy-start
  21.4 0.0 copy-start.4
  21.4 0.0 copy-start.6
  21.5 0.0 copy-start.7
  21.5 0.0 copy-start.8
  21.5 0.4 %nonlinear.1 = f32[8,24,256]{2,1,0:T(8,128)S(1)} custom-call(f32[8,48,256]{2,1,0:T(8,128)S(1)} %all-to-all-done.fields, bf16[64,192]{1,0:T(8,128)(2,1)S(1)} %copy-done.10, bf16[64,192]{1,0:T(8,128)(2,1)S(1)} %copy-done.9), custom_call_target="tpu_custom_call" | custom-call | flops 8589934592 | bytes 16777216 | tf_op jit(solution)/shard_map/nonlinear/pallas_call | solution.py:357
  21.9 0.0 copy-start.1
  21.9 0.0 copy-start.3
  21.9 11.5 %all_to_all.10.forcing = f32[8,24,256]{2,1,0:T(8,128)S(1)} all-to-all(f32[8,24,256]{2,1,0:T(8,128)S(1)} %nonlinear.1), channel_id=1, replica_groups=mesh['runs'=2,'mode'=8,'mer'=2] {'mode'}, dimensions={0} | all-to-all | bytes 393216 | tf_op jit(solution)/shard_map/all_to_all | solution.py:364
  33.4 0.0 copy-done
  33.4 0.0 copy-done.4
  33.4 0.0 copy-done.6
  33.4 0.0 copy-done.7
  33.4 0.0 copy-done.8
  33.4 0.8 %rhs_edge.1 = (f32[24,1024]{1,0:T(8,128)S(1)}, f32[24,128]{1,0:T(8,128)S(1)}) custom-call(f32[8,24,256]{2,1,0:T(8,128)S(1)} %all_to_all.10.forcing, f8e4m3fn[2048,1024]{1,0:T(32,128)(4,1)S(1)} %copy-done, f8e4m3fn[2048,128]{1,0:T(32,128)(4,1)S(1)} %copy-done.7, f8e4m3fn[1024,128]{1,0:T(32,128)(4,1)S(1)} %copy-done.6, f32[8,128]{1,0:T(8,128)S(1)} %copy-done.8, ...), custom_call_target="tpu_custom_call" | custom-call | tf_op jit(solution)/shard_map/rhs_edge/pallas_call | solution.py:383
  34.3 0.1 collective-permute-start
  34.3 0.0 copy-done.1
  34.3 0.0 copy-done.3
  34.4 0.0 copy-start.5
  34.4 0.0 copy-start.2
  34.4 1.1 %rhs.1 = (f32[24,2048]{1,0:T(8,128)S(1)}, f32[24,1024]{1,0:T(8,128)S(1)}, f32[24,128]{1,0:T(8,128)S(1)}) custom-call(f32[8,24,256]{2,1,0:T(8,128)S(1)} %all_to_all.10.forcing, f32[24,1024]{1,0:T(8,128)S(1)} %get-tuple-element.49.spread, f8e4m3fn[2048,1024]{1,0:T(32,128)(4,1)S(1)} %copy-done, f8e4m3fn[1024,2048]{1,0:T(32,128)(4,1)S(1)} %copy-done.1, ...), custom_call_target="tpu_custom_call" | custom-call | flops 1073741824 | bytes 2097152 | tf_op jit(solution)/shard_map/rhs/pallas_call | solution.py:387
  35.4 0.1 collective-permute-done.edge
  35.5 0.0 copy-done.5
  35.5 0.6 %image_edge.1 = (f32[24,1024]{1,0:T(8,128)S(1)}, f32[24,256]{1,0:T(8,128)S(1)}) custom-call(f32[24,128]{1,0:T(8,128)S(1)} %get-tuple-element.48.edge_own, f32[24,128]{1,0:T(8,128)S(1)} %collective-permute-done.edge, f32[24,1024]{1,0:T(8,128)S(1)} %get-tuple-element.52.sums, f32[24,128]{1,0:T(8,128)S(1)} %get-tuple-element.53.inner, ...), custom_call_target="tpu_custom_call" | custom-call | tf_op jit(solution)/shard_map/image_edge/pallas_call | solution.py:390
  36.1 0.5 %collective-permute-start.1 = (f32[24,256]{1,0:T(8,128)S(1)}, f32[24,256]{1,0:T(8,128)S(1)}, u32[]{:S(2)}, u32[]{:S(2)}) collective-permute-start(f32[24,256]{1,0:T(8,128)S(1)} %get-tuple-element.55.own), channel_id=1, source_target_pairs={{0,1},{1,0},{2,3},{3,2},{4,5},{5,4},{6,7},{7,6},{8,9},{9,8},{10,11... | collective-permute-start | bytes 73736 | tf_op jit(solution)/shard_map/ppermute | solution.py:369
  36.6 0.0 copy-done.2
  36.6 1.1 %image.1 = (f32[24,2048]{1,0:T(8,128)S(1)}, f32[24,2048]{1,0:T(8,128)S(1)}, f32[24,1024]{1,0:T(8,128)S(1)}) custom-call(f32[24,2048]{1,0:T(8,128)S(1)} %get-tuple-element.56.local, f32[24,128]{1,0:T(8,128)S(1)} %collective-permute-done.edge, f32[24,1024]{1,0:T(8,128)S(1)} %get-tuple-element.57.sums, f8e4m3fn[2048,1024]{1,0:T(32,128)(4,1)S(1)} %copy-done, ...), custom_call_target="tpu_custom_call" | custom-call | flops 1073741824 | bytes 2097152 | tf_op jit(solution)/shard_map/image/pallas_call | solution.py:394
  37.7 0.0 collective-permute-done.1.edge
  37.7 0.6 %resid.1 = (f32[24,2048]{1,0:T(8,128)S(1)}, f32[24,128]{1,0:T(8,128)S(1)}) custom-call(f32[24,256]{1,0:T(8,128)S(1)} %get-tuple-element.55.own, f32[24,256]{1,0:T(8,128)S(1)} %collective-permute-done.1.edge, f32[24,2048]{1,0:T(8,128)S(1)} %get-tuple-element.59.rhs, f32[24,2048]{1,0:T(8,128)S(1)} %get-tuple-element.60.image, ...), custom_call_target="tpu_custom_call" | custom-call | tf_op jit(solution)/shard_map/resid/pallas_call | solution.py:397
  38.3 0.1 collective-permute-start.2
  38.4 1.1 %collective-permute-done.2.norms = f32[24,128]{1,0:T(8,128)S(1)} collective-permute-done((f32[24,128]{1,0:T(8,128)S(1)}, f32[24,128]{1,0:T(8,128)S(1)}, u32[]{:S(2)}, u32[]{:S(2)}) %collective-permute-start.2) | collective-permute-done | bytes 12320 | tf_op jit(solution)/shard_map/ppermute | solution.py:369
  39.5 1.0 %last.1 = (f32[3,2,2,2048]{3,2,1,0:T(2,128)}, f32[3,2,2,2048]{3,2,1,0:T(2,128)}) custom-call(f32[24,256]{1,0:T(8,128)S(1)} %collective-permute-done.1.edge, f32[24,256]{1,0:T(8,128)S(1)} %get-tuple-element.55.own, f32[24,128]{1,0:T(8,128)S(1)} %get-tuple-element.62.norms_own, f32[24,128]{1,0:T(8,128)S(1)} %collective-permute-done.2.norms, ...), custom_call_target="tpu_custom_call" | custom-call | tf_op jit(solution)/shard_map/last/pallas_call | solution.py:401
Async XLA Ops:
  2.5 19.0 %all-to-all-start = ((f32[8,48,256]{2,1,0:T(8,128)}), f32[8,48,256]{2,1,0:T(8,128)S(1)}, u32[]{:S(2)}, u32[]{:S(2)}) async-start(f32[8,48,256]{2,1,0:T(8,128)} %pack.1), calls=%async_computation | async-start | bytes 786432 | tf_op jit(solution)/shard_map/all_to_all | solution.py:322
  9.7 11.7 %copy-start.9 = (bf16[64,192]{1,0:T(8,128)(2,1)S(1)}, bf16[64,192]{1,0:T(8,128)(2,1)}, u32[]{:S(2)}) copy-start(bf16[64,192]{1,0:T(8,128)(2,1)} %constant.5.clone.analysis) | copy-start | bytes 73732
  9.7 11.7 %copy-start.10 = (bf16[64,192]{1,0:T(8,128)(2,1)S(1)}, bf16[64,192]{1,0:T(8,128)(2,1)}, u32[]{:S(2)}) copy-start(bf16[64,192]{1,0:T(8,128)(2,1)} %constant.4.clone.synthesis) | copy-start | bytes 73732
  21.4 12.0 %copy-start = (f8e4m3fn[2048,1024]{1,0:T(32,128)(4,1)S(1)}, f8e4m3fn[2048,1024]{1,0:T(32,128)(4,1)}, u32[]{:S(2)}) copy-start(f8e4m3fn[2048,1024]{1,0:T(32,128)(4,1)} %get-tuple-element.43.touch) | copy-start | bytes 6291460
  21.4 12.0 %copy-start.4 = (f32[8,1024]{1,0:T(8,128)S(1)}, f32[8,1024]{1,0:T(8,128)}, u32[]{:S(2)}) copy-start(f32[8,1024]{1,0:T(8,128)} %get-tuple-element.47.coefs) | copy-start | bytes 98308
  21.4 12.0 %copy-start.6 = (f8e4m3fn[1024,128]{1,0:T(32,128)(4,1)S(1)}, f8e4m3fn[1024,128]{1,0:T(32,128)(4,1)}, u32[]{:S(2)}) copy-start(f8e4m3fn[1024,128]{1,0:T(32,128)(4,1)} %get-tuple-element.45.edge_back) | copy-start | bytes 393220
  21.5 12.0 %copy-start.7 = (f8e4m3fn[2048,128]{1,0:T(32,128)(4,1)S(1)}, f8e4m3fn[2048,128]{1,0:T(32,128)(4,1)}, u32[]{:S(2)}) copy-start(f8e4m3fn[2048,128]{1,0:T(32,128)(4,1)} %get-tuple-element.44.at_iface) | copy-start | bytes 786436
  21.5 12.0 %copy-start.8 = (f32[8,128]{1,0:T(8,128)S(1)}, f32[8,128]{1,0:T(8,128)}, u32[]{:S(2)}) copy-start(f32[8,128]{1,0:T(8,128)} %get-tuple-element.46.edge_diag) | copy-start | bytes 12292
  21.9 12.4 %copy-start.1 = (f8e4m3fn[1024,2048]{1,0:T(32,128)(4,1)S(1)}, f8e4m3fn[1024,2048]{1,0:T(32,128)(4,1)}, u32[]{:S(2)}) copy-start(f8e4m3fn[1024,2048]{1,0:T(32,128)(4,1)} %get-tuple-element.50.back) | copy-start | bytes 6291460
  21.9 12.4 %copy-start.3 = (f32[8,2048]{1,0:T(8,128)S(1)}, f32[8,2048]{1,0:T(8,128)}, u32[]{:S(2)}) copy-start(f32[8,2048]{1,0:T(8,128)} %get-tuple-element.51.diag) | copy-start | bytes 196612
  34.3 1.2 %collective-permute-start = (f32[24,128]{1,0:T(8,128)S(1)}, f32[24,128]{1,0:T(8,128)S(1)}, u32[]{:S(2)}, u32[]{:S(2)}) collective-permute-start(f32[24,128]{1,0:T(8,128)S(1)} %get-tuple-element.48.edge_own), channel_id=1, source_target_pairs={{0,1},{1,0},{2,3},{3,2},{4,5},{5,4},{6,7},{7,6},{8,9},{9,8},{10,11... | collective-permute-start | bytes 36872 | tf_op jit(solution)/shard_map/ppermute | solution.py:369
  34.4 1.1 %copy-start.5 = (f8e4m3fn[128,1024]{1,0:T(32,128)(4,1)S(1)}, f8e4m3fn[128,1024]{1,0:T(32,128)(4,1)}, u32[]{:S(2)}) copy-start(f8e4m3fn[128,1024]{1,0:T(32,128)(4,1)} %get-tuple-element.54.edge_touch) | copy-start | bytes 393220
  34.4 2.2 %copy-start.2 = (f8e4m3fn[128,2048]{1,0:T(32,128)(4,1)S(1)}, f8e4m3fn[128,2048]{1,0:T(32,128)(4,1)}, u32[]{:S(2)}) copy-start(f8e4m3fn[128,2048]{1,0:T(32,128)(4,1)} %get-tuple-element.58.from_iface) | copy-start | bytes 786436
  36.1 1.6 %collective-permute-start.1 = (f32[24,256]{1,0:T(8,128)S(1)}, f32[24,256]{1,0:T(8,128)S(1)}, u32[]{:S(2)}, u32[]{:S(2)}) collective-permute-start(f32[24,256]{1,0:T(8,128)S(1)} %get-tuple-element.55.own), channel_id=1, source_target_pairs={{0,1},{1,0},{2,3},{3,2},{4,5},{5,4},{6,7},{7,6},{8,9},{9,8},{10,11... | collective-permute-start | bytes 73736 | tf_op jit(solution)/shard_map/ppermute | solution.py:369
  38.3 1.2 %collective-permute-start.2 = (f32[24,128]{1,0:T(8,128)S(1)}, f32[24,128]{1,0:T(8,128)S(1)}, u32[]{:S(2)}, u32[]{:S(2)}) collective-permute-start(f32[24,128]{1,0:T(8,128)S(1)} %get-tuple-element.62.norms_own), channel_id=1, source_target_pairs={{0,1},{1,0},{2,3},{3,2},{4,5},{5,4},{6,7},{7,6},{8,9},{9,8},{10,11... | collective-permute-start | bytes 36872 | tf_op jit(solution)/shard_map/ppermute | solution.py:369

commit v7 on v4

--- a/solution.py
+++ b/solution.py
@@ -13,6 +13,8 @@
 diffusion_ratio = 2.0
 f32 = jnp.float32
 bf16 = jnp.bfloat16
+f8 = jnp.float8_e4m3fn
+largest, radix, exact_below = 16.0, 32.0, 2048.0
 small, medium, large = 16 * 2**20, 54 * 2**20, 60 * 2**20
 
 
@@ -61,6 +63,34 @@
     for i in range(1, count):
         total = total + out[i * rows : (i + 1) * rows]
     return total
+
+
+def short_product(array, exact, count=4):
+    rows = array.shape[0]
+    top = jnp.maximum(jnp.max(jnp.abs(array), axis=1, keepdims=True), 1e-30)
+    parts = []
+    rest = array * (largest / top)
+    for _ in range(count):
+        part = jnp.round(rest)
+        parts.append(part)
+        rest = (rest - part) * radix
+    out = jnp.dot(jnp.concatenate(parts, axis=0).astype(f8), exact[...], preferred_element_type=f32)
+    total = out[(count - 1) * rows :]
+    for i in reversed(range(count - 1)):
+        total = total * (1.0 / radix) + out[i * rows : (i + 1) * rows]
+    return total * (top / largest)
+
+
+def spread_into(target, values, back, diag, base):
+    few = jnp.max(diag[4:5, :]) * largest <= exact_below
+
+    @pl.when(few)
+    def _():
+        target[...] = base + short_product(values, back)
+
+    @pl.when(jnp.logical_not(few))
+    def _():
+        target[...] = base + product(values, back[...].astype(f32).astype(bf16), 3)
 
 
 def table_product(table, values):
@@ -126,7 +156,7 @@
             out[j, span, :] = fields[j, span, :] + coef[j * pair : (j + 1) * pair]
 
 
-def mesh_kernel(nodes_hbm, mass_hbm, radial_hbm, stiff_hbm, iface_hbm, touch_out, back_out, at_iface, from_iface, diag, coefs, edge_touch, edge_back, edge_diag, touch, back, elem_nodes, mass, radial, stiff, iface, in_sems, out_sems):
+def mesh_kernel(nodes_hbm, mass_hbm, radial_hbm, stiff_hbm, iface_hbm, touch_out, back_out, at_iface, from_iface, diag, coefs, edge_touch, edge_back, edge_diag, touch, back, touch8, back8, elem_nodes, mass, radial, stiff, iface, in_sems, out_sems):
     loads = start_all(
         (nodes_hbm, mass_hbm, radial_hbm, stiff_hbm, iface_hbm), (elem_nodes, mass, radial, stiff, iface), in_sems
     )
@@ -151,18 +181,25 @@
             count = jnp.right_shift(total, 4 * q) & 15
             touch[q * words : (q + 1) * words, span] = count.astype(f32).astype(bf16)
         column = pl.ds(c * width, width)
-        sent.append(pltpu.make_async_copy(touch.at[:, column], touch_out.at[:, column], out_sems.at[c]))
+        touch8[:, span] = touch[:, span].astype(f32).astype(f8)
+        sent.append(pltpu.make_async_copy(touch8.at[:, column], touch_out.at[:, column], out_sems.at[c]))
         sent[-1].start()
         back[span, :] = touch[:, span].T
-        sent.append(pltpu.make_async_copy(back.at[column, :], back_out.at[column, :], out_sems.at[elems // width + c]))
+        back8[span, :] = back[span, :].astype(f32).astype(f8)
+        sent.append(pltpu.make_async_copy(back8.at[column, :], back_out.at[column, :], out_sems.at[elems // width + c]))
         sent[-1].start()
     node = lax.broadcasted_iota(jnp.int32, (nodes, shared), 0)
     hit = jnp.where(iface[...] == node, 1.0, 0.0)
     at_iface[...] = hit.astype(bf16)
+    last = pl.ds(elems, shared)
+    touch8[:, elems:] = hit.astype(f8)
+    sent.append(pltpu.make_async_copy(touch8.at[:, last], touch_out.at[:, last], out_sems.at[2 * elems // width]))
+    sent[-1].start()
     from_iface[...] = hit.T.astype(bf16)
     zero = jnp.zeros((5, elems), f32)
+    one = jnp.ones((1, elems), f32)
     coefs[...] = jnp.concatenate([mass[...] / 12.0, radial[...] / 12.0, stiff[...], zero], axis=0)
-    scaled = jnp.concatenate([mass[...] / 12.0, radial[...] / 12.0, 6.0 * stiff[...], zero], axis=0)
+    scaled = jnp.concatenate([mass[...] / 12.0, radial[...] / 12.0, 6.0 * stiff[...], one * 0.0, one, zero[:3]], axis=0)
     sums = product(scaled, back, 3)
     hits = jnp.dot(jnp.ones((16, shared), bf16), from_iface[...], preferred_element_type=f32)
     row = lax.broadcasted_iota(jnp.int32, (8, nodes), 0)
@@ -210,18 +247,19 @@
     return jnp.concatenate([forcing[b] for b in range(forcing.shape[0])], axis=1)
 
 
-def rhs_edge_kernel(forcing, touch, at_iface, edge_back, edge_diag, coefs, spread_out, edge):
-    given = together(forcing)
-    spread = product(given, touch) * coefs[0:1, :]
+def rhs_edge_kernel(forcing, touch, edge_back, edge_diag, coefs, spread_out, edge):
+    elems = coefs.shape[1]
+    sums = short_product(together(forcing), touch)
+    spread = sums[:, :elems] * coefs[0:1, :]
     spread_out[...] = spread
-    edge[...] = edge_diag[0:1, :] * product(given, at_iface, 3) + product(spread, edge_back, 3)
+    edge[...] = edge_diag[0:1, :] * sums[:, elems:] + product(spread, edge_back, 3)
 
 
 def rhs_kernel(per_dev, modes, forcing, spread, touch, back, diag, local, sums, inner):
     rows = spread.shape[0]
-    image = diag[0:1, :] * together(forcing) + product(spread[...], back)
-    local[...] = image
-    sums[...] = product(image, touch)
+    spread_into(local, spread[...], back, diag, diag[0:1, :] * together(forcing))
+    image = local[...]
+    sums[...] = short_product(image, touch.at[:, : spread.shape[1]])
     square = (2.0 * diag[3:4, :] - 1.0) * image * image
     inner[...] = lanes(row_sum(square), row_sum(at_nodes(row_factors(rows, per_dev, modes), diag) * square))
 
@@ -244,9 +282,9 @@
     factors = row_factors(local.shape[0], per_dev, modes)
     rhs = local[...] + product(edge[...], from_iface, 3)
     rhs_out[...] = rhs
-    image = at_nodes(factors, diag) * rhs + product(at_elems(factors, coefs) * sums[...], back)
-    image_out[...] = image
-    sums_out[...] = product(image, touch)
+    spread = at_elems(factors, coefs) * sums[...]
+    spread_into(image_out, spread, back, diag, at_nodes(factors, diag) * rhs)
+    sums_out[...] = short_product(image_out[...], touch.at[:, : spread.shape[1]])
 
 
 def resid_kernel(per_dev, modes, own, edge, rhs, image, sums, image_sums, from_iface, edge_touch, diag, coefs, resid_out, norms_out):
@@ -323,8 +361,8 @@
         ).transpose(1, 0, 2)
     columns = lax.all_to_all(packed, "mode", 0, 0, tiled=True)
     tables = (
-        shape(nodes, elems, kind=bf16),
-        shape(elems, nodes, kind=bf16),
+        shape(nodes, elems + shared, kind=f8),
+        shape(elems, nodes, kind=f8),
         shape(nodes, shared, kind=bf16),
         shape(shared, nodes, kind=bf16),
         shape(8, nodes),
@@ -342,13 +380,15 @@
         scratch_shapes=[
             pltpu.VMEM((nodes, elems), bf16),
             pltpu.VMEM((elems, nodes), bf16),
+            pltpu.VMEM((nodes, elems + shared), f8),
+            pltpu.VMEM((elems, nodes), f8),
             pltpu.VMEM(elem_nodes.shape, jnp.int32),
             pltpu.VMEM((1, elems), f32),
             pltpu.VMEM((1, elems), f32),
             pltpu.VMEM((1, elems), f32),
             pltpu.VMEM(iface.shape, jnp.int32),
             pltpu.SemaphoreType.DMA((5,)),
-            pltpu.SemaphoreType.DMA((2 * elems // math.gcd(elems, 256),)),
+            pltpu.SemaphoreType.DMA((2 * elems // math.gcd(elems, 256) + 1,)),
         ],
         compiler_params=params(large),
         name="incidence",
@@ -383,7 +423,7 @@
 
     full, part, small_row = shape(rows, nodes), shape(rows, elems), shape(rows, 128)
     spread, edge_own = call(rhs_edge_kernel, "rhs_edge", (part, shape(rows, shared)))(
-        forcing, touch, at_iface, edge_back, edge_diag, coefs
+        forcing, touch, edge_back, edge_diag, coefs
     )
     edge = swap(edge_own)
     local, sums, inner = call(rhs_kernel, "rhs", (full, part, small_row), 2**30)(

time: 41.8 us -> 40.4 us (0.967)
  waiting for transfers between devices: 6.93 us -> 5.58 us
    all_to_all x1, waiting for transfers between devices: 5.8 us -> 4.43 us  [per_device(): columns = lax.all_to_all(packed, 'mode', 0, 0, tiled=True)]
    pallas_call x1, Pallas kernels: 5.89 us -> 7.23 us  [per_device(): pl.pallas_call(mesh_kernel, in_specs=[in_hbm] * 5, out_specs=(in_hbm, in_...]
    pallas_call x1, Pallas kernels: 1.61 us -> 1.15 us  [per_device(): call(rhs_kernel, 'rhs', (full, part, small_row), 2 ** 30)]
    pallas_call x1, Pallas kernels: 1.7 us -> 1.25 us  [per_device(): call(image_kernel, 'image', (full, full, part), 2 ** 30)]
  transfers between devices with their start and end apart: 4 -> 4, of which waited for: 2 -> 2; matrix products, arithmetic and copies ran while one was open for 0% -> 0% of each run, Pallas kernels for 22% -> 24%
where the time goes in v7:
time: 40.4 us; the launch traced here: 40.1 us
  Pallas kernels  14.2 us (35%)
  blocking collectives  11.5 us (28%)
  starting transfers between devices  7.98 us (20%)
  waiting for transfers between devices  5.58 us (14%)
  between operations  0.81 us (2%)
    all_to_all x1, blocking collectives, per_device(): forcing = lax.all_to_all(terms, 'mode', 0, 0, tiled=True)  11.5 us
    all_to_all x1, starting transfers between devices, per_device(): columns = lax.all_to_all(packed, 'mode', 0, 0, tiled=True)  7.26 us
    pallas_call x1, Pallas kernels, per_device(): pl.pallas_call(mesh_kernel, in_specs=[in_hbm] * 5, out_specs=(in_hbm, in_...  7.23 us
    all_to_all x1, waiting for transfers between devices, per_device(): columns = lax.all_to_all(packed, 'mode', 0, 0, tiled=True)  4.43 us
    pallas_call x1, Pallas kernels, per_device(): pl.pallas_call(pack_kernel, in_specs=[in_hbm] * 4, out_shape=shape(owners...  1.79 us
    pallas_call x1, Pallas kernels, per_device(): call(image_kernel, 'image', (full, full, part), 2 ** 30)  1.25 us
    pallas_call x1, Pallas kernels, per_device(): call(rhs_kernel, 'rhs', (full, part, small_row), 2 ** 30)  1.15 us
    ppermute x3, waiting for transfers between devices, swap(): return lax.ppermute(array, 'mer', [(0, 1), (1, 0)])  1.14 us
  transfers between devices with their start and end apart: 4, of which 2 were waited for; matrix products, arithmetic and copies ran while one was open for 0% of the time, Pallas kernels for 24%

profile of v7, /device:TPU:0, one launch (start us, length us, event | category | flops | bytes accessed | tf_op | source)
XLA Modules:
  0.0 40.1 jit_solution(11050076351788609154)
XLA Ops:
  0.6 1.8 %pack.1 = f32[8,48,256]{2,1,0:T(8,128)} custom-call(f32[3,2,2,2048]{3,2,1,0:T(2,128)} %vel.1, f32[3,2,2,2048]{3,2,1,0:T(2,128)} %mag.1, f32[3,2,2,2048]{3,2,1,0:T(2,128)} %vort.1, f32[3,2,2,2048]{3,2,1,0:T(2,128)} %cur.1), custom_call_target="tpu_custom_call" | custom-call | tf_op jit(solution)/shard_map/pack/pallas_call | solution.py:344
  2.4 7.3 %all-to-all-start = ((f32[8,48,256]{2,1,0:T(8,128)}), f32[8,48,256]{2,1,0:T(8,128)S(1)}, u32[]{:S(2)}, u32[]{:S(2)}) async-start(f32[8,48,256]{2,1,0:T(8,128)} %pack.1), calls=%async_computation | async-start | bytes 786432 | tf_op jit(solution)/shard_map/all_to_all | solution.py:362
  9.7 0.0 copy-start.8
  9.7 0.0 copy-start.9
  9.7 7.2 %incidence.1 = (f8e4m3fn[2048,1152]{1,0:T(32,128)(4,1)}, f8e4m3fn[1024,2048]{1,0:T(32,128)(4,1)}, bf16[2048,128]{1,0:T(8,128)(2,1)}, bf16[128,2048]{1,0:T(8,128)...) custom-call(s32[6,1024]{1,0:T(8,128)} %nodes_hbm.1, ...), custom_call_target="tpu_custom_call" | custom-call | flops 2147483648 | bytes 8388608 | tf_op jit(solution)/shard_map/incidence/pallas_call | solution.py:375
  17.0 4.4 %all-to-all-done.fields = f32[8,48,256]{2,1,0:T(8,128)S(1)} async-done(((f32[8,48,256]{2,1,0:T(8,128)}), f32[8,48,256]{2,1,0:T(8,128)S(1)}, u32[]{:S(2)}, u32[]{:S(2)}) %all-to-all-start) | async-done | bytes 393248 | tf_op jit(solution)/shard_map/all_to_all | solution.py:362
  21.4 0.0 copy-done.8
  21.4 0.0 copy-done.9
  21.4 0.0 copy-start
  21.4 0.0 copy-start.4
  21.4 0.0 copy-start.6
  21.4 0.0 copy-start.7
  21.4 0.4 %nonlinear.1 = f32[8,24,256]{2,1,0:T(8,128)S(1)} custom-call(f32[8,48,256]{2,1,0:T(8,128)S(1)} %all-to-all-done.fields, bf16[64,192]{1,0:T(8,128)(2,1)S(1)} %copy-done.8, bf16[64,192]{1,0:T(8,128)(2,1)S(1)} %copy-done.9), custom_call_target="tpu_custom_call" | custom-call | flops 8589934592 | bytes 16777216 | tf_op jit(solution)/shard_map/nonlinear/pallas_call | solution.py:399
  21.8 0.0 copy-start.1
  21.8 0.0 copy-start.5
  21.9 11.5 %all_to_all.10.forcing = f32[8,24,256]{2,1,0:T(8,128)S(1)} all-to-all(f32[8,24,256]{2,1,0:T(8,128)S(1)} %nonlinear.1), channel_id=1, replica_groups=mesh['runs'=2,'mode'=8,'mer'=2] {'mode'}, dimensions={0} | all-to-all | bytes 393216 | tf_op jit(solution)/shard_map/all_to_all | solution.py:406
  33.3 0.0 copy-done
  33.3 0.0 copy-done.4
  33.4 0.0 copy-done.6
  33.4 0.0 copy-done.7
  33.4 0.6 %rhs_edge.1 = (f32[24,1024]{1,0:T(8,128)S(1)}, f32[24,128]{1,0:T(8,128)S(1)}) custom-call(f32[8,24,256]{2,1,0:T(8,128)S(1)} %all_to_all.10.forcing, f8e4m3fn[2048,1152]{1,0:T(32,128)(4,1)S(1)} %copy-done, bf16[1024,128]{1,0:T(8,128)(2,1)S(1)} %copy-done.4, f32[8,128]{1,0:T(8,128)S(1)} %copy-done.7, f32[8,1024]{1,0:T(8,128)S(1)} %copy-done.6), custom_call_target="tpu_custom_call" | custom-call | tf_op jit(solution)/shard_map/rhs_edge/pallas_call | solution.py:425
  34.0 0.1 collective-permute-start
  34.1 0.0 copy-done.1
  34.1 0.0 copy-done.5
  34.1 0.0 copy-start.3
  34.1 0.0 copy-start.2
  34.1 1.2 %rhs.1 = (f32[24,2048]{1,0:T(8,128)S(1)}, f32[24,1024]{1,0:T(8,128)S(1)}, f32[24,128]{1,0:T(8,128)S(1)}) custom-call(f32[8,24,256]{2,1,0:T(8,128)S(1)} %all_to_all.10.forcing, f32[24,1024]{1,0:T(8,128)S(1)} %get-tuple-element.45.spread, f8e4m3fn[2048,1152]{1,0:T(32,128)(4,1)S(1)} %copy-done, f8e4m3fn[1024,2048]{1,0:T(32,128)(4,1)S(1)} %copy-done.1, ...), custom_call_target="tpu_custom_call" | custom-call | flops 1073741824 | bytes 2097152 | tf_op jit(solution)/shard_map/rhs/pallas_call | solution.py:429
  35.3 0.0 collective-permute-done.edge
  35.3 0.0 copy-done.3
  35.3 0.4 image_edge.1
  35.7 0.5 %collective-permute-start.1 = (f32[24,256]{1,0:T(8,128)S(1)}, f32[24,256]{1,0:T(8,128)S(1)}, u32[]{:S(2)}, u32[]{:S(2)}) collective-permute-start(f32[24,256]{1,0:T(8,128)S(1)} %get-tuple-element.51.own), channel_id=1, source_target_pairs={{0,1},{1,0},{2,3},{3,2},{4,5},{5,4},{6,7},{7,6},{8,9},{9,8},{10,11... | collective-permute-start | bytes 73736 | tf_op jit(solution)/shard_map/ppermute | solution.py:411
  36.2 0.0 copy-done.2
  36.2 1.2 %image.1 = (f32[24,2048]{1,0:T(8,128)S(1)}, f32[24,2048]{1,0:T(8,128)S(1)}, f32[24,1024]{1,0:T(8,128)S(1)}) custom-call(f32[24,2048]{1,0:T(8,128)S(1)} %get-tuple-element.52.local, f32[24,128]{1,0:T(8,128)S(1)} %collective-permute-done.edge, f32[24,1024]{1,0:T(8,128)S(1)} %get-tuple-element.53.sums, f8e4m3fn[2048,1152]{1,0:T(32,128)(4,1)S(1)} %copy-done, ...), custom_call_target="tpu_custom_call" | custom-call | flops 1073741824 | bytes 2097152 | tf_op jit(solution)/shard_map/image/pallas_call | solution.py:436
  37.5 0.0 collective-permute-done.1.edge
  37.5 0.4 resid.1
  37.9 0.1 collective-permute-start.2
  38.0 1.1 %collective-permute-done.2.norms = f32[24,128]{1,0:T(8,128)S(1)} collective-permute-done((f32[24,128]{1,0:T(8,128)S(1)}, f32[24,128]{1,0:T(8,128)S(1)}, u32[]{:S(2)}, u32[]{:S(2)}) %collective-permute-start.2) | collective-permute-done | bytes 12320 | tf_op jit(solution)/shard_map/ppermute | solution.py:411
  39.1 1.0 %last.1 = (f32[3,2,2,2048]{3,2,1,0:T(2,128)}, f32[3,2,2,2048]{3,2,1,0:T(2,128)}) custom-call(f32[24,256]{1,0:T(8,128)S(1)} %collective-permute-done.1.edge, f32[24,256]{1,0:T(8,128)S(1)} %get-tuple-element.51.own, f32[24,128]{1,0:T(8,128)S(1)} %get-tuple-element.58.norms_own, f32[24,128]{1,0:T(8,128)S(1)} %collective-permute-done.2.norms, ...), custom_call_target="tpu_custom_call" | custom-call | tf_op jit(solution)/shard_map/last/pallas_call | solution.py:443
Async XLA Ops:
  2.4 19.0 %all-to-all-start = ((f32[8,48,256]{2,1,0:T(8,128)}), f32[8,48,256]{2,1,0:T(8,128)S(1)}, u32[]{:S(2)}, u32[]{:S(2)}) async-start(f32[8,48,256]{2,1,0:T(8,128)} %pack.1), calls=%async_computation | async-start | bytes 786432 | tf_op jit(solution)/shard_map/all_to_all | solution.py:362
  9.7 11.7 %copy-start.8 = (bf16[64,192]{1,0:T(8,128)(2,1)S(1)}, bf16[64,192]{1,0:T(8,128)(2,1)}, u32[]{:S(2)}) copy-start(bf16[64,192]{1,0:T(8,128)(2,1)} %constant.4.clone.synthesis) | copy-start | bytes 73732
  9.7 11.7 %copy-start.9 = (bf16[64,192]{1,0:T(8,128)(2,1)S(1)}, bf16[64,192]{1,0:T(8,128)(2,1)}, u32[]{:S(2)}) copy-start(bf16[64,192]{1,0:T(8,128)(2,1)} %constant.5.clone.analysis) | copy-start | bytes 73732
  21.4 12.0 %copy-start = (f8e4m3fn[2048,1152]{1,0:T(32,128)(4,1)S(1)}, f8e4m3fn[2048,1152]{1,0:T(32,128)(4,1)}, u32[]{:S(2)}) copy-start(f8e4m3fn[2048,1152]{1,0:T(32,128)(4,1)} %get-tuple-element.40.touch) | copy-start | bytes 7077892
  21.4 12.0 %copy-start.4 = (bf16[1024,128]{1,0:T(8,128)(2,1)S(1)}, bf16[1024,128]{1,0:T(8,128)(2,1)}, u32[]{:S(2)}) copy-start(bf16[1024,128]{1,0:T(8,128)(2,1)} %get-tuple-element.41.edge_back) | copy-start | bytes 786436
  21.4 12.0 %copy-start.6 = (f32[8,1024]{1,0:T(8,128)S(1)}, f32[8,1024]{1,0:T(8,128)}, u32[]{:S(2)}) copy-start(f32[8,1024]{1,0:T(8,128)} %get-tuple-element.43.coefs) | copy-start | bytes 98308
  21.4 11.9 %copy-start.7 = (f32[8,128]{1,0:T(8,128)S(1)}, f32[8,128]{1,0:T(8,128)}, u32[]{:S(2)}) copy-start(f32[8,128]{1,0:T(8,128)} %get-tuple-element.42.edge_diag) | copy-start | bytes 12292
  21.8 12.3 %copy-start.1 = (f8e4m3fn[1024,2048]{1,0:T(32,128)(4,1)S(1)}, f8e4m3fn[1024,2048]{1,0:T(32,128)(4,1)}, u32[]{:S(2)}) copy-start(f8e4m3fn[1024,2048]{1,0:T(32,128)(4,1)} %get-tuple-element.46.back) | copy-start | bytes 6291460
  21.8 12.3 %copy-start.5 = (f32[8,2048]{1,0:T(8,128)S(1)}, f32[8,2048]{1,0:T(8,128)}, u32[]{:S(2)}) copy-start(f32[8,2048]{1,0:T(8,128)} %get-tuple-element.47.diag) | copy-start | bytes 196612
  34.0 1.3 %collective-permute-start = (f32[24,128]{1,0:T(8,128)S(1)}, f32[24,128]{1,0:T(8,128)S(1)}, u32[]{:S(2)}, u32[]{:S(2)}) collective-permute-start(f32[24,128]{1,0:T(8,128)S(1)} %get-tuple-element.44.edge_own), channel_id=1, source_target_pairs={{0,1},{1,0},{2,3},{3,2},{4,5},{5,4},{6,7},{7,6},{8,9},{9,8},{10,11... | collective-permute-start | bytes 36872 | tf_op jit(solution)/shard_map/ppermute | solution.py:411
  34.1 1.2 %copy-start.3 = (bf16[128,1024]{1,0:T(8,128)(2,1)S(1)}, bf16[128,1024]{1,0:T(8,128)(2,1)}, u32[]{:S(2)}) copy-start(bf16[128,1024]{1,0:T(8,128)(2,1)} %get-tuple-element.50.edge_touch) | copy-start | bytes 786436
  34.1 2.1 %copy-start.2 = (bf16[128,2048]{1,0:T(8,128)(2,1)S(1)}, bf16[128,2048]{1,0:T(8,128)(2,1)}, u32[]{:S(2)}) copy-start(bf16[128,2048]{1,0:T(8,128)(2,1)} %get-tuple-element.54.from_iface) | copy-start | bytes 1572868
  35.7 1.8 %collective-permute-start.1 = (f32[24,256]{1,0:T(8,128)S(1)}, f32[24,256]{1,0:T(8,128)S(1)}, u32[]{:S(2)}, u32[]{:S(2)}) collective-permute-start(f32[24,256]{1,0:T(8,128)S(1)} %get-tuple-element.51.own), channel_id=1, source_target_pairs={{0,1},{1,0},{2,3},{3,2},{4,5},{5,4},{6,7},{7,6},{8,9},{9,8},{10,11... | collective-permute-start | bytes 73736 | tf_op jit(solution)/shard_map/ppermute | solution.py:411
  37.9 1.2 %collective-permute-start.2 = (f32[24,128]{1,0:T(8,128)S(1)}, f32[24,128]{1,0:T(8,128)S(1)}, u32[]{:S(2)}, u32[]{:S(2)}) collective-permute-start(f32[24,128]{1,0:T(8,128)S(1)} %get-tuple-element.58.norms_own), channel_id=1, source_target_pairs={{0,1},{1,0},{2,3},{3,2},{4,5},{5,4},{6,7},{7,6},{8,9},{9,8},{10,11... | collective-permute-start | bytes 36872 | tf_op jit(solution)/shard_map/ppermute | solution.py:411

commit v8 on v7

--- a/solution.py
+++ b/solution.py
@@ -65,8 +65,7 @@
     return total
 
 
-def short_product(array, exact, count=4):
-    rows = array.shape[0]
+def short_parts(array, count=4):
     top = jnp.maximum(jnp.max(jnp.abs(array), axis=1, keepdims=True), 1e-30)
     parts = []
     rest = array * (largest / top)
@@ -74,11 +73,20 @@
         part = jnp.round(rest)
         parts.append(part)
         rest = (rest - part) * radix
-    out = jnp.dot(jnp.concatenate(parts, axis=0).astype(f8), exact[...], preferred_element_type=f32)
+    return jnp.concatenate(parts, axis=0), top / largest
+
+
+def short_total(out, scale, count=4):
+    rows = scale.shape[0]
     total = out[(count - 1) * rows :]
     for i in reversed(range(count - 1)):
         total = total * (1.0 / radix) + out[i * rows : (i + 1) * rows]
-    return total * (top / largest)
+    return total * scale
+
+
+def short_product(array, exact):
+    parts, scale = short_parts(array)
+    return short_total(jnp.dot(parts.astype(f8), exact[...], preferred_element_type=f32), scale)
 
 
 def spread_into(target, values, back, diag, base):
@@ -109,27 +117,36 @@
     return copies
 
 
-def pack_kernel(vel, mag, vort, cur, out, held, ready, in_sems, out_sems):
-    blocks, rows, block = out.shape
-    copies = start_all((vel, mag, vort, cur), [held.at[i] for i in range(4)], in_sems)
-    sent = []
+def ring_pack_kernel(vel, mag, vort, cur, synthesis_hbm, analysis_hbm, *rest):
+    *outs, synthesis, analysis, held, in_sems = rest
+    owners, block = len(outs), outs[0].shape[1]
+    me = lax.axis_index("mode")
+    copies = start_all(
+        (vel, mag, vort, cur, synthesis_hbm, analysis_hbm),
+        [*(held.at[i] for i in range(4)), synthesis, analysis],
+        in_sems,
+    )
+    starts = [pl.multiple_of(lax.rem(me + d, owners) * block, block) for d in range(owners)]
     row = 0
     for i in range(4):
         copies[i].wait()
-        field = held.at[i]
-        comps, _, per_dev, _ = field.shape
+        _, comps, _, per_dev, _ = held.shape
         for c in range(comps):
             for s in range(2):
-                piece = field[c, s]
-                for b in range(blocks):
-                    ready[b, row : row + per_dev, :] = piece[:, b * block : (b + 1) * block]
+                for d in range(owners):
+                    outs[d][row : row + per_dev, :] = held[i, c, s, :, pl.ds(starts[d], block)]
                 row += per_dev
-        if i % 2:
-            half = pl.ds(i // 2 * (rows // 2), rows // 2)
-            sent.append(pltpu.make_async_copy(ready.at[:, half, :], out.at[:, half, :], out_sems.at[i // 2]))
-            sent[-1].start()
-    for copy in sent:
+    for copy in copies[4:]:
         copy.wait()
+
+
+def ring_nonlinear_kernel(*refs):
+    *blocks, synthesis, analysis, out, fields = refs
+    owners = len(blocks)
+    me = lax.axis_index("mode")
+    for d in range(owners):
+        fields[lax.rem(me + owners - d, owners)] = blocks[d][...]
+    nonlinear_kernel(fields, synthesis, analysis, out)
 
 
 def nonlinear_kernel(fields, synthesis, analysis, out):
@@ -247,9 +264,25 @@
     return jnp.concatenate([forcing[b] for b in range(forcing.shape[0])], axis=1)
 
 
-def rhs_edge_kernel(forcing, touch, edge_back, edge_diag, coefs, spread_out, edge):
+def rhs_edge_kernel(forcing, touch_hbm, back_hbm, diag_hbm, coefs_hbm, spread_out, edge, touch, edge_back, edge_diag, coefs, sems):
+    nodes = touch.shape[0]
     elems = coefs.shape[1]
-    sums = short_product(together(forcing), touch)
+    width = nodes // 4
+    spans = [pl.ds(i * width, width) for i in range(4)]
+    loads = start_all(
+        [touch_hbm.at[span, :] for span in spans] + [coefs_hbm, back_hbm, diag_hbm],
+        [touch.at[span, :] for span in spans] + [coefs, edge_back, edge_diag],
+        sems,
+    )
+    parts, scale = short_parts(together(forcing))
+    out = 0.0
+    for i in range(4):
+        loads[i].wait()
+        some = parts[:, i * width : (i + 1) * width].astype(f8)
+        out = out + jnp.dot(some, touch[i * width : (i + 1) * width, :], preferred_element_type=f32)
+    sums = short_total(out, scale)
+    for load in loads[4:]:
+        load.wait()
     spread = sums[:, :elems] * coefs[0:1, :]
     spread_out[...] = spread
     edge[...] = edge_diag[0:1, :] * sums[:, elems:] + product(spread, edge_back, 3)
@@ -340,26 +373,44 @@
         return jax.ShapeDtypeStruct(dims, kind)
 
     in_hbm = pl.BlockSpec(memory_space=pltpu.HBM)
-    if block % 128 == 0:
-        packed = pl.pallas_call(
-            pack_kernel,
-            in_specs=[in_hbm] * 4,
-            out_shape=shape(owners, 2 * rows, block),
-            out_specs=in_hbm,
-            scratch_shapes=[
-                pltpu.VMEM((4, *velocity.shape), f32),
-                pltpu.VMEM((owners, 2 * rows, block), f32),
-                pltpu.SemaphoreType.DMA((4,)),
-                pltpu.SemaphoreType.DMA((2,)),
-            ],
-            compiler_params=params(large),
+
+    def pin(array):
+        return pltpu.with_memory_space_constraint(array, pltpu.HBM)
+
+    nonlinear_cost = pl.CostEstimate(flops=2**33, bytes_accessed=2**24, transcendentals=0)
+    if owners <= 8 and block % 128 == 0:
+        *blocks, synthesis, analysis = pl.pallas_call(
+            ring_pack_kernel,
+            in_specs=[in_hbm] * 6,
+            out_shape=(pltpu.VMEM((2 * rows, block), f32),) * owners
+            + tuple(pltpu.VMEM(t.shape, t.dtype) for t in (synthesis, analysis)),
+            scratch_shapes=[pltpu.VMEM((4, *velocity.shape), f32), pltpu.SemaphoreType.DMA((6,))],
+            compiler_params=params(medium),
             name="pack",
-        )(velocity, magnetic, vorticity, current)
+        )(*(pin(a) for a in (velocity, magnetic, vorticity, current, synthesis, analysis)))
+        for d in range(1, owners):
+            blocks[d] = lax.ppermute(blocks[d], "mode", [(i, (i + d) % owners) for i in range(owners)])
+        terms = pl.pallas_call(
+            ring_nonlinear_kernel,
+            out_shape=shape(owners, rows, block),
+            scratch_shapes=[pltpu.VMEM((owners, 2 * rows, block), f32)],
+            compiler_params=params(),
+            name="nonlinear",
+            cost_estimate=nonlinear_cost,
+        )(*blocks, synthesis, analysis)
     else:
         packed = jnp.concatenate(
             [a.reshape(rows // 2, owners, block) for a in (velocity, magnetic, vorticity, current)], axis=0
         ).transpose(1, 0, 2)
-    columns = lax.all_to_all(packed, "mode", 0, 0, tiled=True)
+        terms = pl.pallas_call(
+            nonlinear_kernel,
+            out_shape=shape(owners, rows, block),
+            compiler_params=params(),
+            name="nonlinear",
+            cost_estimate=nonlinear_cost,
+        )(lax.all_to_all(packed, "mode", 0, 0, tiled=True), synthesis, analysis)
+    terms, elem_nodes = lax.optimization_barrier((terms, elem_nodes))
+    forcing = lax.all_to_all(terms, "mode", 0, 0, tiled=True)
     tables = (
         shape(nodes, elems + shared, kind=f8),
         shape(elems, nodes, kind=f8),
@@ -394,16 +445,7 @@
         name="incidence",
         cost_estimate=pl.CostEstimate(flops=2**31, bytes_accessed=2**23, transcendentals=0),
     )(elem_nodes, mass, radial, stiff, iface)
-    columns, *built = lax.optimization_barrier((columns, *built))
     touch, back, at_iface, from_iface, diag, coefs, edge_touch, edge_back, edge_diag = built
-    terms = pl.pallas_call(
-        nonlinear_kernel,
-        out_shape=pltpu.VMEM((owners, rows, block), f32),
-        compiler_params=params(),
-        name="nonlinear",
-        cost_estimate=pl.CostEstimate(flops=2**33, bytes_accessed=2**24, transcendentals=0),
-    )(pltpu.with_memory_space_constraint(columns, pltpu.VMEM), synthesis, analysis)
-    forcing = lax.all_to_all(terms, "mode", 0, 0, tiled=True)
     if block % 128:
         forcing = forcing.transpose(1, 0, 2).reshape(1, rows, nodes)
 
@@ -411,10 +453,9 @@
         return lax.ppermute(array, "mer", [(0, 1), (1, 0)])
 
     def call(kernel, name, outs, work=0):
-        own = () if kernel is rhs_edge_kernel else (per_dev, modes)
         cost = pl.CostEstimate(flops=work, bytes_accessed=work // 512, transcendentals=0) if work else None
         return pl.pallas_call(
-            functools.partial(kernel, *own),
+            functools.partial(kernel, per_dev, modes),
             out_shape=tuple(outs),
             compiler_params=params(),
             name=name,
@@ -422,9 +463,15 @@
         )
 
     full, part, small_row = shape(rows, nodes), shape(rows, elems), shape(rows, 128)
-    spread, edge_own = call(rhs_edge_kernel, "rhs_edge", (part, shape(rows, shared)))(
-        forcing, touch, edge_back, edge_diag, coefs
-    )
+    kept = [pltpu.VMEM(a.shape, a.dtype) for a in (touch, edge_back, edge_diag, coefs)]
+    spread, edge_own, touch, edge_back, edge_diag, coefs = pl.pallas_call(
+        rhs_edge_kernel,
+        in_specs=[in_vmem] + [in_hbm] * 4,
+        out_shape=(part, shape(rows, shared), *kept),
+        scratch_shapes=[pltpu.SemaphoreType.DMA((7,))],
+        compiler_params=params(),
+        name="rhs_edge",
+    )(forcing, *(pin(a) for a in (touch, edge_back, edge_diag, coefs)))
     edge = swap(edge_own)
     local, sums, inner = call(rhs_kernel, "rhs", (full, part, small_row), 2**30)(
         forcing, spread, touch, back, diag

time: 40.4 us -> 41.3 us (1.022)
  starting transfers between devices: 7.98 us -> 19.9 us
  blocking collectives: 11.5 us -> 0 us
  Pallas kernels: 14.2 us -> 15.9 us
  waiting for transfers between devices: 5.58 us -> 4.34 us
    ppermute x0 -> x7, starting transfers between devices: none -> 13.8 us  [per_device(): lax.ppermute(blocks[d], 'mode', [(i, (i + d) % owners) for i in range(own...]
    all_to_all x1 -> x0, blocking collectives: 11.5 us -> none  [per_device(): forcing = lax.all_to_all(terms, 'mode', 0, 0, tiled=True)]
    all_to_all x1, waiting for transfers between devices: 4.43 us -> 0.54 us  [per_device(): forcing = lax.all_to_all(terms, 'mode', 0, 0, tiled=True)]
    ppermute x0 -> x7, waiting for transfers between devices: none -> 2.66 us  [per_device(): lax.ppermute(blocks[d], 'mode', [(i, (i + d) % owners) for i in range(own...]
    all_to_all x1, starting transfers between devices: 7.26 us -> 5.41 us  [per_device(): forcing = lax.all_to_all(terms, 'mode', 0, 0, tiled=True)]
    pallas_call x3, Pallas kernels: 2.85 us -> 4.59 us  [the longest x1 2.32 us: per_device(): pl.pallas_call(rhs_edge_kernel, in_specs=[in_vmem] + [in_hbm] * 4, out_sh...]
  transfers between devices with their start and end apart: 4 -> 11, of which waited for: 2 -> 5; matrix products, arithmetic and copies ran while one was open for 0% -> 0% of each run, Pallas kernels for 24% -> 23%
where the time goes in v8:
time: 41.3 us; the launch traced here: 40.9 us
  starting transfers between devices  19.9 us (48%)
  Pallas kernels  15.9 us (38%)
  waiting for transfers between devices  4.34 us (11%)
  between operations  0.77 us (2%)
    ppermute x7, starting transfers between devices, per_device(): lax.ppermute(blocks[d], 'mode', [(i, (i + d) % owners) for i in range(own...  13.8 us
    pallas_call x1, Pallas kernels, per_device(): pl.pallas_call(mesh_kernel, in_specs=[in_hbm] * 5, out_specs=(in_hbm, in_...  7.21 us
    all_to_all x1, starting transfers between devices, per_device(): forcing = lax.all_to_all(terms, 'mode', 0, 0, tiled=True)  5.41 us
    ppermute x7, waiting for transfers between devices, per_device(): lax.ppermute(blocks[d], 'mode', [(i, (i + d) % owners) for i in range(own...  2.66 us
    pallas_call x1, Pallas kernels, per_device(): pl.pallas_call(rhs_edge_kernel, in_specs=[in_vmem] + [in_hbm] * 4, out_sh...  2.32 us
    pallas_call x1, Pallas kernels, per_device(): call(image_kernel, 'image', (full, full, part), 2 ** 30)  1.24 us
    ppermute x3, waiting for transfers between devices, swap(): return lax.ppermute(array, 'mer', [(0, 1), (1, 0)])  1.14 us
    pallas_call x1, Pallas kernels, per_device(): call(rhs_kernel, 'rhs', (full, part, small_row), 2 ** 30)  1.14 us
  transfers between devices with their start and end apart: 11, of which 5 were waited for; matrix products, arithmetic and copies ran while one was open for 0% of the time, Pallas kernels for 23%

profile of v8, /device:TPU:0, one launch (start us, length us, event | category | flops | bytes accessed | tf_op | source)
XLA Modules:
  0.0 40.9 jit_solution(10907842413704318633)
XLA Ops:
  0.6 1.1 %pack.1 = (f32[48,256]{1,0:T(8,128)S(1)}, f32[48,256]{1,0:T(8,128)S(1)}, f32[48,256]{1,0:T(8,128)S(1)}, f32[48,256]{1,0:T(8,128)S(1)}, f32[48,256]{1,0:T(8,128)S...) custom-call(f32[3,2,2,2048]{3,2,1,0:T(2,128)} %vel.1, ...), custom_call_target="tpu_custom_call" | custom-call | tf_op jit(solution)/shard_map/pack/pallas_call | solution.py:382
  1.8 3.0 %collective-permute-start = (f32[48,256]{1,0:T(8,128)S(1)}, f32[48,256]{1,0:T(8,128)S(1)}, u32[]{:S(2)}, u32[]{:S(2)}) collective-permute-start(f32[48,256]{1,0:T(8,128)S(1)} %get-tuple-element.39), channel_id=1, source_target_pairs={{0,2},{2,4},{4,6},{6,8},{8,10},{10,12},{12,14},{14,0},{1,3},{3,5},... | collective-permute-start | bytes 147464 | tf_op jit(solution)/shard_map/ppermute | solution.py:392
  4.8 1.6 %collective-permute-start.1 = (f32[48,256]{1,0:T(8,128)S(1)}, f32[48,256]{1,0:T(8,128)S(1)}, u32[]{:S(2)}, u32[]{:S(2)}) collective-permute-start(f32[48,256]{1,0:T(8,128)S(1)} %get-tuple-element.40), channel_id=1, source_target_pairs={{0,4},{2,6},{4,8},{6,10},{8,12},{10,14},{12,0},{14,2},{1,5},{3,7},... | collective-permute-start | bytes 147464 | tf_op jit(solution)/shard_map/ppermute | solution.py:392
  6.3 2.6 %collective-permute-start.2 = (f32[48,256]{1,0:T(8,128)S(1)}, f32[48,256]{1,0:T(8,128)S(1)}, u32[]{:S(2)}, u32[]{:S(2)}) collective-permute-start(f32[48,256]{1,0:T(8,128)S(1)} %get-tuple-element.41), channel_id=1, source_target_pairs={{0,6},{2,8},{4,10},{6,12},{8,14},{10,0},{12,2},{14,4},{1,7},{3,9},... | collective-permute-start | bytes 147464 | tf_op jit(solution)/shard_map/ppermute | solution.py:392
  8.9 1.2 %collective-permute-start.3 = (f32[48,256]{1,0:T(8,128)S(1)}, f32[48,256]{1,0:T(8,128)S(1)}, u32[]{:S(2)}, u32[]{:S(2)}) collective-permute-start(f32[48,256]{1,0:T(8,128)S(1)} %get-tuple-element.42), channel_id=1, source_target_pairs={{0,8},{2,10},{4,12},{6,14},{8,0},{10,2},{12,4},{14,6},{1,9},{3,11}... | collective-permute-start | bytes 147464 | tf_op jit(solution)/shard_map/ppermute | solution.py:392
  10.1 2.6 %collective-permute-start.4 = (f32[48,256]{1,0:T(8,128)S(1)}, f32[48,256]{1,0:T(8,128)S(1)}, u32[]{:S(2)}, u32[]{:S(2)}) collective-permute-start(f32[48,256]{1,0:T(8,128)S(1)} %get-tuple-element.43), channel_id=1, source_target_pairs={{0,10},{2,12},{4,14},{6,0},{8,2},{10,4},{12,6},{14,8},{1,11},{3,13... | collective-permute-start | bytes 147464 | tf_op jit(solution)/shard_map/ppermute | solution.py:392
  12.8 0.0 collective-permute-done.refs_1_
  12.8 1.3 %collective-permute-start.5 = (f32[48,256]{1,0:T(8,128)S(1)}, f32[48,256]{1,0:T(8,128)S(1)}, u32[]{:S(2)}, u32[]{:S(2)}) collective-permute-start(f32[48,256]{1,0:T(8,128)S(1)} %get-tuple-element.44), channel_id=1, source_target_pairs={{0,12},{2,14},{4,0},{6,2},{8,4},{10,6},{12,8},{14,10},{1,13},{3,15... | collective-permute-start | bytes 147464 | tf_op jit(solution)/shard_map/ppermute | solution.py:392
  14.1 0.0 collective-permute-done.1.refs_2_
  14.1 1.4 %collective-permute-start.6 = (f32[48,256]{1,0:T(8,128)S(1)}, f32[48,256]{1,0:T(8,128)S(1)}, u32[]{:S(2)}, u32[]{:S(2)}) collective-permute-start(f32[48,256]{1,0:T(8,128)S(1)} %get-tuple-element.45), channel_id=1, source_target_pairs={{0,14},{2,0},{4,2},{6,4},{8,6},{10,8},{12,10},{14,12},{1,15},{3,1}... | collective-permute-start | bytes 147464 | tf_op jit(solution)/shard_map/ppermute | solution.py:392
  15.5 0.0 collective-permute-done.2.refs_3_
  15.5 0.0 collective-permute-done.3.refs_4_
  15.5 0.3 collective-permute-done.4.refs_5_
  15.9 1.4 %collective-permute-done.5.refs_6_ = f32[48,256]{1,0:T(8,128)S(1)} collective-permute-done((f32[48,256]{1,0:T(8,128)S(1)}, f32[48,256]{1,0:T(8,128)S(1)}, u32[]{:S(2)}, u32[]{:S(2)}) %collective-permute-start.5) | collective-permute-done | bytes 49184 | tf_op jit(solution)/shard_map/ppermute | solution.py:392
  17.2 1.0 %collective-permute-done.6.refs_7_ = f32[48,256]{1,0:T(8,128)S(1)} collective-permute-done((f32[48,256]{1,0:T(8,128)S(1)}, f32[48,256]{1,0:T(8,128)S(1)}, u32[]{:S(2)}, u32[]{:S(2)}) %collective-permute-start.6) | collective-permute-done | bytes 49184 | tf_op jit(solution)/shard_map/ppermute | solution.py:392
  18.2 1.1 %nonlinear.1 = f32[8,24,256]{2,1,0:T(8,128)} custom-call(f32[48,256]{1,0:T(8,128)S(1)} %get-tuple-element.38.refs_0_, f32[48,256]{1,0:T(8,128)S(1)} %collective-permute-done.refs_1_, f32[48,256]{1,0:T(8,128)S(1)} %collective-permute-done.1.refs_2_, f32[48,256]{1,0:T(8,128)S(1)} %collective-permute-done.2.refs_3_, ...), custom_call_target="tpu_custom_call" | custom-call | flops 8589934592 | bytes 16777216 | tf_op jit(solution)/shard_map/nonlinear/pallas_call | solution.py:393
  19.3 5.4 %all-to-all-start = ((f32[8,24,256]{2,1,0:T(8,128)}), f32[8,24,256]{2,1,0:T(8,128)S(1)}, u32[]{:S(2)}, u32[]{:S(2)}) async-start(f32[8,24,256]{2,1,0:T(8,128)} %nonlinear.1), calls=%async_computation | async-start | bytes 393216 | tf_op jit(solution)/shard_map/all_to_all | solution.py:413
  24.7 7.2 %incidence.1 = (f8e4m3fn[2048,1152]{1,0:T(32,128)(4,1)}, f8e4m3fn[1024,2048]{1,0:T(32,128)(4,1)}, bf16[2048,128]{1,0:T(8,128)(2,1)}, bf16[128,2048]{1,0:T(8,128)...) custom-call(s32[6,1024]{1,0:T(8,128)} %nodes_hbm, ...), custom_call_target="tpu_custom_call" | custom-call | flops 2147483648 | bytes 8388608 | tf_op jit(solution)/shard_map/incidence/pallas_call | solution.py:426
  32.0 0.0 copy-start
  32.0 0.0 copy-start.3
  32.0 0.5 %all-to-all-done.forcing = f32[8,24,256]{2,1,0:T(8,128)S(1)} async-done(((f32[8,24,256]{2,1,0:T(8,128)}), f32[8,24,256]{2,1,0:T(8,128)S(1)}, u32[]{:S(2)}, u32[]{:S(2)}) %all-to-all-start) | async-done | bytes 196640 | tf_op jit(solution)/shard_map/all_to_all | solution.py:413
  32.5 2.3 %rhs_edge.1 = (f32[24,1024]{1,0:T(8,128)S(1)}, f32[24,128]{1,0:T(8,128)S(1)}, f8e4m3fn[2048,1152]{1,0:T(32,128)(4,1)S(1)}, bf16[1024,128]{1,0:T(8,128)(2,1)S(1)}...) custom-call(f32[8,24,256]{2,1,0:T(8,128)S(1)} %all-to-all-done.forcing, ...), custom_call_target="tpu_custom_call" | custom-call | tf_op jit(solution)/shard_map/rhs_edge/pallas_call | solution.py:467
  34.9 0.1 collective-permute-start.7
  34.9 0.0 copy-done
  34.9 0.0 copy-done.3
  35.0 0.0 copy-start.2
  35.0 0.0 copy-start.1
  35.0 1.1 %rhs.1 = (f32[24,2048]{1,0:T(8,128)S(1)}, f32[24,1024]{1,0:T(8,128)S(1)}, f32[24,128]{1,0:T(8,128)S(1)}) custom-call(f32[8,24,256]{2,1,0:T(8,128)S(1)} %all-to-all-done.forcing, f32[24,1024]{1,0:T(8,128)S(1)} %get-tuple-element.55.spread, f8e4m3fn[2048,1152]{1,0:T(32,128)(4,1)S(1)} %get-tuple-element.56.touch, f8e4m3fn[1024,2048]{1,0:T(32,128)(4,1)S(1)} %copy-done, ...), custom_call_target="tpu_custom_call" | custom-call | flops 1073741824 | bytes 2097152 | tf_op jit(solution)/shard_map/rhs/pallas_call | solution.py:476
  36.1 0.0 collective-permute-done.7.edge
  36.1 0.0 copy-done.2
  36.1 0.4 image_edge.1
  36.5 0.5 %collective-permute-start.8 = (f32[24,256]{1,0:T(8,128)S(1)}, f32[24,256]{1,0:T(8,128)S(1)}, u32[]{:S(2)}, u32[]{:S(2)}) collective-permute-start(f32[24,256]{1,0:T(8,128)S(1)} %get-tuple-element.65.own), channel_id=1, source_target_pairs={{0,1},{1,0},{2,3},{3,2},{4,5},{5,4},{6,7},{7,6},{8,9},{9,8},{10,11... | collective-permute-start | bytes 73736 | tf_op jit(solution)/shard_map/ppermute | solution.py:453
  37.0 0.0 copy-done.1
  37.0 1.2 %image.1 = (f32[24,2048]{1,0:T(8,128)S(1)}, f32[24,2048]{1,0:T(8,128)S(1)}, f32[24,1024]{1,0:T(8,128)S(1)}) custom-call(f32[24,2048]{1,0:T(8,128)S(1)} %get-tuple-element.66.local, f32[24,128]{1,0:T(8,128)S(1)} %collective-permute-done.7.edge, f32[24,1024]{1,0:T(8,128)S(1)} %get-tuple-element.67.sums, f8e4m3fn[2048,1152]{1,0:T(32,128)(4,1)S(1)} %get-tuple-element.56.touch, ...), custom_call_target="tpu_custom_call" | custom-call | flops 1073741824 | bytes 2097152 | tf_op jit(solution)/shard_map/image/pallas_call | solution.py:483
  38.3 0.0 collective-permute-done.8.edge
  38.3 0.4 resid.1
  38.7 0.1 collective-permute-start.9
  38.8 1.1 %collective-permute-done.9.norms = f32[24,128]{1,0:T(8,128)S(1)} collective-permute-done((f32[24,128]{1,0:T(8,128)S(1)}, f32[24,128]{1,0:T(8,128)S(1)}, u32[]{:S(2)}, u32[]{:S(2)}) %collective-permute-start.9) | collective-permute-done | bytes 12320 | tf_op jit(solution)/shard_map/ppermute | solution.py:453
  39.9 1.0 %last.1 = (f32[3,2,2,2048]{3,2,1,0:T(2,128)}, f32[3,2,2,2048]{3,2,1,0:T(2,128)}) custom-call(f32[24,256]{1,0:T(8,128)S(1)} %collective-permute-done.8.edge, f32[24,256]{1,0:T(8,128)S(1)} %get-tuple-element.65.own, f32[24,128]{1,0:T(8,128)S(1)} %get-tuple-element.72.norms_own, f32[24,128]{1,0:T(8,128)S(1)} %collective-permute-done.9.norms, ...), custom_call_target="tpu_custom_call" | custom-call | tf_op jit(solution)/shard_map/last/pallas_call | solution.py:490
Async XLA Ops:
  1.8 11.0 %collective-permute-start = (f32[48,256]{1,0:T(8,128)S(1)}, f32[48,256]{1,0:T(8,128)S(1)}, u32[]{:S(2)}, u32[]{:S(2)}) collective-permute-start(f32[48,256]{1,0:T(8,128)S(1)} %get-tuple-element.39), channel_id=1, source_target_pairs={{0,2},{2,4},{4,6},{6,8},{8,10},{10,12},{12,14},{14,0},{1,3},{3,5},... | collective-permute-start | bytes 147464 | tf_op jit(solution)/shard_map/ppermute | solution.py:392
  4.8 9.3 %collective-permute-start.1 = (f32[48,256]{1,0:T(8,128)S(1)}, f32[48,256]{1,0:T(8,128)S(1)}, u32[]{:S(2)}, u32[]{:S(2)}) collective-permute-start(f32[48,256]{1,0:T(8,128)S(1)} %get-tuple-element.40), channel_id=1, source_target_pairs={{0,4},{2,6},{4,8},{6,10},{8,12},{10,14},{12,0},{14,2},{1,5},{3,7},... | collective-permute-start | bytes 147464 | tf_op jit(solution)/shard_map/ppermute | solution.py:392
  6.3 9.2 %collective-permute-start.2 = (f32[48,256]{1,0:T(8,128)S(1)}, f32[48,256]{1,0:T(8,128)S(1)}, u32[]{:S(2)}, u32[]{:S(2)}) collective-permute-start(f32[48,256]{1,0:T(8,128)S(1)} %get-tuple-element.41), channel_id=1, source_target_pairs={{0,6},{2,8},{4,10},{6,12},{8,14},{10,0},{12,2},{14,4},{1,7},{3,9},... | collective-permute-start | bytes 147464 | tf_op jit(solution)/shard_map/ppermute | solution.py:392
  8.9 6.6 %collective-permute-start.3 = (f32[48,256]{1,0:T(8,128)S(1)}, f32[48,256]{1,0:T(8,128)S(1)}, u32[]{:S(2)}, u32[]{:S(2)}) collective-permute-start(f32[48,256]{1,0:T(8,128)S(1)} %get-tuple-element.42), channel_id=1, source_target_pairs={{0,8},{2,10},{4,12},{6,14},{8,0},{10,2},{12,4},{14,6},{1,9},{3,11}... | collective-permute-start | bytes 147464 | tf_op jit(solution)/shard_map/ppermute | solution.py:392
  10.1 5.7 %collective-permute-start.4 = (f32[48,256]{1,0:T(8,128)S(1)}, f32[48,256]{1,0:T(8,128)S(1)}, u32[]{:S(2)}, u32[]{:S(2)}) collective-permute-start(f32[48,256]{1,0:T(8,128)S(1)} %get-tuple-element.43), channel_id=1, source_target_pairs={{0,10},{2,12},{4,14},{6,0},{8,2},{10,4},{12,6},{14,8},{1,11},{3,13... | collective-permute-start | bytes 147464 | tf_op jit(solution)/shard_map/ppermute | solution.py:392
  12.8 4.5 %collective-permute-start.5 = (f32[48,256]{1,0:T(8,128)S(1)}, f32[48,256]{1,0:T(8,128)S(1)}, u32[]{:S(2)}, u32[]{:S(2)}) collective-permute-start(f32[48,256]{1,0:T(8,128)S(1)} %get-tuple-element.44), channel_id=1, source_target_pairs={{0,12},{2,14},{4,0},{6,2},{8,4},{10,6},{12,8},{14,10},{1,13},{3,15... | collective-permute-start | bytes 147464 | tf_op jit(solution)/shard_map/ppermute | solution.py:392
  14.1 4.1 %collective-permute-start.6 = (f32[48,256]{1,0:T(8,128)S(1)}, f32[48,256]{1,0:T(8,128)S(1)}, u32[]{:S(2)}, u32[]{:S(2)}) collective-permute-start(f32[48,256]{1,0:T(8,128)S(1)} %get-tuple-element.45), channel_id=1, source_target_pairs={{0,14},{2,0},{4,2},{6,4},{8,6},{10,8},{12,10},{14,12},{1,15},{3,1}... | collective-permute-start | bytes 147464 | tf_op jit(solution)/shard_map/ppermute | solution.py:392
  19.3 13.2 %all-to-all-start = ((f32[8,24,256]{2,1,0:T(8,128)}), f32[8,24,256]{2,1,0:T(8,128)S(1)}, u32[]{:S(2)}, u32[]{:S(2)}) async-start(f32[8,24,256]{2,1,0:T(8,128)} %nonlinear.1), calls=%async_computation | async-start | bytes 393216 | tf_op jit(solution)/shard_map/all_to_all | solution.py:413
  32.0 3.0 %copy-start = (f8e4m3fn[1024,2048]{1,0:T(32,128)(4,1)S(1)}, f8e4m3fn[1024,2048]{1,0:T(32,128)(4,1)}, u32[]{:S(2)}) copy-start(f8e4m3fn[1024,2048]{1,0:T(32,128)(4,1)} %get-tuple-element.57.back) | copy-start | bytes 6291460
  32.0 3.0 %copy-start.3 = (f32[8,2048]{1,0:T(8,128)S(1)}, f32[8,2048]{1,0:T(8,128)}, u32[]{:S(2)}) copy-start(f32[8,2048]{1,0:T(8,128)} %get-tuple-element.58.diag) | copy-start | bytes 196612
  34.9 1.3 %collective-permute-start.7 = (f32[24,128]{1,0:T(8,128)S(1)}, f32[24,128]{1,0:T(8,128)S(1)}, u32[]{:S(2)}, u32[]{:S(2)}) collective-permute-start(f32[24,128]{1,0:T(8,128)S(1)} %get-tuple-element.54.edge_own), channel_id=1, source_target_pairs={{0,1},{1,0},{2,3},{3,2},{4,5},{5,4},{6,7},{7,6},{8,9},{9,8},{10,11... | collective-permute-start | bytes 36872 | tf_op jit(solution)/shard_map/ppermute | solution.py:453
  35.0 1.2 %copy-start.2 = (bf16[128,1024]{1,0:T(8,128)(2,1)S(1)}, bf16[128,1024]{1,0:T(8,128)(2,1)}, u32[]{:S(2)}) copy-start(bf16[128,1024]{1,0:T(8,128)(2,1)} %get-tuple-element.61.edge_touch) | copy-start | bytes 786436
  35.0 2.1 %copy-start.1 = (bf16[128,2048]{1,0:T(8,128)(2,1)S(1)}, bf16[128,2048]{1,0:T(8,128)(2,1)}, u32[]{:S(2)}) copy-start(bf16[128,2048]{1,0:T(8,128)(2,1)} %get-tuple-element.68.from_iface) | copy-start | bytes 1572868
  36.5 1.8 %collective-permute-start.8 = (f32[24,256]{1,0:T(8,128)S(1)}, f32[24,256]{1,0:T(8,128)S(1)}, u32[]{:S(2)}, u32[]{:S(2)}) collective-permute-start(f32[24,256]{1,0:T(8,128)S(1)} %get-tuple-element.65.own), channel_id=1, source_target_pairs={{0,1},{1,0},{2,3},{3,2},{4,5},{5,4},{6,7},{7,6},{8,9},{9,8},{10,11... | collective-permute-start | bytes 73736 | tf_op jit(solution)/shard_map/ppermute | solution.py:453
  38.7 1.2 %collective-permute-start.9 = (f32[24,128]{1,0:T(8,128)S(1)}, f32[24,128]{1,0:T(8,128)S(1)}, u32[]{:S(2)}, u32[]{:S(2)}) collective-permute-start(f32[24,128]{1,0:T(8,128)S(1)} %get-tuple-element.72.norms_own), channel_id=1, source_target_pairs={{0,1},{1,0},{2,3},{3,2},{4,5},{5,4},{6,7},{7,6},{8,9},{9,8},{10,11... | collective-permute-start | bytes 36872 | tf_op jit(solution)/shard_map/ppermute | solution.py:453

commit v9 on v8

--- a/solution.py
+++ b/solution.py
@@ -173,18 +173,23 @@
             out[j, span, :] = fields[j, span, :] + coef[j * pair : (j + 1) * pair]
 
 
-def mesh_kernel(nodes_hbm, mass_hbm, radial_hbm, stiff_hbm, iface_hbm, touch_out, back_out, at_iface, from_iface, diag, coefs, edge_touch, edge_back, edge_diag, touch, back, touch8, back8, elem_nodes, mass, radial, stiff, iface, in_sems, out_sems):
+def mesh_kernel(nodes_hbm, mass_hbm, radial_hbm, stiff_hbm, iface_hbm, touch_out, back_out, from_iface, diag, coefs, edge_touch, edge_back, edge_diag, touch, back, elem_nodes, mass, radial, stiff, iface, in_sems, out_sems):
     loads = start_all(
         (nodes_hbm, mass_hbm, radial_hbm, stiff_hbm, iface_hbm), (elem_nodes, mass, radial, stiff, iface), in_sems
     )
     for load in loads:
         load.wait()
-    nodes, elems = touch.shape
+    elems, nodes = back.shape
     shared = iface.shape[1]
     fields = 8
     words = nodes // fields
     width = math.gcd(elems, 256)
     sent = []
+
+    def send(source, target):
+        sent.append(pltpu.make_async_copy(source, target, out_sems.at[len(sent)]))
+        sent[-1].start()
+
     for c in range(elems // width):
         span = slice(c * width, (c + 1) * width)
         word = lax.broadcasted_iota(jnp.int32, (words, width), 0)
@@ -195,36 +200,37 @@
             value = jnp.left_shift(1, field * 4)
             total = total + jnp.where(ids - field * words == word, value, 0)
         for q in range(fields):
-            count = jnp.right_shift(total, 4 * q) & 15
-            touch[q * words : (q + 1) * words, span] = count.astype(f32).astype(bf16)
+            count = (jnp.right_shift(total, 4 * q) & 15).astype(f32)
+            touch[q * words : (q + 1) * words, span] = count.astype(f8)
+            back[span, q * words : (q + 1) * words] = count.T.astype(f8)
         column = pl.ds(c * width, width)
-        touch8[:, span] = touch[:, span].astype(f32).astype(f8)
-        sent.append(pltpu.make_async_copy(touch8.at[:, column], touch_out.at[:, column], out_sems.at[c]))
-        sent[-1].start()
-        back[span, :] = touch[:, span].T
-        back8[span, :] = back[span, :].astype(f32).astype(f8)
-        sent.append(pltpu.make_async_copy(back8.at[column, :], back_out.at[column, :], out_sems.at[elems // width + c]))
-        sent[-1].start()
+        send(touch.at[:, column], touch_out.at[:, column])
+        send(back.at[column, :], back_out.at[column, :])
     node = lax.broadcasted_iota(jnp.int32, (nodes, shared), 0)
     hit = jnp.where(iface[...] == node, 1.0, 0.0)
-    at_iface[...] = hit.astype(bf16)
-    last = pl.ds(elems, shared)
-    touch8[:, elems:] = hit.astype(f8)
-    sent.append(pltpu.make_async_copy(touch8.at[:, last], touch_out.at[:, last], out_sems.at[2 * elems // width]))
-    sent[-1].start()
-    from_iface[...] = hit.T.astype(bf16)
+    touch[:, elems:] = hit.astype(f8)
+    send(touch.at[:, pl.ds(elems, shared)], touch_out.at[:, pl.ds(elems, shared)])
+    hit = hit.T
+    from_iface[...] = hit.astype(bf16)
+    counts = jnp.dot(hit.astype(f8), touch[:, :elems], preferred_element_type=f32)
+    edge_touch[...] = counts.astype(bf16)
+    edge_back[...] = counts.T.astype(bf16)
     zero = jnp.zeros((5, elems), f32)
     one = jnp.ones((1, elems), f32)
     coefs[...] = jnp.concatenate([mass[...] / 12.0, radial[...] / 12.0, stiff[...], zero], axis=0)
-    scaled = jnp.concatenate([mass[...] / 12.0, radial[...] / 12.0, 6.0 * stiff[...], one * 0.0, one, zero[:3]], axis=0)
-    sums = product(scaled, back, 3)
-    hits = jnp.dot(jnp.ones((16, shared), bf16), from_iface[...], preferred_element_type=f32)
+    scaled = jnp.concatenate(
+        [mass[...] / 12.0, radial[...] / 12.0, 6.0 * stiff[...], one * 0.0, one, zero[:3]], axis=0
+    )
+    diag[...] = short_product(scaled, back)
+
+    @pl.when(jnp.max(diag[4:5, :]) * largest > exact_below)
+    def _():
+        diag[...] = product(scaled, back[...].astype(f32).astype(bf16), 3)
+
+    edge_diag[...] = short_product(diag[...], touch.at[:, elems:])
+    hits = jnp.sum(hit, axis=0, keepdims=True)
     row = lax.broadcasted_iota(jnp.int32, (8, nodes), 0)
-    diag[...] = jnp.where(row == 3, 1.0 - 0.5 * hits[:8], sums)
-    edge_diag[...] = product(sums, at_iface, 3)
-    counts = jnp.dot(from_iface[...], touch[...], preferred_element_type=f32)
-    edge_touch[...] = counts.astype(bf16)
-    edge_back[...] = counts.T.astype(bf16)
+    diag[...] = jnp.where(row == 3, 1.0 - 0.5 * hits, diag[...])
     for copy in sent:
         copy.wait()
 
@@ -414,7 +420,6 @@
     tables = (
         shape(nodes, elems + shared, kind=f8),
         shape(elems, nodes, kind=f8),
-        shape(nodes, shared, kind=bf16),
         shape(shared, nodes, kind=bf16),
         shape(8, nodes),
         shape(8, elems),
@@ -426,11 +431,9 @@
     built = pl.pallas_call(
         mesh_kernel,
         in_specs=[in_hbm] * 5,
-        out_specs=(in_hbm, in_hbm, *[in_vmem] * 7),
+        out_specs=(in_hbm, in_hbm, *[in_vmem] * 6),
         out_shape=tables,
         scratch_shapes=[
-            pltpu.VMEM((nodes, elems), bf16),
-            pltpu.VMEM((elems, nodes), bf16),
             pltpu.VMEM((nodes, elems + shared), f8),
             pltpu.VMEM((elems, nodes), f8),
             pltpu.VMEM(elem_nodes.shape, jnp.int32),
@@ -445,7 +448,7 @@
         name="incidence",
         cost_estimate=pl.CostEstimate(flops=2**31, bytes_accessed=2**23, transcendentals=0),
     )(elem_nodes, mass, radial, stiff, iface)
-    touch, back, at_iface, from_iface, diag, coefs, edge_touch, edge_back, edge_diag = built
+    touch, back, from_iface, diag, coefs, edge_touch, edge_back, edge_diag = built
     if block % 128:
         forcing = forcing.transpose(1, 0, 2).reshape(1, rows, nodes)
 

time: 41.3 us -> 41.2 us (level)
  Pallas kernels: 15.9 us -> 14.5 us
  waiting for transfers between devices: 4.34 us -> 5.65 us
    pallas_call x1, Pallas kernels: 7.21 us -> 5.9 us  [per_device(): pl.pallas_call(mesh_kernel, in_specs=[in_hbm] * 5, out_specs=(in_hbm, in_...]
    all_to_all x1, waiting for transfers between devices: 0.54 us -> 1.85 us  [per_device(): forcing = lax.all_to_all(terms, 'mode', 0, 0, tiled=True)]
  transfers between devices with their start and end apart: 11 -> 11, of which waited for: 5 -> 5; matrix products, arithmetic and copies ran while one was open for 0% -> 0% of each run, Pallas kernels for 23% -> 20%
where the time goes in v9:
time: 41.2 us; the launch traced here: 40.8 us
  starting transfers between devices  19.9 us (48%)
  Pallas kernels  14.5 us (35%)
  waiting for transfers between devices  5.65 us (14%)
  between operations  0.77 us (2%)
    ppermute x7, starting transfers between devices, per_device(): lax.ppermute(blocks[d], 'mode', [(i, (i + d) % owners) for i in range(own...  13.8 us
    pallas_call x1, Pallas kernels, per_device(): pl.pallas_call(mesh_kernel, in_specs=[in_hbm] * 5, out_specs=(in_hbm, in_...  5.9 us
    all_to_all x1, starting transfers between devices, per_device(): forcing = lax.all_to_all(terms, 'mode', 0, 0, tiled=True)  5.41 us
    ppermute x7, waiting for transfers between devices, per_device(): lax.ppermute(blocks[d], 'mode', [(i, (i + d) % owners) for i in range(own...  2.66 us
    pallas_call x1, Pallas kernels, per_device(): pl.pallas_call(rhs_edge_kernel, in_specs=[in_vmem] + [in_hbm] * 4, out_sh...  2.23 us
    all_to_all x1, waiting for transfers between devices, per_device(): forcing = lax.all_to_all(terms, 'mode', 0, 0, tiled=True)  1.85 us
    pallas_call x1, Pallas kernels, per_device(): call(image_kernel, 'image', (full, full, part), 2 ** 30)  1.24 us
    pallas_call x1, Pallas kernels, per_device(): call(rhs_kernel, 'rhs', (full, part, small_row), 2 ** 30)  1.14 us
  transfers between devices with their start and end apart: 11, of which 5 were waited for; matrix products, arithmetic and copies ran while one was open for 0% of the time, Pallas kernels for 20%

profile of v9, /device:TPU:0, one launch (start us, length us, event | category | flops | bytes accessed | tf_op | source)
XLA Modules:
  0.0 40.8 jit_solution(7573835100546822764)
XLA Ops:
  0.6 1.1 %pack.1 = (f32[48,256]{1,0:T(8,128)S(1)}, f32[48,256]{1,0:T(8,128)S(1)}, f32[48,256]{1,0:T(8,128)S(1)}, f32[48,256]{1,0:T(8,128)S(1)}, f32[48,256]{1,0:T(8,128)S...) custom-call(f32[3,2,2,2048]{3,2,1,0:T(2,128)} %vel.1, ...), custom_call_target="tpu_custom_call" | custom-call | tf_op jit(solution)/shard_map/pack/pallas_call | solution.py:388
  1.8 3.0 %collective-permute-start = (f32[48,256]{1,0:T(8,128)S(1)}, f32[48,256]{1,0:T(8,128)S(1)}, u32[]{:S(2)}, u32[]{:S(2)}) collective-permute-start(f32[48,256]{1,0:T(8,128)S(1)} %get-tuple-element.39), channel_id=1, source_target_pairs={{0,2},{2,4},{4,6},{6,8},{8,10},{10,12},{12,14},{14,0},{1,3},{3,5},... | collective-permute-start | bytes 147464 | tf_op jit(solution)/shard_map/ppermute | solution.py:398
  4.8 1.6 %collective-permute-start.1 = (f32[48,256]{1,0:T(8,128)S(1)}, f32[48,256]{1,0:T(8,128)S(1)}, u32[]{:S(2)}, u32[]{:S(2)}) collective-permute-start(f32[48,256]{1,0:T(8,128)S(1)} %get-tuple-element.40), channel_id=1, source_target_pairs={{0,4},{2,6},{4,8},{6,10},{8,12},{10,14},{12,0},{14,2},{1,5},{3,7},... | collective-permute-start | bytes 147464 | tf_op jit(solution)/shard_map/ppermute | solution.py:398
  6.3 2.6 %collective-permute-start.2 = (f32[48,256]{1,0:T(8,128)S(1)}, f32[48,256]{1,0:T(8,128)S(1)}, u32[]{:S(2)}, u32[]{:S(2)}) collective-permute-start(f32[48,256]{1,0:T(8,128)S(1)} %get-tuple-element.41), channel_id=1, source_target_pairs={{0,6},{2,8},{4,10},{6,12},{8,14},{10,0},{12,2},{14,4},{1,7},{3,9},... | collective-permute-start | bytes 147464 | tf_op jit(solution)/shard_map/ppermute | solution.py:398
  8.9 1.2 %collective-permute-start.3 = (f32[48,256]{1,0:T(8,128)S(1)}, f32[48,256]{1,0:T(8,128)S(1)}, u32[]{:S(2)}, u32[]{:S(2)}) collective-permute-start(f32[48,256]{1,0:T(8,128)S(1)} %get-tuple-element.42), channel_id=1, source_target_pairs={{0,8},{2,10},{4,12},{6,14},{8,0},{10,2},{12,4},{14,6},{1,9},{3,11}... | collective-permute-start | bytes 147464 | tf_op jit(solution)/shard_map/ppermute | solution.py:398
  10.1 2.6 %collective-permute-start.4 = (f32[48,256]{1,0:T(8,128)S(1)}, f32[48,256]{1,0:T(8,128)S(1)}, u32[]{:S(2)}, u32[]{:S(2)}) collective-permute-start(f32[48,256]{1,0:T(8,128)S(1)} %get-tuple-element.43), channel_id=1, source_target_pairs={{0,10},{2,12},{4,14},{6,0},{8,2},{10,4},{12,6},{14,8},{1,11},{3,13... | collective-permute-start | bytes 147464 | tf_op jit(solution)/shard_map/ppermute | solution.py:398
  12.8 0.0 collective-permute-done.refs_1_
  12.8 1.3 %collective-permute-start.5 = (f32[48,256]{1,0:T(8,128)S(1)}, f32[48,256]{1,0:T(8,128)S(1)}, u32[]{:S(2)}, u32[]{:S(2)}) collective-permute-start(f32[48,256]{1,0:T(8,128)S(1)} %get-tuple-element.44), channel_id=1, source_target_pairs={{0,12},{2,14},{4,0},{6,2},{8,4},{10,6},{12,8},{14,10},{1,13},{3,15... | collective-permute-start | bytes 147464 | tf_op jit(solution)/shard_map/ppermute | solution.py:398
  14.1 0.0 collective-permute-done.1.refs_2_
  14.1 1.4 %collective-permute-start.6 = (f32[48,256]{1,0:T(8,128)S(1)}, f32[48,256]{1,0:T(8,128)S(1)}, u32[]{:S(2)}, u32[]{:S(2)}) collective-permute-start(f32[48,256]{1,0:T(8,128)S(1)} %get-tuple-element.45), channel_id=1, source_target_pairs={{0,14},{2,0},{4,2},{6,4},{8,6},{10,8},{12,10},{14,12},{1,15},{3,1}... | collective-permute-start | bytes 147464 | tf_op jit(solution)/shard_map/ppermute | solution.py:398
  15.5 0.0 collective-permute-done.2.refs_3_
  15.5 0.0 collective-permute-done.3.refs_4_
  15.5 0.3 collective-permute-done.4.refs_5_
  15.9 1.4 %collective-permute-done.5.refs_6_ = f32[48,256]{1,0:T(8,128)S(1)} collective-permute-done((f32[48,256]{1,0:T(8,128)S(1)}, f32[48,256]{1,0:T(8,128)S(1)}, u32[]{:S(2)}, u32[]{:S(2)}) %collective-permute-start.5) | collective-permute-done | bytes 49184 | tf_op jit(solution)/shard_map/ppermute | solution.py:398
  17.2 1.0 %collective-permute-done.6.refs_7_ = f32[48,256]{1,0:T(8,128)S(1)} collective-permute-done((f32[48,256]{1,0:T(8,128)S(1)}, f32[48,256]{1,0:T(8,128)S(1)}, u32[]{:S(2)}, u32[]{:S(2)}) %collective-permute-start.6) | collective-permute-done | bytes 49184 | tf_op jit(solution)/shard_map/ppermute | solution.py:398
  18.2 1.1 %nonlinear.1 = f32[8,24,256]{2,1,0:T(8,128)} custom-call(f32[48,256]{1,0:T(8,128)S(1)} %get-tuple-element.38.refs_0_, f32[48,256]{1,0:T(8,128)S(1)} %collective-permute-done.refs_1_, f32[48,256]{1,0:T(8,128)S(1)} %collective-permute-done.1.refs_2_, f32[48,256]{1,0:T(8,128)S(1)} %collective-permute-done.2.refs_3_, ...), custom_call_target="tpu_custom_call" | custom-call | flops 8589934592 | bytes 16777216 | tf_op jit(solution)/shard_map/nonlinear/pallas_call | solution.py:399
  19.3 5.4 %all-to-all-start = ((f32[8,24,256]{2,1,0:T(8,128)}), f32[8,24,256]{2,1,0:T(8,128)S(1)}, u32[]{:S(2)}, u32[]{:S(2)}) async-start(f32[8,24,256]{2,1,0:T(8,128)} %nonlinear.1), calls=%async_computation | async-start | bytes 393216 | tf_op jit(solution)/shard_map/all_to_all | solution.py:419
  24.7 5.9 %incidence.1 = (f8e4m3fn[2048,1152]{1,0:T(32,128)(4,1)}, f8e4m3fn[1024,2048]{1,0:T(32,128)(4,1)}, bf16[128,2048]{1,0:T(8,128)(2,1)}, f32[8,2048]{1,0:T(8,128)}, ...) custom-call(s32[6,1024]{1,0:T(8,128)} %nodes_hbm, ...), custom_call_target="tpu_custom_call" | custom-call | flops 2147483648 | bytes 8388608 | tf_op jit(solution)/shard_map/incidence/pallas_call | solution.py:431
  30.7 0.0 copy-start
  30.7 0.0 copy-start.3
  30.7 1.9 %all-to-all-done.forcing = f32[8,24,256]{2,1,0:T(8,128)S(1)} async-done(((f32[8,24,256]{2,1,0:T(8,128)}), f32[8,24,256]{2,1,0:T(8,128)S(1)}, u32[]{:S(2)}, u32[]{:S(2)}) %all-to-all-start) | async-done | bytes 196640 | tf_op jit(solution)/shard_map/all_to_all | solution.py:419
  32.5 2.2 %rhs_edge.1 = (f32[24,1024]{1,0:T(8,128)S(1)}, f32[24,128]{1,0:T(8,128)S(1)}, f8e4m3fn[2048,1152]{1,0:T(32,128)(4,1)S(1)}, bf16[1024,128]{1,0:T(8,128)(2,1)S(1)}...) custom-call(f32[8,24,256]{2,1,0:T(8,128)S(1)} %all-to-all-done.forcing, ...), custom_call_target="tpu_custom_call" | custom-call | tf_op jit(solution)/shard_map/rhs_edge/pallas_call | solution.py:470
  34.8 0.1 collective-permute-start.7
  34.8 0.0 copy-done
  34.9 0.0 copy-done.3
  34.9 0.0 copy-start.2
  34.9 0.0 copy-start.1
  34.9 1.1 %rhs.1 = (f32[24,2048]{1,0:T(8,128)S(1)}, f32[24,1024]{1,0:T(8,128)S(1)}, f32[24,128]{1,0:T(8,128)S(1)}) custom-call(f32[8,24,256]{2,1,0:T(8,128)S(1)} %all-to-all-done.forcing, f32[24,1024]{1,0:T(8,128)S(1)} %get-tuple-element.55.spread, f8e4m3fn[2048,1152]{1,0:T(32,128)(4,1)S(1)} %get-tuple-element.56.touch, f8e4m3fn[1024,2048]{1,0:T(32,128)(4,1)S(1)} %copy-done, ...), custom_call_target="tpu_custom_call" | custom-call | flops 1073741824 | bytes 2097152 | tf_op jit(solution)/shard_map/rhs/pallas_call | solution.py:479
  36.0 0.0 collective-permute-done.7.edge
  36.0 0.0 copy-done.2
  36.1 0.4 image_edge.1
  36.4 0.5 %collective-permute-start.8 = (f32[24,256]{1,0:T(8,128)S(1)}, f32[24,256]{1,0:T(8,128)S(1)}, u32[]{:S(2)}, u32[]{:S(2)}) collective-permute-start(f32[24,256]{1,0:T(8,128)S(1)} %get-tuple-element.65.own), channel_id=1, source_target_pairs={{0,1},{1,0},{2,3},{3,2},{4,5},{5,4},{6,7},{7,6},{8,9},{9,8},{10,11... | collective-permute-start | bytes 73736 | tf_op jit(solution)/shard_map/ppermute | solution.py:456
  37.0 0.0 copy-done.1
  37.0 1.2 %image.1 = (f32[24,2048]{1,0:T(8,128)S(1)}, f32[24,2048]{1,0:T(8,128)S(1)}, f32[24,1024]{1,0:T(8,128)S(1)}) custom-call(f32[24,2048]{1,0:T(8,128)S(1)} %get-tuple-element.66.local, f32[24,128]{1,0:T(8,128)S(1)} %collective-permute-done.7.edge, f32[24,1024]{1,0:T(8,128)S(1)} %get-tuple-element.67.sums, f8e4m3fn[2048,1152]{1,0:T(32,128)(4,1)S(1)} %get-tuple-element.56.touch, ...), custom_call_target="tpu_custom_call" | custom-call | flops 1073741824 | bytes 2097152 | tf_op jit(solution)/shard_map/image/pallas_call | solution.py:486
  38.2 0.0 collective-permute-done.8.edge
  38.2 0.4 resid.1
  38.6 0.1 collective-permute-start.9
  38.7 1.1 %collective-permute-done.9.norms = f32[24,128]{1,0:T(8,128)S(1)} collective-permute-done((f32[24,128]{1,0:T(8,128)S(1)}, f32[24,128]{1,0:T(8,128)S(1)}, u32[]{:S(2)}, u32[]{:S(2)}) %collective-permute-start.9) | collective-permute-done | bytes 12320 | tf_op jit(solution)/shard_map/ppermute | solution.py:456
  39.9 1.0 %last.1 = (f32[3,2,2,2048]{3,2,1,0:T(2,128)}, f32[3,2,2,2048]{3,2,1,0:T(2,128)}) custom-call(f32[24,256]{1,0:T(8,128)S(1)} %collective-permute-done.8.edge, f32[24,256]{1,0:T(8,128)S(1)} %get-tuple-element.65.own, f32[24,128]{1,0:T(8,128)S(1)} %get-tuple-element.72.norms_own, f32[24,128]{1,0:T(8,128)S(1)} %collective-permute-done.9.norms, ...), custom_call_target="tpu_custom_call" | custom-call | tf_op jit(solution)/shard_map/last/pallas_call | solution.py:493
Async XLA Ops:
  1.8 11.0 %collective-permute-start = (f32[48,256]{1,0:T(8,128)S(1)}, f32[48,256]{1,0:T(8,128)S(1)}, u32[]{:S(2)}, u32[]{:S(2)}) collective-permute-start(f32[48,256]{1,0:T(8,128)S(1)} %get-tuple-element.39), channel_id=1, source_target_pairs={{0,2},{2,4},{4,6},{6,8},{8,10},{10,12},{12,14},{14,0},{1,3},{3,5},... | collective-permute-start | bytes 147464 | tf_op jit(solution)/shard_map/ppermute | solution.py:398
  4.8 9.3 %collective-permute-start.1 = (f32[48,256]{1,0:T(8,128)S(1)}, f32[48,256]{1,0:T(8,128)S(1)}, u32[]{:S(2)}, u32[]{:S(2)}) collective-permute-start(f32[48,256]{1,0:T(8,128)S(1)} %get-tuple-element.40), channel_id=1, source_target_pairs={{0,4},{2,6},{4,8},{6,10},{8,12},{10,14},{12,0},{14,2},{1,5},{3,7},... | collective-permute-start | bytes 147464 | tf_op jit(solution)/shard_map/ppermute | solution.py:398
  6.3 9.2 %collective-permute-start.2 = (f32[48,256]{1,0:T(8,128)S(1)}, f32[48,256]{1,0:T(8,128)S(1)}, u32[]{:S(2)}, u32[]{:S(2)}) collective-permute-start(f32[48,256]{1,0:T(8,128)S(1)} %get-tuple-element.41), channel_id=1, source_target_pairs={{0,6},{2,8},{4,10},{6,12},{8,14},{10,0},{12,2},{14,4},{1,7},{3,9},... | collective-permute-start | bytes 147464 | tf_op jit(solution)/shard_map/ppermute | solution.py:398
  8.9 6.6 %collective-permute-start.3 = (f32[48,256]{1,0:T(8,128)S(1)}, f32[48,256]{1,0:T(8,128)S(1)}, u32[]{:S(2)}, u32[]{:S(2)}) collective-permute-start(f32[48,256]{1,0:T(8,128)S(1)} %get-tuple-element.42), channel_id=1, source_target_pairs={{0,8},{2,10},{4,12},{6,14},{8,0},{10,2},{12,4},{14,6},{1,9},{3,11}... | collective-permute-start | bytes 147464 | tf_op jit(solution)/shard_map/ppermute | solution.py:398
  10.1 5.7 %collective-permute-start.4 = (f32[48,256]{1,0:T(8,128)S(1)}, f32[48,256]{1,0:T(8,128)S(1)}, u32[]{:S(2)}, u32[]{:S(2)}) collective-permute-start(f32[48,256]{1,0:T(8,128)S(1)} %get-tuple-element.43), channel_id=1, source_target_pairs={{0,10},{2,12},{4,14},{6,0},{8,2},{10,4},{12,6},{14,8},{1,11},{3,13... | collective-permute-start | bytes 147464 | tf_op jit(solution)/shard_map/ppermute | solution.py:398
  12.8 4.5 %collective-permute-start.5 = (f32[48,256]{1,0:T(8,128)S(1)}, f32[48,256]{1,0:T(8,128)S(1)}, u32[]{:S(2)}, u32[]{:S(2)}) collective-permute-start(f32[48,256]{1,0:T(8,128)S(1)} %get-tuple-element.44), channel_id=1, source_target_pairs={{0,12},{2,14},{4,0},{6,2},{8,4},{10,6},{12,8},{14,10},{1,13},{3,15... | collective-permute-start | bytes 147464 | tf_op jit(solution)/shard_map/ppermute | solution.py:398
  14.1 4.1 %collective-permute-start.6 = (f32[48,256]{1,0:T(8,128)S(1)}, f32[48,256]{1,0:T(8,128)S(1)}, u32[]{:S(2)}, u32[]{:S(2)}) collective-permute-start(f32[48,256]{1,0:T(8,128)S(1)} %get-tuple-element.45), channel_id=1, source_target_pairs={{0,14},{2,0},{4,2},{6,4},{8,6},{10,8},{12,10},{14,12},{1,15},{3,1}... | collective-permute-start | bytes 147464 | tf_op jit(solution)/shard_map/ppermute | solution.py:398
  19.3 13.2 %all-to-all-start = ((f32[8,24,256]{2,1,0:T(8,128)}), f32[8,24,256]{2,1,0:T(8,128)S(1)}, u32[]{:S(2)}, u32[]{:S(2)}) async-start(f32[8,24,256]{2,1,0:T(8,128)} %nonlinear.1), calls=%async_computation | async-start | bytes 393216 | tf_op jit(solution)/shard_map/all_to_all | solution.py:419
  30.7 4.2 %copy-start = (f8e4m3fn[1024,2048]{1,0:T(32,128)(4,1)S(1)}, f8e4m3fn[1024,2048]{1,0:T(32,128)(4,1)}, u32[]{:S(2)}) copy-start(f8e4m3fn[1024,2048]{1,0:T(32,128)(4,1)} %get-tuple-element.57.back) | copy-start | bytes 6291460
  30.7 4.2 %copy-start.3 = (f32[8,2048]{1,0:T(8,128)S(1)}, f32[8,2048]{1,0:T(8,128)}, u32[]{:S(2)}) copy-start(f32[8,2048]{1,0:T(8,128)} %get-tuple-element.58.diag) | copy-start | bytes 196612
  34.8 1.3 %collective-permute-start.7 = (f32[24,128]{1,0:T(8,128)S(1)}, f32[24,128]{1,0:T(8,128)S(1)}, u32[]{:S(2)}, u32[]{:S(2)}) collective-permute-start(f32[24,128]{1,0:T(8,128)S(1)} %get-tuple-element.54.edge_own), channel_id=1, source_target_pairs={{0,1},{1,0},{2,3},{3,2},{4,5},{5,4},{6,7},{7,6},{8,9},{9,8},{10,11... | collective-permute-start | bytes 36872 | tf_op jit(solution)/shard_map/ppermute | solution.py:456
  34.9 1.2 %copy-start.2 = (bf16[128,1024]{1,0:T(8,128)(2,1)S(1)}, bf16[128,1024]{1,0:T(8,128)(2,1)}, u32[]{:S(2)}) copy-start(bf16[128,1024]{1,0:T(8,128)(2,1)} %get-tuple-element.61.edge_touch) | copy-start | bytes 786436
  34.9 2.1 %copy-start.1 = (bf16[128,2048]{1,0:T(8,128)(2,1)S(1)}, bf16[128,2048]{1,0:T(8,128)(2,1)}, u32[]{:S(2)}) copy-start(bf16[128,2048]{1,0:T(8,128)(2,1)} %get-tuple-element.68.from_iface) | copy-start | bytes 1572868
  36.4 1.8 %collective-permute-start.8 = (f32[24,256]{1,0:T(8,128)S(1)}, f32[24,256]{1,0:T(8,128)S(1)}, u32[]{:S(2)}, u32[]{:S(2)}) collective-permute-start(f32[24,256]{1,0:T(8,128)S(1)} %get-tuple-element.65.own), channel_id=1, source_target_pairs={{0,1},{1,0},{2,3},{3,2},{4,5},{5,4},{6,7},{7,6},{8,9},{9,8},{10,11... | collective-permute-start | bytes 73736 | tf_op jit(solution)/shard_map/ppermute | solution.py:456
  38.6 1.2 %collective-permute-start.9 = (f32[24,128]{1,0:T(8,128)S(1)}, f32[24,128]{1,0:T(8,128)S(1)}, u32[]{:S(2)}, u32[]{:S(2)}) collective-permute-start(f32[24,128]{1,0:T(8,128)S(1)} %get-tuple-element.72.norms_own), channel_id=1, source_target_pairs={{0,1},{1,0},{2,3},{3,2},{4,5},{5,4},{6,7},{7,6},{8,9},{9,8},{10,11... | collective-permute-start | bytes 36872 | tf_op jit(solution)/shard_map/ppermute | solution.py:456

commit v10 on v9

--- a/solution.py
+++ b/solution.py
@@ -173,7 +173,7 @@
             out[j, span, :] = fields[j, span, :] + coef[j * pair : (j + 1) * pair]
 
 
-def mesh_kernel(nodes_hbm, mass_hbm, radial_hbm, stiff_hbm, iface_hbm, touch_out, back_out, from_iface, diag, coefs, edge_touch, edge_back, edge_diag, touch, back, elem_nodes, mass, radial, stiff, iface, in_sems, out_sems):
+def mesh_kernel(nodes_hbm, mass_hbm, radial_hbm, stiff_hbm, iface_hbm, touch, back, from_iface, diag, coefs, edge_touch, edge_back, edge_diag, elem_nodes, mass, radial, stiff, iface, in_sems):
     loads = start_all(
         (nodes_hbm, mass_hbm, radial_hbm, stiff_hbm, iface_hbm), (elem_nodes, mass, radial, stiff, iface), in_sems
     )
@@ -184,12 +184,6 @@
     fields = 8
     words = nodes // fields
     width = math.gcd(elems, 256)
-    sent = []
-
-    def send(source, target):
-        sent.append(pltpu.make_async_copy(source, target, out_sems.at[len(sent)]))
-        sent[-1].start()
-
     for c in range(elems // width):
         span = slice(c * width, (c + 1) * width)
         word = lax.broadcasted_iota(jnp.int32, (words, width), 0)
@@ -203,13 +197,9 @@
             count = (jnp.right_shift(total, 4 * q) & 15).astype(f32)
             touch[q * words : (q + 1) * words, span] = count.astype(f8)
             back[span, q * words : (q + 1) * words] = count.T.astype(f8)
-        column = pl.ds(c * width, width)
-        send(touch.at[:, column], touch_out.at[:, column])
-        send(back.at[column, :], back_out.at[column, :])
     node = lax.broadcasted_iota(jnp.int32, (nodes, shared), 0)
     hit = jnp.where(iface[...] == node, 1.0, 0.0)
     touch[:, elems:] = hit.astype(f8)
-    send(touch.at[:, pl.ds(elems, shared)], touch_out.at[:, pl.ds(elems, shared)])
     hit = hit.T
     from_iface[...] = hit.astype(bf16)
     counts = jnp.dot(hit.astype(f8), touch[:, :elems], preferred_element_type=f32)
@@ -231,8 +221,6 @@
     hits = jnp.sum(hit, axis=0, keepdims=True)
     row = lax.broadcasted_iota(jnp.int32, (8, nodes), 0)
     diag[...] = jnp.where(row == 3, 1.0 - 0.5 * hits, diag[...])
-    for copy in sent:
-        copy.wait()
 
 
 def row_factors(rows, per_dev, modes):
@@ -270,25 +258,9 @@
     return jnp.concatenate([forcing[b] for b in range(forcing.shape[0])], axis=1)
 
 
-def rhs_edge_kernel(forcing, touch_hbm, back_hbm, diag_hbm, coefs_hbm, spread_out, edge, touch, edge_back, edge_diag, coefs, sems):
-    nodes = touch.shape[0]
+def rhs_edge_kernel(forcing, touch, edge_back, edge_diag, coefs, spread_out, edge):
     elems = coefs.shape[1]
-    width = nodes // 4
-    spans = [pl.ds(i * width, width) for i in range(4)]
-    loads = start_all(
-        [touch_hbm.at[span, :] for span in spans] + [coefs_hbm, back_hbm, diag_hbm],
-        [touch.at[span, :] for span in spans] + [coefs, edge_back, edge_diag],
-        sems,
-    )
-    parts, scale = short_parts(together(forcing))
-    out = 0.0
-    for i in range(4):
-        loads[i].wait()
-        some = parts[:, i * width : (i + 1) * width].astype(f8)
-        out = out + jnp.dot(some, touch[i * width : (i + 1) * width, :], preferred_element_type=f32)
-    sums = short_total(out, scale)
-    for load in loads[4:]:
-        load.wait()
+    sums = short_product(together(forcing), touch)
     spread = sums[:, :elems] * coefs[0:1, :]
     spread_out[...] = spread
     edge[...] = edge_diag[0:1, :] * sums[:, elems:] + product(spread, edge_back, 3)
@@ -384,6 +356,32 @@
         return pltpu.with_memory_space_constraint(array, pltpu.HBM)
 
     nonlinear_cost = pl.CostEstimate(flops=2**33, bytes_accessed=2**24, transcendentals=0)
+    tables = (
+        shape(nodes, elems + shared, kind=f8),
+        shape(elems, nodes, kind=f8),
+        shape(shared, nodes, kind=bf16),
+        shape(8, nodes),
+        shape(8, elems),
+        shape(shared, elems, kind=bf16),
+        shape(elems, shared, kind=bf16),
+        shape(8, shared),
+    )
+    built = pl.pallas_call(
+        mesh_kernel,
+        in_specs=[in_hbm] * 5,
+        out_shape=tuple(pltpu.VMEM(t.shape, t.dtype) for t in tables),
+        scratch_shapes=[
+            pltpu.VMEM(elem_nodes.shape, jnp.int32),
+            pltpu.VMEM((1, elems), f32),
+            pltpu.VMEM((1, elems), f32),
+            pltpu.VMEM((1, elems), f32),
+            pltpu.VMEM(iface.shape, jnp.int32),
+            pltpu.SemaphoreType.DMA((5,)),
+        ],
+        compiler_params=params(),
+        name="incidence",
+        cost_estimate=pl.CostEstimate(flops=2**31, bytes_accessed=2**23, transcendentals=0),
+    )(*(pin(a) for a in (elem_nodes, mass, radial, stiff, iface)))
     if owners <= 8 and block % 128 == 0:
         *blocks, synthesis, analysis = pl.pallas_call(
             ring_pack_kernel,
@@ -396,9 +394,10 @@
         )(*(pin(a) for a in (velocity, magnetic, vorticity, current, synthesis, analysis)))
         for d in range(1, owners):
             blocks[d] = lax.ppermute(blocks[d], "mode", [(i, (i + d) % owners) for i in range(owners)])
+        *blocks, built = lax.optimization_barrier((*blocks, built))
         terms = pl.pallas_call(
             ring_nonlinear_kernel,
-            out_shape=shape(owners, rows, block),
+            out_shape=pltpu.VMEM((owners, rows, block), f32),
             scratch_shapes=[pltpu.VMEM((owners, 2 * rows, block), f32)],
             compiler_params=params(),
             name="nonlinear",
@@ -415,40 +414,8 @@
             name="nonlinear",
             cost_estimate=nonlinear_cost,
         )(lax.all_to_all(packed, "mode", 0, 0, tiled=True), synthesis, analysis)
-    terms, elem_nodes = lax.optimization_barrier((terms, elem_nodes))
+    touch, back, from_iface, diag, coefs, edge_touch, edge_back, edge_diag = built
     forcing = lax.all_to_all(terms, "mode", 0, 0, tiled=True)
-    tables = (
-        shape(nodes, elems + shared, kind=f8),
-        shape(elems, nodes, kind=f8),
-        shape(shared, nodes, kind=bf16),
-        shape(8, nodes),
-        shape(8, elems),
-        shape(shared, elems, kind=bf16),
-        shape(elems, shared, kind=bf16),
-        shape(8, shared),
-    )
-    in_vmem = pl.BlockSpec(memory_space=pltpu.VMEM)
-    built = pl.pallas_call(
-        mesh_kernel,
-        in_specs=[in_hbm] * 5,
-        out_specs=(in_hbm, in_hbm, *[in_vmem] * 6),
-        out_shape=tables,
-        scratch_shapes=[
-            pltpu.VMEM((nodes, elems + shared), f8),
-            pltpu.VMEM((elems, nodes), f8),
-            pltpu.VMEM(elem_nodes.shape, jnp.int32),
-            pltpu.VMEM((1, elems), f32),
-            pltpu.VMEM((1, elems), f32),
-            pltpu.VMEM((1, elems), f32),
-            pltpu.VMEM(iface.shape, jnp.int32),
-            pltpu.SemaphoreType.DMA((5,)),
-            pltpu.SemaphoreType.DMA((2 * elems // math.gcd(elems, 256) + 1,)),
-        ],
-        compiler_params=params(large),
-        name="incidence",
-        cost_estimate=pl.CostEstimate(flops=2**31, bytes_accessed=2**23, transcendentals=0),
-    )(elem_nodes, mass, radial, stiff, iface)
-    touch, back, from_iface, diag, coefs, edge_touch, edge_back, edge_diag = built
     if block % 128:
         forcing = forcing.transpose(1, 0, 2).reshape(1, rows, nodes)
 
@@ -466,15 +433,12 @@
         )
 
     full, part, small_row = shape(rows, nodes), shape(rows, elems), shape(rows, 128)
-    kept = [pltpu.VMEM(a.shape, a.dtype) for a in (touch, edge_back, edge_diag, coefs)]
-    spread, edge_own, touch, edge_back, edge_diag, coefs = pl.pallas_call(
+    spread, edge_own = pl.pallas_call(
         rhs_edge_kernel,
-        in_specs=[in_vmem] + [in_hbm] * 4,
-        out_shape=(part, shape(rows, shared), *kept),
-        scratch_shapes=[pltpu.SemaphoreType.DMA((7,))],
+        out_shape=(part, shape(rows, shared)),
         compiler_params=params(),
         name="rhs_edge",
-    )(forcing, *(pin(a) for a in (touch, edge_back, edge_diag, coefs)))
+    )(forcing, touch, edge_back, edge_diag, coefs)
     edge = swap(edge_own)
     local, sums, inner = call(rhs_kernel, "rhs", (full, part, small_row), 2**30)(
         forcing, spread, touch, back, diag

time: 41.2 us -> 38.6 us (0.937)
  blocking collectives: 0 us -> 11.1 us
  starting transfers between devices: 19.9 us -> 14.5 us
  waiting for transfers between devices: 5.65 us -> 1.19 us
  Pallas kernels: 14.5 us -> 10.9 us
    all_to_all x0 -> x1, blocking collectives: none -> 11.1 us  [per_device(): forcing = lax.all_to_all(terms, 'mode', 0, 0, tiled=True)]
    all_to_all x1 -> x0, starting transfers between devices: 5.41 us -> none  [per_device(): forcing = lax.all_to_all(terms, 'mode', 0, 0, tiled=True)]
    pallas_call x3, Pallas kernels: 9.27 us -> 5.59 us  [the longest x1 4.49 us: per_device(): pl.pallas_call(mesh_kernel, in_specs=[in_hbm] * 5, out_shape=tuple((pltpu...]
    ppermute x7, waiting for transfers between devices: 2.66 us -> 0.02 us  [per_device(): lax.ppermute(blocks[d], 'mode', [(i, (i + d) % owners) for i in range(own...]
    all_to_all x1 -> x0, waiting for transfers between devices: 1.85 us -> none  [per_device(): forcing = lax.all_to_all(terms, 'mode', 0, 0, tiled=True)]
  transfers between devices with their start and end apart: 11 -> 10, of which waited for: 5 -> 1; matrix products, arithmetic and copies ran while one was open for 0% -> 0% of each run, Pallas kernels for 20% -> 18%
where the time goes in v10:
time: 38.6 us; the launch traced here: 38.4 us
  starting transfers between devices  14.5 us (38%)
  blocking collectives  11.1 us (29%)
  Pallas kernels  10.9 us (28%)
  waiting for transfers between devices  1.19 us (3%)
  between operations  0.75 us (2%)
    ppermute x7, starting transfers between devices, per_device(): lax.ppermute(blocks[d], 'mode', [(i, (i + d) % owners) for i in range(own...  13.8 us
    all_to_all x1, blocking collectives, per_device(): forcing = lax.all_to_all(terms, 'mode', 0, 0, tiled=True)  11.1 us
    pallas_call x1, Pallas kernels, per_device(): pl.pallas_call(mesh_kernel, in_specs=[in_hbm] * 5, out_shape=tuple((pltpu...  4.49 us
    pallas_call x1, Pallas kernels, per_device(): call(image_kernel, 'image', (full, full, part), 2 ** 30)  1.24 us
    ppermute x3, waiting for transfers between devices, swap(): return lax.ppermute(array, 'mer', [(0, 1), (1, 0)])  1.17 us
    pallas_call x1, Pallas kernels, per_device(): call(rhs_kernel, 'rhs', (full, part, small_row), 2 ** 30)  1.16 us
    pallas_call x1, Pallas kernels, per_device(): pl.pallas_call(ring_pack_kernel, in_specs=[in_hbm] * 6, out_shape=(pltpu....  1.13 us
    pallas_call x1, Pallas kernels, per_device(): pl.pallas_call(last_kernel, out_shape=(out, out), compiler_params=params(...  0.99 us
  transfers between devices with their start and end apart: 10, of which 1 were waited for; matrix products, arithmetic and copies ran while one was open for 0% of the time, Pallas kernels for 18%

profile of v10, /device:TPU:0, one launch (start us, length us, event | category | flops | bytes accessed | tf_op | source)
XLA Modules:
  0.0 38.4 jit_solution(16347098673496678429)
XLA Ops:
  0.6 1.1 %pack.1 = (f32[48,256]{1,0:T(8,128)S(1)}, f32[48,256]{1,0:T(8,128)S(1)}, f32[48,256]{1,0:T(8,128)S(1)}, f32[48,256]{1,0:T(8,128)S(1)}, f32[48,256]{1,0:T(8,128)S...) custom-call(f32[3,2,2,2048]{3,2,1,0:T(2,128)} %vel.1, ...), custom_call_target="tpu_custom_call" | custom-call | tf_op jit(solution)/shard_map/pack/pallas_call | solution.py:386
  1.8 3.0 %collective-permute-start = (f32[48,256]{1,0:T(8,128)S(1)}, f32[48,256]{1,0:T(8,128)S(1)}, u32[]{:S(2)}, u32[]{:S(2)}) collective-permute-start(f32[48,256]{1,0:T(8,128)S(1)} %get-tuple-element.49), channel_id=1, source_target_pairs={{0,2},{2,4},{4,6},{6,8},{8,10},{10,12},{12,14},{14,0},{1,3},{3,5},... | collective-permute-start | bytes 147464 | tf_op jit(solution)/shard_map/ppermute | solution.py:396
  4.8 1.6 %collective-permute-start.1 = (f32[48,256]{1,0:T(8,128)S(1)}, f32[48,256]{1,0:T(8,128)S(1)}, u32[]{:S(2)}, u32[]{:S(2)}) collective-permute-start(f32[48,256]{1,0:T(8,128)S(1)} %get-tuple-element.50), channel_id=1, source_target_pairs={{0,4},{2,6},{4,8},{6,10},{8,12},{10,14},{12,0},{14,2},{1,5},{3,7},... | collective-permute-start | bytes 147464 | tf_op jit(solution)/shard_map/ppermute | solution.py:396
  6.3 2.6 %collective-permute-start.2 = (f32[48,256]{1,0:T(8,128)S(1)}, f32[48,256]{1,0:T(8,128)S(1)}, u32[]{:S(2)}, u32[]{:S(2)}) collective-permute-start(f32[48,256]{1,0:T(8,128)S(1)} %get-tuple-element.51), channel_id=1, source_target_pairs={{0,6},{2,8},{4,10},{6,12},{8,14},{10,0},{12,2},{14,4},{1,7},{3,9},... | collective-permute-start | bytes 147464 | tf_op jit(solution)/shard_map/ppermute | solution.py:396
  8.9 1.2 %collective-permute-start.3 = (f32[48,256]{1,0:T(8,128)S(1)}, f32[48,256]{1,0:T(8,128)S(1)}, u32[]{:S(2)}, u32[]{:S(2)}) collective-permute-start(f32[48,256]{1,0:T(8,128)S(1)} %get-tuple-element.52), channel_id=1, source_target_pairs={{0,8},{2,10},{4,12},{6,14},{8,0},{10,2},{12,4},{14,6},{1,9},{3,11}... | collective-permute-start | bytes 147464 | tf_op jit(solution)/shard_map/ppermute | solution.py:396
  10.1 2.6 %collective-permute-start.4 = (f32[48,256]{1,0:T(8,128)S(1)}, f32[48,256]{1,0:T(8,128)S(1)}, u32[]{:S(2)}, u32[]{:S(2)}) collective-permute-start(f32[48,256]{1,0:T(8,128)S(1)} %get-tuple-element.53), channel_id=1, source_target_pairs={{0,10},{2,12},{4,14},{6,0},{8,2},{10,4},{12,6},{14,8},{1,11},{3,13... | collective-permute-start | bytes 147464 | tf_op jit(solution)/shard_map/ppermute | solution.py:396
  12.8 0.0 collective-permute-done.refs_1_
  12.8 1.3 %collective-permute-start.5 = (f32[48,256]{1,0:T(8,128)S(1)}, f32[48,256]{1,0:T(8,128)S(1)}, u32[]{:S(2)}, u32[]{:S(2)}) collective-permute-start(f32[48,256]{1,0:T(8,128)S(1)} %get-tuple-element.54), channel_id=1, source_target_pairs={{0,12},{2,14},{4,0},{6,2},{8,4},{10,6},{12,8},{14,10},{1,13},{3,15... | collective-permute-start | bytes 147464 | tf_op jit(solution)/shard_map/ppermute | solution.py:396
  14.1 0.0 collective-permute-done.1.refs_2_
  14.1 1.4 %collective-permute-start.6 = (f32[48,256]{1,0:T(8,128)S(1)}, f32[48,256]{1,0:T(8,128)S(1)}, u32[]{:S(2)}, u32[]{:S(2)}) collective-permute-start(f32[48,256]{1,0:T(8,128)S(1)} %get-tuple-element.55), channel_id=1, source_target_pairs={{0,14},{2,0},{4,2},{6,4},{8,6},{10,8},{12,10},{14,12},{1,15},{3,1}... | collective-permute-start | bytes 147464 | tf_op jit(solution)/shard_map/ppermute | solution.py:396
  15.5 4.5 %incidence.1 = (f8e4m3fn[2048,1152]{1,0:T(32,128)(4,1)S(1)}, f8e4m3fn[1024,2048]{1,0:T(32,128)(4,1)S(1)}, bf16[128,2048]{1,0:T(8,128)(2,1)S(1)}, f32[8,2048]{1,0...) custom-call(s32[6,1024]{1,0:T(8,128)} %nodes_hbm.1, ...), custom_call_target="tpu_custom_call" | custom-call | flops 2147483648 | bytes 8388608 | tf_op jit(solution)/shard_map/incidence/pallas_call | solution.py:369
  20.0 0.0 collective-permute-done.2.refs_3_
  20.0 0.0 collective-permute-done.3.refs_4_
  20.1 0.0 collective-permute-done.4.refs_5_
  20.1 0.0 collective-permute-done.5.refs_6_
  20.1 0.0 collective-permute-done.6.refs_7_
  20.1 0.5 %nonlinear.1 = f32[8,24,256]{2,1,0:T(8,128)S(1)} custom-call(f32[48,256]{1,0:T(8,128)S(1)} %get-tuple-element.64.refs_0_, f32[48,256]{1,0:T(8,128)S(1)} %collective-permute-done.refs_1_, f32[48,256]{1,0:T(8,128)S(1)} %collective-permute-done.1.refs_2_, f32[48,256]{1,0:T(8,128)S(1)} %collective-permute-done.2.refs_3_, ...), custom_call_target="tpu_custom_call" | custom-call | flops 8589934592 | bytes 16777216 | tf_op jit(solution)/shard_map/nonlinear/pallas_call | solution.py:398
  20.5 11.1 %all_to_all.5.forcing = f32[8,24,256]{2,1,0:T(8,128)S(1)} all-to-all(f32[8,24,256]{2,1,0:T(8,128)S(1)} %nonlinear.1), channel_id=1, replica_groups=mesh['runs'=2,'mode'=8,'mer'=2] {'mode'}, dimensions={0} | all-to-all | bytes 393216 | tf_op jit(solution)/shard_map/all_to_all | solution.py:418
  31.6 0.6 %rhs_edge.1 = (f32[24,1024]{1,0:T(8,128)S(1)}, f32[24,128]{1,0:T(8,128)S(1)}) custom-call(f32[8,24,256]{2,1,0:T(8,128)S(1)} %all_to_all.5.forcing, f8e4m3fn[2048,1152]{1,0:T(32,128)(4,1)S(1)} %get-tuple-element.74.touch, bf16[1024,128]{1,0:T(8,128)(2,1)S(1)} %get-tuple-element.75.edge_back, f32[8,128]{1,0:T(8,128)S(1)} %get-tuple-element.76.edge_diag, ...), custom_call_target="tpu_custom_call" | custom-call | tf_op jit(solution)/shard_map/rhs_edge/pallas_call | solution.py:436
  32.3 0.1 collective-permute-start.7
  32.4 1.2 %rhs.1 = (f32[24,2048]{1,0:T(8,128)S(1)}, f32[24,1024]{1,0:T(8,128)S(1)}, f32[24,128]{1,0:T(8,128)S(1)}) custom-call(f32[8,24,256]{2,1,0:T(8,128)S(1)} %all_to_all.5.forcing, f32[24,1024]{1,0:T(8,128)S(1)} %get-tuple-element.79.spread, f8e4m3fn[2048,1152]{1,0:T(32,128)(4,1)S(1)} %get-tuple-element.74.touch, ...), custom_call_target="tpu_custom_call" | custom-call | flops 1073741824 | bytes 2097152 | tf_op jit(solution)/shard_map/rhs/pallas_call | solution.py:443
  33.5 0.0 collective-permute-done.7.edge
  33.5 0.4 image_edge.1
  33.9 0.6 %collective-permute-start.8 = (f32[24,256]{1,0:T(8,128)S(1)}, f32[24,256]{1,0:T(8,128)S(1)}, u32[]{:S(2)}, u32[]{:S(2)}) collective-permute-start(f32[24,256]{1,0:T(8,128)S(1)} %get-tuple-element.85.own), channel_id=1, source_target_pairs={{0,1},{1,0},{2,3},{3,2},{4,5},{5,4},{6,7},{7,6},{8,9},{9,8},{10,11... | collective-permute-start | bytes 73736 | tf_op jit(solution)/shard_map/ppermute | solution.py:423
  34.5 1.2 %image.1 = (f32[24,2048]{1,0:T(8,128)S(1)}, f32[24,2048]{1,0:T(8,128)S(1)}, f32[24,1024]{1,0:T(8,128)S(1)}) custom-call(f32[24,2048]{1,0:T(8,128)S(1)} %get-tuple-element.86.local, f32[24,128]{1,0:T(8,128)S(1)} %collective-permute-done.7.edge, f32[24,1024]{1,0:T(8,128)S(1)} %get-tuple-element.87.sums, f8e4m3fn[2048,1152]{1,0:T(32,128)(4,1)S(1)} %get-tuple-element.74.touch, ...), custom_call_target="tpu_custom_call" | custom-call | flops 1073741824 | bytes 2097152 | tf_op jit(solution)/shard_map/image/pallas_call | solution.py:450
  35.7 0.0 collective-permute-done.8.edge
  35.7 0.4 %resid.1 = (f32[24,2048]{1,0:T(8,128)S(1)}, f32[24,128]{1,0:T(8,128)S(1)}) custom-call(f32[24,256]{1,0:T(8,128)S(1)} %get-tuple-element.85.own, f32[24,256]{1,0:T(8,128)S(1)} %collective-permute-done.8.edge, f32[24,2048]{1,0:T(8,128)S(1)} %get-tuple-element.89.rhs, f32[24,2048]{1,0:T(8,128)S(1)} %get-tuple-element.90.image, ...), custom_call_target="tpu_custom_call" | custom-call | tf_op jit(solution)/shard_map/resid/pallas_call | solution.py:453
  36.1 0.1 collective-permute-start.9
  36.2 1.2 %collective-permute-done.9.norms = f32[24,128]{1,0:T(8,128)S(1)} collective-permute-done((f32[24,128]{1,0:T(8,128)S(1)}, f32[24,128]{1,0:T(8,128)S(1)}, u32[]{:S(2)}, u32[]{:S(2)}) %collective-permute-start.9) | collective-permute-done | bytes 12320 | tf_op jit(solution)/shard_map/ppermute | solution.py:423
  37.4 1.0 %last.1 = (f32[3,2,2,2048]{3,2,1,0:T(2,128)}, f32[3,2,2,2048]{3,2,1,0:T(2,128)}) custom-call(f32[24,256]{1,0:T(8,128)S(1)} %collective-permute-done.8.edge, f32[24,256]{1,0:T(8,128)S(1)} %get-tuple-element.85.own, f32[24,128]{1,0:T(8,128)S(1)} %get-tuple-element.92.norms_own, f32[24,128]{1,0:T(8,128)S(1)} %collective-permute-done.9.norms, ...), custom_call_target="tpu_custom_call" | custom-call | tf_op jit(solution)/shard_map/last/pallas_call | solution.py:457
Async XLA Ops:
  1.8 11.0 %collective-permute-start = (f32[48,256]{1,0:T(8,128)S(1)}, f32[48,256]{1,0:T(8,128)S(1)}, u32[]{:S(2)}, u32[]{:S(2)}) collective-permute-start(f32[48,256]{1,0:T(8,128)S(1)} %get-tuple-element.49), channel_id=1, source_target_pairs={{0,2},{2,4},{4,6},{6,8},{8,10},{10,12},{12,14},{14,0},{1,3},{3,5},... | collective-permute-start | bytes 147464 | tf_op jit(solution)/shard_map/ppermute | solution.py:396
  4.8 9.3 %collective-permute-start.1 = (f32[48,256]{1,0:T(8,128)S(1)}, f32[48,256]{1,0:T(8,128)S(1)}, u32[]{:S(2)}, u32[]{:S(2)}) collective-permute-start(f32[48,256]{1,0:T(8,128)S(1)} %get-tuple-element.50), channel_id=1, source_target_pairs={{0,4},{2,6},{4,8},{6,10},{8,12},{10,14},{12,0},{14,2},{1,5},{3,7},... | collective-permute-start | bytes 147464 | tf_op jit(solution)/shard_map/ppermute | solution.py:396
  6.3 13.7 %collective-permute-start.2 = (f32[48,256]{1,0:T(8,128)S(1)}, f32[48,256]{1,0:T(8,128)S(1)}, u32[]{:S(2)}, u32[]{:S(2)}) collective-permute-start(f32[48,256]{1,0:T(8,128)S(1)} %get-tuple-element.51), channel_id=1, source_target_pairs={{0,6},{2,8},{4,10},{6,12},{8,14},{10,0},{12,2},{14,4},{1,7},{3,9},... | collective-permute-start | bytes 147464 | tf_op jit(solution)/shard_map/ppermute | solution.py:396
  8.9 11.2 %collective-permute-start.3 = (f32[48,256]{1,0:T(8,128)S(1)}, f32[48,256]{1,0:T(8,128)S(1)}, u32[]{:S(2)}, u32[]{:S(2)}) collective-permute-start(f32[48,256]{1,0:T(8,128)S(1)} %get-tuple-element.52), channel_id=1, source_target_pairs={{0,8},{2,10},{4,12},{6,14},{8,0},{10,2},{12,4},{14,6},{1,9},{3,11}... | collective-permute-start | bytes 147464 | tf_op jit(solution)/shard_map/ppermute | solution.py:396
  10.1 9.9 %collective-permute-start.4 = (f32[48,256]{1,0:T(8,128)S(1)}, f32[48,256]{1,0:T(8,128)S(1)}, u32[]{:S(2)}, u32[]{:S(2)}) collective-permute-start(f32[48,256]{1,0:T(8,128)S(1)} %get-tuple-element.53), channel_id=1, source_target_pairs={{0,10},{2,12},{4,14},{6,0},{8,2},{10,4},{12,6},{14,8},{1,11},{3,13... | collective-permute-start | bytes 147464 | tf_op jit(solution)/shard_map/ppermute | solution.py:396
  12.8 7.3 %collective-permute-start.5 = (f32[48,256]{1,0:T(8,128)S(1)}, f32[48,256]{1,0:T(8,128)S(1)}, u32[]{:S(2)}, u32[]{:S(2)}) collective-permute-start(f32[48,256]{1,0:T(8,128)S(1)} %get-tuple-element.54), channel_id=1, source_target_pairs={{0,12},{2,14},{4,0},{6,2},{8,4},{10,6},{12,8},{14,10},{1,13},{3,15... | collective-permute-start | bytes 147464 | tf_op jit(solution)/shard_map/ppermute | solution.py:396
  14.1 6.0 %collective-permute-start.6 = (f32[48,256]{1,0:T(8,128)S(1)}, f32[48,256]{1,0:T(8,128)S(1)}, u32[]{:S(2)}, u32[]{:S(2)}) collective-permute-start(f32[48,256]{1,0:T(8,128)S(1)} %get-tuple-element.55), channel_id=1, source_target_pairs={{0,14},{2,0},{4,2},{6,4},{8,6},{10,8},{12,10},{14,12},{1,15},{3,1}... | collective-permute-start | bytes 147464 | tf_op jit(solution)/shard_map/ppermute | solution.py:396
  32.3 1.2 %collective-permute-start.7 = (f32[24,128]{1,0:T(8,128)S(1)}, f32[24,128]{1,0:T(8,128)S(1)}, u32[]{:S(2)}, u32[]{:S(2)}) collective-permute-start(f32[24,128]{1,0:T(8,128)S(1)} %get-tuple-element.78.edge_own), channel_id=1, source_target_pairs={{0,1},{1,0},{2,3},{3,2},{4,5},{5,4},{6,7},{7,6},{8,9},{9,8},{10,11... | collective-permute-start | bytes 36872 | tf_op jit(solution)/shard_map/ppermute | solution.py:423
  33.9 1.8 %collective-permute-start.8 = (f32[24,256]{1,0:T(8,128)S(1)}, f32[24,256]{1,0:T(8,128)S(1)}, u32[]{:S(2)}, u32[]{:S(2)}) collective-permute-start(f32[24,256]{1,0:T(8,128)S(1)} %get-tuple-element.85.own), channel_id=1, source_target_pairs={{0,1},{1,0},{2,3},{3,2},{4,5},{5,4},{6,7},{7,6},{8,9},{9,8},{10,11... | collective-permute-start | bytes 73736 | tf_op jit(solution)/shard_map/ppermute | solution.py:423
  36.1 1.2 %collective-permute-start.9 = (f32[24,128]{1,0:T(8,128)S(1)}, f32[24,128]{1,0:T(8,128)S(1)}, u32[]{:S(2)}, u32[]{:S(2)}) collective-permute-start(f32[24,128]{1,0:T(8,128)S(1)} %get-tuple-element.92.norms_own), channel_id=1, source_target_pairs={{0,1},{1,0},{2,3},{3,2},{4,5},{5,4},{6,7},{7,6},{8,9},{9,8},{10,11... | collective-permute-start | bytes 36872 | tf_op jit(solution)/shard_map/ppermute | solution.py:423

commit v11 on v10

--- a/solution.py
+++ b/solution.py
@@ -117,13 +117,14 @@
     return copies
 
 
-def ring_pack_kernel(vel, mag, vort, cur, synthesis_hbm, analysis_hbm, *rest):
-    *outs, synthesis, analysis, held, in_sems = rest
+def ring_pack_kernel(vel, mag, vort, cur, *rest):
+    *rest, held, in_sems = rest
+    small, outs, fetched = rest[:7], rest[7:-7], rest[-7:]
     owners, block = len(outs), outs[0].shape[1]
     me = lax.axis_index("mode")
     copies = start_all(
-        (vel, mag, vort, cur, synthesis_hbm, analysis_hbm),
-        [*(held.at[i] for i in range(4)), synthesis, analysis],
+        (vel, mag, vort, cur, *small),
+        [*(held.at[i] for i in range(4)), *fetched],
         in_sems,
     )
     starts = [pl.multiple_of(lax.rem(me + d, owners) * block, block) for d in range(owners)]
@@ -173,12 +174,7 @@
             out[j, span, :] = fields[j, span, :] + coef[j * pair : (j + 1) * pair]
 
 
-def mesh_kernel(nodes_hbm, mass_hbm, radial_hbm, stiff_hbm, iface_hbm, touch, back, from_iface, diag, coefs, edge_touch, edge_back, edge_diag, elem_nodes, mass, radial, stiff, iface, in_sems):
-    loads = start_all(
-        (nodes_hbm, mass_hbm, radial_hbm, stiff_hbm, iface_hbm), (elem_nodes, mass, radial, stiff, iface), in_sems
-    )
-    for load in loads:
-        load.wait()
+def mesh_kernel(elem_nodes, mass, radial, stiff, iface, touch, back, from_iface, diag, coefs, edge_touch, edge_back, edge_diag):
     elems, nodes = back.shape
     shared = iface.shape[1]
     fields = 8
@@ -193,10 +189,11 @@
             field = ids // words
             value = jnp.left_shift(1, field * 4)
             total = total + jnp.where(ids - field * words == word, value, 0)
+        turned = total.T
         for q in range(fields):
-            count = (jnp.right_shift(total, 4 * q) & 15).astype(f32)
-            touch[q * words : (q + 1) * words, span] = count.astype(f8)
-            back[span, q * words : (q + 1) * words] = count.T.astype(f8)
+            part = slice(q * words, (q + 1) * words)
+            touch[part, span] = (jnp.right_shift(total, 4 * q) & 15).astype(f32).astype(f8)
+            back[span, part] = (jnp.right_shift(turned, 4 * q) & 15).astype(f32).astype(f8)
     node = lax.broadcasted_iota(jnp.int32, (nodes, shared), 0)
     hit = jnp.where(iface[...] == node, 1.0, 0.0)
     touch[:, elems:] = hit.astype(f8)
@@ -366,32 +363,27 @@
         shape(elems, shared, kind=bf16),
         shape(8, shared),
     )
-    built = pl.pallas_call(
+    incidence = pl.pallas_call(
         mesh_kernel,
-        in_specs=[in_hbm] * 5,
         out_shape=tuple(pltpu.VMEM(t.shape, t.dtype) for t in tables),
-        scratch_shapes=[
-            pltpu.VMEM(elem_nodes.shape, jnp.int32),
-            pltpu.VMEM((1, elems), f32),
-            pltpu.VMEM((1, elems), f32),
-            pltpu.VMEM((1, elems), f32),
-            pltpu.VMEM(iface.shape, jnp.int32),
-            pltpu.SemaphoreType.DMA((5,)),
-        ],
         compiler_params=params(),
         name="incidence",
         cost_estimate=pl.CostEstimate(flops=2**31, bytes_accessed=2**23, transcendentals=0),
-    )(*(pin(a) for a in (elem_nodes, mass, radial, stiff, iface)))
+    )
+    small_inputs = (elem_nodes, mass, radial, stiff, iface)
     if owners <= 8 and block % 128 == 0:
-        *blocks, synthesis, analysis = pl.pallas_call(
+        small_inputs = (*small_inputs, synthesis, analysis)
+        packed = pl.pallas_call(
             ring_pack_kernel,
-            in_specs=[in_hbm] * 6,
+            in_specs=[in_hbm] * 11,
             out_shape=(pltpu.VMEM((2 * rows, block), f32),) * owners
-            + tuple(pltpu.VMEM(t.shape, t.dtype) for t in (synthesis, analysis)),
-            scratch_shapes=[pltpu.VMEM((4, *velocity.shape), f32), pltpu.SemaphoreType.DMA((6,))],
+            + tuple(pltpu.VMEM(t.shape, t.dtype) for t in small_inputs),
+            scratch_shapes=[pltpu.VMEM((4, *velocity.shape), f32), pltpu.SemaphoreType.DMA((11,))],
             compiler_params=params(medium),
             name="pack",
-        )(*(pin(a) for a in (velocity, magnetic, vorticity, current, synthesis, analysis)))
+        )(*(pin(a) for a in (velocity, magnetic, vorticity, current, *small_inputs)))
+        blocks, small_inputs, (synthesis, analysis) = list(packed[:owners]), packed[owners:-2], packed[-2:]
+        built = incidence(*small_inputs)
         for d in range(1, owners):
             blocks[d] = lax.ppermute(blocks[d], "mode", [(i, (i + d) % owners) for i in range(owners)])
         *blocks, built = lax.optimization_barrier((*blocks, built))
@@ -404,6 +396,7 @@
             cost_estimate=nonlinear_cost,
         )(*blocks, synthesis, analysis)
     else:
+        built = incidence(*small_inputs)
         packed = jnp.concatenate(
             [a.reshape(rows // 2, owners, block) for a in (velocity, magnetic, vorticity, current)], axis=0
         ).transpose(1, 0, 2)

time: 38.6 us -> 38.6 us (level)
  Pallas kernels: 10.9 us -> 10.2 us
  blocking collectives: 11.1 us -> 11.8 us
    all_to_all x1, blocking collectives: 11.1 us -> 11.8 us  [per_device(): forcing = lax.all_to_all(terms, 'mode', 0, 0, tiled=True)]
    pallas_call x2, Pallas kernels: 5.62 us -> 4.95 us  [the longest x1 3.76 us: per_device(): built = incidence(*small_inputs)]
  transfers between devices with their start and end apart: 10 -> 10, of which waited for: 1 -> 1; matrix products, arithmetic and copies ran while one was open for 0% -> 0% of each run, Pallas kernels for 18% -> 16%
where the time goes in v11:
time: 38.6 us; the launch traced here: 38.4 us
  starting transfers between devices  14.5 us (38%)
  blocking collectives  11.8 us (31%)
  Pallas kernels  10.2 us (26%)
  waiting for transfers between devices  1.18 us (3%)
  between operations  0.75 us (2%)
    ppermute x7, starting transfers between devices, per_device(): lax.ppermute(blocks[d], 'mode', [(i, (i + d) % owners) for i in range(own...  13.8 us
    all_to_all x1, blocking collectives, per_device(): forcing = lax.all_to_all(terms, 'mode', 0, 0, tiled=True)  11.8 us
    pallas_call x1, Pallas kernels, per_device(): built = incidence(*small_inputs)  3.76 us
    pallas_call x1, Pallas kernels, per_device(): call(image_kernel, 'image', (full, full, part), 2 ** 30)  1.24 us
    pallas_call x1, Pallas kernels, per_device(): pl.pallas_call(ring_pack_kernel, in_specs=[in_hbm] * 11, out_shape=(pltpu...  1.19 us
    ppermute x3, waiting for transfers between devices, swap(): return lax.ppermute(array, 'mer', [(0, 1), (1, 0)])  1.16 us
    pallas_call x1, Pallas kernels, per_device(): call(rhs_kernel, 'rhs', (full, part, small_row), 2 ** 30)  1.16 us
    pallas_call x1, Pallas kernels, per_device(): pl.pallas_call(last_kernel, out_shape=(out, out), compiler_params=params(...  0.99 us
  transfers between devices with their start and end apart: 10, of which 1 were waited for; matrix products, arithmetic and copies ran while one was open for 0% of the time, Pallas kernels for 16%

profile of v11, /device:TPU:0, one launch (start us, length us, event | category | flops | bytes accessed | tf_op | source)
XLA Modules:
  0.0 38.4 jit_solution(3047672535470903906)
XLA Ops:
  0.6 1.2 %pack.1 = (f32[48,256]{1,0:T(8,128)S(1)}, f32[48,256]{1,0:T(8,128)S(1)}, f32[48,256]{1,0:T(8,128)S(1)}, f32[48,256]{1,0:T(8,128)S(1)}, f32[48,256]{1,0:T(8,128)S...) custom-call(f32[3,2,2,2048]{3,2,1,0:T(2,128)} %vel.1, ...), custom_call_target="tpu_custom_call" | custom-call | tf_op jit(solution)/shard_map/pack/pallas_call | solution.py:376
  1.8 3.0 %collective-permute-start = (f32[48,256]{1,0:T(8,128)S(1)}, f32[48,256]{1,0:T(8,128)S(1)}, u32[]{:S(2)}, u32[]{:S(2)}) collective-permute-start(f32[48,256]{1,0:T(8,128)S(1)} %get-tuple-element.54), channel_id=1, source_target_pairs={{0,2},{2,4},{4,6},{6,8},{8,10},{10,12},{12,14},{14,0},{1,3},{3,5},... | collective-permute-start | bytes 147464 | tf_op jit(solution)/shard_map/ppermute | solution.py:388
  4.8 1.6 %collective-permute-start.1 = (f32[48,256]{1,0:T(8,128)S(1)}, f32[48,256]{1,0:T(8,128)S(1)}, u32[]{:S(2)}, u32[]{:S(2)}) collective-permute-start(f32[48,256]{1,0:T(8,128)S(1)} %get-tuple-element.55), channel_id=1, source_target_pairs={{0,4},{2,6},{4,8},{6,10},{8,12},{10,14},{12,0},{14,2},{1,5},{3,7},... | collective-permute-start | bytes 147464 | tf_op jit(solution)/shard_map/ppermute | solution.py:388
  6.4 2.6 %collective-permute-start.2 = (f32[48,256]{1,0:T(8,128)S(1)}, f32[48,256]{1,0:T(8,128)S(1)}, u32[]{:S(2)}, u32[]{:S(2)}) collective-permute-start(f32[48,256]{1,0:T(8,128)S(1)} %get-tuple-element.56), channel_id=1, source_target_pairs={{0,6},{2,8},{4,10},{6,12},{8,14},{10,0},{12,2},{14,4},{1,7},{3,9},... | collective-permute-start | bytes 147464 | tf_op jit(solution)/shard_map/ppermute | solution.py:388
  9.0 1.2 %collective-permute-start.3 = (f32[48,256]{1,0:T(8,128)S(1)}, f32[48,256]{1,0:T(8,128)S(1)}, u32[]{:S(2)}, u32[]{:S(2)}) collective-permute-start(f32[48,256]{1,0:T(8,128)S(1)} %get-tuple-element.57), channel_id=1, source_target_pairs={{0,8},{2,10},{4,12},{6,14},{8,0},{10,2},{12,4},{14,6},{1,9},{3,11}... | collective-permute-start | bytes 147464 | tf_op jit(solution)/shard_map/ppermute | solution.py:388
  10.2 2.6 %collective-permute-start.4 = (f32[48,256]{1,0:T(8,128)S(1)}, f32[48,256]{1,0:T(8,128)S(1)}, u32[]{:S(2)}, u32[]{:S(2)}) collective-permute-start(f32[48,256]{1,0:T(8,128)S(1)} %get-tuple-element.58), channel_id=1, source_target_pairs={{0,10},{2,12},{4,14},{6,0},{8,2},{10,4},{12,6},{14,8},{1,11},{3,13... | collective-permute-start | bytes 147464 | tf_op jit(solution)/shard_map/ppermute | solution.py:388
  12.8 0.0 collective-permute-done.refs_1_
  12.8 1.3 %collective-permute-start.5 = (f32[48,256]{1,0:T(8,128)S(1)}, f32[48,256]{1,0:T(8,128)S(1)}, u32[]{:S(2)}, u32[]{:S(2)}) collective-permute-start(f32[48,256]{1,0:T(8,128)S(1)} %get-tuple-element.59), channel_id=1, source_target_pairs={{0,12},{2,14},{4,0},{6,2},{8,4},{10,6},{12,8},{14,10},{1,13},{3,15... | collective-permute-start | bytes 147464 | tf_op jit(solution)/shard_map/ppermute | solution.py:388
  14.2 0.0 collective-permute-done.1.refs_2_
  14.2 1.4 %collective-permute-start.6 = (f32[48,256]{1,0:T(8,128)S(1)}, f32[48,256]{1,0:T(8,128)S(1)}, u32[]{:S(2)}, u32[]{:S(2)}) collective-permute-start(f32[48,256]{1,0:T(8,128)S(1)} %get-tuple-element.60), channel_id=1, source_target_pairs={{0,14},{2,0},{4,2},{6,4},{8,6},{10,8},{12,10},{14,12},{1,15},{3,1}... | collective-permute-start | bytes 147464 | tf_op jit(solution)/shard_map/ppermute | solution.py:388
  15.6 3.8 %incidence.1 = (f8e4m3fn[2048,1152]{1,0:T(32,128)(4,1)S(1)}, f8e4m3fn[1024,2048]{1,0:T(32,128)(4,1)S(1)}, bf16[128,2048]{1,0:T(8,128)(2,1)S(1)}, f32[8,2048]{1,0...) custom-call(s32[6,1024]{1,0:T(8,128)S(1)} %get-tuple-element.61.elem, ...), custom_call_target="tpu_custom_call" | custom-call | flops 2147483648 | bytes 8388608 | tf_op jit(solution)/shard_map/incidence/pallas_call | solution.py:386
  19.4 0.0 collective-permute-done.2.refs_3_
  19.4 0.0 collective-permute-done.3.refs_4_
  19.4 0.0 collective-permute-done.4.refs_5_
  19.4 0.0 collective-permute-done.5.refs_6_
  19.4 0.0 collective-permute-done.6.refs_7_
  19.4 0.5 %nonlinear.1 = f32[8,24,256]{2,1,0:T(8,128)S(1)} custom-call(f32[48,256]{1,0:T(8,128)S(1)} %get-tuple-element.74.refs_0_, f32[48,256]{1,0:T(8,128)S(1)} %collective-permute-done.refs_1_, f32[48,256]{1,0:T(8,128)S(1)} %collective-permute-done.1.refs_2_, f32[48,256]{1,0:T(8,128)S(1)} %collective-permute-done.2.refs_3_, ...), custom_call_target="tpu_custom_call" | custom-call | flops 8589934592 | bytes 16777216 | tf_op jit(solution)/shard_map/nonlinear/pallas_call | solution.py:390
  19.9 11.8 %all_to_all.5.forcing = f32[8,24,256]{2,1,0:T(8,128)S(1)} all-to-all(f32[8,24,256]{2,1,0:T(8,128)S(1)} %nonlinear.1), channel_id=1, replica_groups=mesh['runs'=2,'mode'=8,'mer'=2] {'mode'}, dimensions={0} | all-to-all | bytes 393216 | tf_op jit(solution)/shard_map/all_to_all | solution.py:411
  31.7 0.6 %rhs_edge.1 = (f32[24,1024]{1,0:T(8,128)S(1)}, f32[24,128]{1,0:T(8,128)S(1)}) custom-call(f32[8,24,256]{2,1,0:T(8,128)S(1)} %all_to_all.5.forcing, f8e4m3fn[2048,1152]{1,0:T(32,128)(4,1)S(1)} %get-tuple-element.84.touch, bf16[1024,128]{1,0:T(8,128)(2,1)S(1)} %get-tuple-element.85.edge_back, f32[8,128]{1,0:T(8,128)S(1)} %get-tuple-element.86.edge_diag, ...), custom_call_target="tpu_custom_call" | custom-call | tf_op jit(solution)/shard_map/rhs_edge/pallas_call | solution.py:429
  32.4 0.1 collective-permute-start.7
  32.4 1.2 %rhs.1 = (f32[24,2048]{1,0:T(8,128)S(1)}, f32[24,1024]{1,0:T(8,128)S(1)}, f32[24,128]{1,0:T(8,128)S(1)}) custom-call(f32[8,24,256]{2,1,0:T(8,128)S(1)} %all_to_all.5.forcing, f32[24,1024]{1,0:T(8,128)S(1)} %get-tuple-element.89.spread, f8e4m3fn[2048,1152]{1,0:T(32,128)(4,1)S(1)} %get-tuple-element.84.touch, ...), custom_call_target="tpu_custom_call" | custom-call | flops 1073741824 | bytes 2097152 | tf_op jit(solution)/shard_map/rhs/pallas_call | solution.py:436
  33.6 0.0 collective-permute-done.7.edge
  33.6 0.4 image_edge.1
  34.0 0.6 %collective-permute-start.8 = (f32[24,256]{1,0:T(8,128)S(1)}, f32[24,256]{1,0:T(8,128)S(1)}, u32[]{:S(2)}, u32[]{:S(2)}) collective-permute-start(f32[24,256]{1,0:T(8,128)S(1)} %get-tuple-element.95.own), channel_id=1, source_target_pairs={{0,1},{1,0},{2,3},{3,2},{4,5},{5,4},{6,7},{7,6},{8,9},{9,8},{10,11... | collective-permute-start | bytes 73736 | tf_op jit(solution)/shard_map/ppermute | solution.py:416
  34.5 1.2 %image.1 = (f32[24,2048]{1,0:T(8,128)S(1)}, f32[24,2048]{1,0:T(8,128)S(1)}, f32[24,1024]{1,0:T(8,128)S(1)}) custom-call(f32[24,2048]{1,0:T(8,128)S(1)} %get-tuple-element.96.local, f32[24,128]{1,0:T(8,128)S(1)} %collective-permute-done.7.edge, f32[24,1024]{1,0:T(8,128)S(1)} %get-tuple-element.97.sums, f8e4m3fn[2048,1152]{1,0:T(32,128)(4,1)S(1)} %get-tuple-element.84.touch, ...), custom_call_target="tpu_custom_call" | custom-call | flops 1073741824 | bytes 2097152 | tf_op jit(solution)/shard_map/image/pallas_call | solution.py:443
  35.8 0.0 collective-permute-done.8.edge
  35.8 0.4 %resid.1 = (f32[24,2048]{1,0:T(8,128)S(1)}, f32[24,128]{1,0:T(8,128)S(1)}) custom-call(f32[24,256]{1,0:T(8,128)S(1)} %get-tuple-element.95.own, f32[24,256]{1,0:T(8,128)S(1)} %collective-permute-done.8.edge, f32[24,2048]{1,0:T(8,128)S(1)} %get-tuple-element.99.rhs, f32[24,2048]{1,0:T(8,128)S(1)} %get-tuple-element.100.image, ...), custom_call_target="tpu_custom_call" | custom-call | tf_op jit(solution)/shard_map/resid/pallas_call | solution.py:446
  36.2 0.1 collective-permute-start.9
  36.3 1.2 %collective-permute-done.9.norms = f32[24,128]{1,0:T(8,128)S(1)} collective-permute-done((f32[24,128]{1,0:T(8,128)S(1)}, f32[24,128]{1,0:T(8,128)S(1)}, u32[]{:S(2)}, u32[]{:S(2)}) %collective-permute-start.9) | collective-permute-done | bytes 12320 | tf_op jit(solution)/shard_map/ppermute | solution.py:416
  37.4 1.0 %last.1 = (f32[3,2,2,2048]{3,2,1,0:T(2,128)}, f32[3,2,2,2048]{3,2,1,0:T(2,128)}) custom-call(f32[24,256]{1,0:T(8,128)S(1)} %collective-permute-done.8.edge, f32[24,256]{1,0:T(8,128)S(1)} %get-tuple-element.95.own, f32[24,128]{1,0:T(8,128)S(1)} %get-tuple-element.102.norms_own, f32[24,128]{1,0:T(8,128)S(1)} %collective-permute-done.9.norms, ...), custom_call_target="tpu_custom_call" | custom-call | tf_op jit(solution)/shard_map/last/pallas_call | solution.py:450
Async XLA Ops:
  1.8 11.0 %collective-permute-start = (f32[48,256]{1,0:T(8,128)S(1)}, f32[48,256]{1,0:T(8,128)S(1)}, u32[]{:S(2)}, u32[]{:S(2)}) collective-permute-start(f32[48,256]{1,0:T(8,128)S(1)} %get-tuple-element.54), channel_id=1, source_target_pairs={{0,2},{2,4},{4,6},{6,8},{8,10},{10,12},{12,14},{14,0},{1,3},{3,5},... | collective-permute-start | bytes 147464 | tf_op jit(solution)/shard_map/ppermute | solution.py:388
  4.8 9.3 %collective-permute-start.1 = (f32[48,256]{1,0:T(8,128)S(1)}, f32[48,256]{1,0:T(8,128)S(1)}, u32[]{:S(2)}, u32[]{:S(2)}) collective-permute-start(f32[48,256]{1,0:T(8,128)S(1)} %get-tuple-element.55), channel_id=1, source_target_pairs={{0,4},{2,6},{4,8},{6,10},{8,12},{10,14},{12,0},{14,2},{1,5},{3,7},... | collective-permute-start | bytes 147464 | tf_op jit(solution)/shard_map/ppermute | solution.py:388
  6.4 13.0 %collective-permute-start.2 = (f32[48,256]{1,0:T(8,128)S(1)}, f32[48,256]{1,0:T(8,128)S(1)}, u32[]{:S(2)}, u32[]{:S(2)}) collective-permute-start(f32[48,256]{1,0:T(8,128)S(1)} %get-tuple-element.56), channel_id=1, source_target_pairs={{0,6},{2,8},{4,10},{6,12},{8,14},{10,0},{12,2},{14,4},{1,7},{3,9},... | collective-permute-start | bytes 147464 | tf_op jit(solution)/shard_map/ppermute | solution.py:388
  9.0 10.4 %collective-permute-start.3 = (f32[48,256]{1,0:T(8,128)S(1)}, f32[48,256]{1,0:T(8,128)S(1)}, u32[]{:S(2)}, u32[]{:S(2)}) collective-permute-start(f32[48,256]{1,0:T(8,128)S(1)} %get-tuple-element.57), channel_id=1, source_target_pairs={{0,8},{2,10},{4,12},{6,14},{8,0},{10,2},{12,4},{14,6},{1,9},{3,11}... | collective-permute-start | bytes 147464 | tf_op jit(solution)/shard_map/ppermute | solution.py:388
  10.2 9.2 %collective-permute-start.4 = (f32[48,256]{1,0:T(8,128)S(1)}, f32[48,256]{1,0:T(8,128)S(1)}, u32[]{:S(2)}, u32[]{:S(2)}) collective-permute-start(f32[48,256]{1,0:T(8,128)S(1)} %get-tuple-element.58), channel_id=1, source_target_pairs={{0,10},{2,12},{4,14},{6,0},{8,2},{10,4},{12,6},{14,8},{1,11},{3,13... | collective-permute-start | bytes 147464 | tf_op jit(solution)/shard_map/ppermute | solution.py:388
  12.8 6.6 %collective-permute-start.5 = (f32[48,256]{1,0:T(8,128)S(1)}, f32[48,256]{1,0:T(8,128)S(1)}, u32[]{:S(2)}, u32[]{:S(2)}) collective-permute-start(f32[48,256]{1,0:T(8,128)S(1)} %get-tuple-element.59), channel_id=1, source_target_pairs={{0,12},{2,14},{4,0},{6,2},{8,4},{10,6},{12,8},{14,10},{1,13},{3,15... | collective-permute-start | bytes 147464 | tf_op jit(solution)/shard_map/ppermute | solution.py:388
  14.2 5.2 %collective-permute-start.6 = (f32[48,256]{1,0:T(8,128)S(1)}, f32[48,256]{1,0:T(8,128)S(1)}, u32[]{:S(2)}, u32[]{:S(2)}) collective-permute-start(f32[48,256]{1,0:T(8,128)S(1)} %get-tuple-element.60), channel_id=1, source_target_pairs={{0,14},{2,0},{4,2},{6,4},{8,6},{10,8},{12,10},{14,12},{1,15},{3,1}... | collective-permute-start | bytes 147464 | tf_op jit(solution)/shard_map/ppermute | solution.py:388
  32.4 1.2 %collective-permute-start.7 = (f32[24,128]{1,0:T(8,128)S(1)}, f32[24,128]{1,0:T(8,128)S(1)}, u32[]{:S(2)}, u32[]{:S(2)}) collective-permute-start(f32[24,128]{1,0:T(8,128)S(1)} %get-tuple-element.88.edge_own), channel_id=1, source_target_pairs={{0,1},{1,0},{2,3},{3,2},{4,5},{5,4},{6,7},{7,6},{8,9},{9,8},{10,11... | collective-permute-start | bytes 36872 | tf_op jit(solution)/shard_map/ppermute | solution.py:416
  34.0 1.8 %collective-permute-start.8 = (f32[24,256]{1,0:T(8,128)S(1)}, f32[24,256]{1,0:T(8,128)S(1)}, u32[]{:S(2)}, u32[]{:S(2)}) collective-permute-start(f32[24,256]{1,0:T(8,128)S(1)} %get-tuple-element.95.own), channel_id=1, source_target_pairs={{0,1},{1,0},{2,3},{3,2},{4,5},{5,4},{6,7},{7,6},{8,9},{9,8},{10,11... | collective-permute-start | bytes 73736 | tf_op jit(solution)/shard_map/ppermute | solution.py:416
  36.2 1.2 %collective-permute-start.9 = (f32[24,128]{1,0:T(8,128)S(1)}, f32[24,128]{1,0:T(8,128)S(1)}, u32[]{:S(2)}, u32[]{:S(2)}) collective-permute-start(f32[24,128]{1,0:T(8,128)S(1)} %get-tuple-element.102.norms_own), channel_id=1, source_target_pairs={{0,1},{1,0},{2,3},{3,2},{4,5},{5,4},{6,7},{7,6},{8,9},{9,8},{10,11... | collective-permute-start | bytes 36872 | tf_op jit(solution)/shard_map/ppermute | solution.py:416
